TPU v7x, 128 devices: a whole 4x4x4 slice. The times are simulated.
128 devices in a mesh: blk: 32 (over x, z, y_hi), inner: 4 (over y_lo, core).
Axes of the slice: x: 4, y: 4 (y_hi: 2, y_lo: 2; y = y_hi * 2 + y_lo), z: 4, core: 2. Of those that a mesh axis runs over, the one named last changes fastest.
Arguments:
- image: bfloat16 [12288, 1024], P('blk'), may hold values from -6 to 6
- text: bfloat16 [12288, 1024], P(('blk', 'inner')), may hold values from -1 to 1
- logit_scale: float32 [1], replicated, may hold values from 20 to 50
Outputs:
- loss: float32 [1], replicated
- grad_image: bfloat16 [12288, 1024], P(('blk', 'inner'))
- grad_text: bfloat16 [12288, 1024], P(('blk', 'inner'))
All inputs are finite; a program needn't handle non-finite values.
Results may differ from a plain program's by a relative error of at most 0.0044.
Values may be sent and summed in bfloat16 or wider, within the bound.
No kernel may reach another device: no remote copies, remote signals or barrier semaphores. Data moves between devices by JAX's collectives and lax.ppermute only.
A program may use at most 128 MiB of HBM per device.

v0:
```python
import math

import jax
import jax.numpy as jnp
from jax import lax
from jax.sharding import PartitionSpec as P

floor_value = -1e30


def joined(value, axis, combine):
    everything = jax.tree.map(lambda part: lax.all_gather(part, axis), value)
    leading = jax.tree.map(lambda part: part[0], everything)

    def turn(k, so_far):
        return combine(so_far, jax.tree.map(lambda part: part[k], everything))

    return lax.fori_loop(1, lax.axis_size(axis), turn, leading)


def from_behind(value, axis, steps):
    count = lax.axis_size(axis)
    pairs = [(source, (source + steps) % count) for source in range(count)]
    return lax.ppermute(value, axis, pairs)


def pair_merge(first, second):
    top = jnp.maximum(first[0], second[0])
    total = first[1] * jnp.exp(first[0] - top) + second[1] * jnp.exp(second[0] - top)
    return (top, total)


def on_device(image, text, logit_scale):
    scale = logit_scale[0]
    n_blk = lax.axis_size("blk")
    n_inner = lax.axis_size("inner")
    blk_id = lax.axis_index("blk")
    inner_id = lax.axis_index("inner")
    tr = text.shape[0]
    rr = image.shape[0]
    width = image.shape[1]
    cols = tr * n_blk

    def scores(tile):
        return scale * jnp.dot(image, tile.T, preferred_element_type=jnp.float32)

    init = (
        jnp.full((rr,), floor_value, jnp.float32),
        jnp.zeros((rr,), jnp.float32),
        jnp.full((cols,), floor_value, jnp.float32),
        jnp.zeros((cols,), jnp.float32),
    )
    piece = lax.all_gather(text, "blk", axis=0, tiled=True)
    rows_in = piece.shape[0]
    step_w = tr * math.gcd(rows_in // tr, 4)

    def one_block(k, state):
        row_max, row_sum, col_max, col_sum = state
        tile = lax.dynamic_slice_in_dim(piece, k * step_w, step_w, 0)
        s = scores(tile)
        new_max = jnp.maximum(row_max, jnp.max(s, axis=1))
        row_sum = row_sum * jnp.exp(row_max - new_max) + jnp.sum(
            jnp.exp(s - new_max[:, None]), axis=1
        )
        top = jnp.max(s, axis=0)
        part = jnp.sum(jnp.exp(s - top[None, :]), axis=0)
        where_at = k * step_w
        col_max = lax.dynamic_update_slice_in_dim(col_max, top, where_at, 0)
        col_sum = lax.dynamic_update_slice_in_dim(col_sum, part, where_at, 0)
        return (new_max, row_sum, col_max, col_sum)

    stats = lax.fori_loop(0, rows_in // step_w, one_block, tuple(init[:4]))
    row_max, row_sum, col_max, col_sum = stats[:4]
    row_max, row_sum = joined((row_max, row_sum), "inner", pair_merge)
    col_max, col_sum = joined((col_max, col_sum), "blk", pair_merge)
    row_lse = row_max + jnp.log(row_sum)
    col_lse = col_max + jnp.log(col_sum)
    paired_rows = lax.dynamic_slice_in_dim(image, inner_id * tr, tr, 0)
    diag = scale * jnp.sum(paired_rows.astype(jnp.float32) * text.astype(jnp.float32), axis=1)
    local_terms = (
        jnp.sum(lax.dynamic_slice_in_dim(row_lse, inner_id * tr, tr, 0))
        + jnp.sum(lax.dynamic_slice_in_dim(col_lse, blk_id * tr, tr, 0))
        - 2.0 * jnp.sum(diag)
    )
    summed = lax.psum(local_terms, ("blk", "inner"))
    loss = (summed / (2.0 * cols * n_inner)).reshape(1)
    row_ids = lax.iota(jnp.int32, rr)

    def grad_tile(tile, owner, offset, grad_rows):
        rows_in = tile.shape[0]
        s = scores(tile)
        lse_cols = lax.dynamic_slice_in_dim(col_lse, owner * tr + offset, rows_in, 0)
        col_ids = lax.iota(jnp.int32, rows_in)
        eye = (owner == blk_id) & (row_ids[:, None] == inner_id * tr + offset + col_ids[None, :])
        g = 0.5 * (jnp.exp(s - row_lse[:, None]) + jnp.exp(s - lse_cols[None, :]))
        g = (g - jnp.where(eye, 1.0, 0.0)).astype(jnp.bfloat16)
        grad_rows = grad_rows + jnp.dot(g, tile, preferred_element_type=jnp.float32)
        term = lax.dot_general(
            g, image, (((0,), (0,)), ((), ())), preferred_element_type=jnp.float32
        )
        return (grad_rows, term)

    grad_rows = jnp.zeros((rr, width), jnp.float32)

    def circle_step(turn, carry):
        tile, acc, rows_acc = carry
        for half_step in range(2):
            owner = (blk_id - (2 * turn + half_step)) % n_blk
            rows_acc, term = grad_tile(tile, owner, 0, rows_acc)
            acc = acc + term
            tile = from_behind(tile, "blk", 1)
            acc = from_behind(acc, "blk", 1)
        return (tile, acc, rows_acc)

    start = (text, jnp.zeros((tr, width), jnp.float32), grad_rows)
    tile, acc, grad_rows = lax.fori_loop(0, n_blk // 2, circle_step, start)
    image_sum = lax.psum_scatter(grad_rows, "inner", scatter_dimension=0, tiled=True)
    grad_image = (scale * image_sum).astype(jnp.bfloat16)
    grad_text = (scale * acc).astype(jnp.bfloat16)
    return (loss, grad_image, grad_text)


def solution(mesh):
    placed = (P("blk", None), P(("blk", "inner"), None), P())
    return jax.shard_map(
        on_device,
        mesh=mesh,
        in_specs=placed,
        out_specs=(P(), P(("blk", "inner"), None), P(("blk", "inner"), None)),
        check_vma=False,
    )
```

profile of v0, /device:TPU:1, one launch (start us, length us, event | category | flops | bytes accessed | tf_op | source)
XLA Modules:
  0.0 999.6 jit_solution(2346833386325532695)
XLA Ops:
  8.9 97.2 %all-gather.8.cloned.1.call-done = bf16[3072,1024]{1,0:T(8,128)(2,1)} async-done(((bf16[96,1024]{1,0:T(8,128)(2,1)}), bf16[3072,1024]{1,0:T(8,128)(2,1)}) %all-gather.8.cloned.1.call-update) | async-done | bytes 6291472 | tf_op jit(solution)/shard_map/all_gather | solution.py:53
  106.1 28.4 %while.76 = (s32[]{:T(128)}, f32[384]{0:T(512)S(1)}, f32[384]{0:T(512)S(1)}, f32[3072]{0:T(1024)S(1)}, f32[3072]{0:T(1024)S(1)}, /*index=5*/f32[]{:T(128)}, bf16...) while((s32[]{:T(128)}, f32[384]{0:T(512)S(1)}, ...), condition=%wide.region_5.0_spmd.clone, body=%wide.region_0.0_spmd.clone.sunk | while | flops 303023232 | bytes 2783930 | solution.py:72
  134.5 78.4 %all-gather.2 = f32[98304]{0:T(1024)S(1)} all-gather(f32[3072]{0:T(1024)S(1)} %get-tuple-element.683), channel_id=4, replica_groups=mesh['blk'=32,'inner'=4] {'blk'}, dimensions={0}, use_global_device_ids=true | all-gather | bytes 405504 | tf_op jit(solution)/shard_map/all_gather | solution.py:12
  213.0 76.5 %all-gather.3 = f32[98304]{0:T(1024)S(1)} all-gather(f32[3072]{0:T(1024)S(1)} %get-tuple-element.684), channel_id=5, replica_groups=mesh['blk'=32,'inner'=4] {'blk'}, dimensions={0}, use_global_device_ids=true | all-gather | bytes 405504 | tf_op jit(solution)/shard_map/all_gather | solution.py:12
  289.6 33.6 %all-gather.5 = f32[4,1,384]{2,1,0:T(1,128)S(1)} all-gather(f32[1,1,384]{2,1,0:T(1,128)S(1)} %reshape.35), channel_id=3, replica_groups=mesh['blk'=32,'inner'=4] {'inner'}, dimensions={0}, use_global_device_ids=true | all-gather | bytes 7680 | tf_op jit(solution)/shard_map/all_gather | solution.py:12
  331.0 558.5 %while.77 = (s32[]{:T(128)}, bf16[96,1024]{1,0:T(8,128)(2,1)S(1)}, f32[96,1024]{1,0:T(8,128)S(1)}, f32[384,1024]{1,0:T(8,128)}, f32[]{:T(128)}, /*index=5*/bf16[...) while((s32[]{:T(128)}, bf16[96,1024]{1,0:T(8,128)(2,1)S(1)}, ...), condition=%wide.region_16.17_spmd.clone, body=%wide.region_15.16_spmd.clone.sunk | while | flops 455098496 | bytes 17751152 | solution.py:116
  354.9 16.2 %collective-permute-done.1 = bf16[96,1024]{1,0:T(8,128)(2,1)S(1)} collective-permute-done((bf16[96,1024]{1,0:T(8,128)(2,1)}, bf16[96,1024]{1,0:T(8,128)(2,1)S(1)}, u32[]{:S(2)}, u32[]{:S(2)}) %collective-permute-start.1) | collective-permute-done | bytes 196640 | tf_op jit(solution)/shard_map/while/body/eval_jaxpr/ppermute | solution.py:24
  393.4 13.8 %collective-permute-done.1 = bf16[96,1024]{1,0:T(8,128)(2,1)S(1)} collective-permute-done((bf16[96,1024]{1,0:T(8,128)(2,1)}, bf16[96,1024]{1,0:T(8,128)(2,1)S(1)}, u32[]{:S(2)}, u32[]{:S(2)}) %collective-permute-start.1) | collective-permute-done | bytes 196640 | tf_op jit(solution)/shard_map/while/body/eval_jaxpr/ppermute | solution.py:24
  427.6 12.0 %collective-permute-done.1 = bf16[96,1024]{1,0:T(8,128)(2,1)S(1)} collective-permute-done((bf16[96,1024]{1,0:T(8,128)(2,1)}, bf16[96,1024]{1,0:T(8,128)(2,1)S(1)}, u32[]{:S(2)}, u32[]{:S(2)}) %collective-permute-start.1) | collective-permute-done | bytes 196640 | tf_op jit(solution)/shard_map/while/body/eval_jaxpr/ppermute | solution.py:24
  441.1 8.7 collective-permute-done
  457.9 10.9 %collective-permute-done.1 = bf16[96,1024]{1,0:T(8,128)(2,1)S(1)} collective-permute-done((bf16[96,1024]{1,0:T(8,128)(2,1)}, bf16[96,1024]{1,0:T(8,128)(2,1)S(1)}, u32[]{:S(2)}, u32[]{:S(2)}) %collective-permute-start.1) | collective-permute-done | bytes 196640 | tf_op jit(solution)/shard_map/while/body/eval_jaxpr/ppermute | solution.py:24
  487.2 11.1 %collective-permute-done.1 = bf16[96,1024]{1,0:T(8,128)(2,1)S(1)} collective-permute-done((bf16[96,1024]{1,0:T(8,128)(2,1)}, bf16[96,1024]{1,0:T(8,128)(2,1)S(1)}, u32[]{:S(2)}, u32[]{:S(2)}) %collective-permute-start.1) | collective-permute-done | bytes 196640 | tf_op jit(solution)/shard_map/while/body/eval_jaxpr/ppermute | solution.py:24
  499.9 10.3 %collective-permute-done = bf16[96,1024]{1,0:T(8,128)(2,1)S(1)} collective-permute-done((bf16[96,1024]{1,0:T(8,128)(2,1)S(1)}, bf16[96,1024]{1,0:T(8,128)(2,1)S(1)}, u32[]{:S(2)}, u32[]{:S(2)}) %collective-permute-start) | collective-permute-done | bytes 196640 | tf_op jit(solution)/shard_map/while/body/eval_jaxpr/ppermute | solution.py:24
  518.3 13.3 %collective-permute-done.1 = bf16[96,1024]{1,0:T(8,128)(2,1)S(1)} collective-permute-done((bf16[96,1024]{1,0:T(8,128)(2,1)}, bf16[96,1024]{1,0:T(8,128)(2,1)S(1)}, u32[]{:S(2)}, u32[]{:S(2)}) %collective-permute-start.1) | collective-permute-done | bytes 196640 | tf_op jit(solution)/shard_map/while/body/eval_jaxpr/ppermute | solution.py:24
  533.1 11.2 %collective-permute-done = bf16[96,1024]{1,0:T(8,128)(2,1)S(1)} collective-permute-done((bf16[96,1024]{1,0:T(8,128)(2,1)S(1)}, bf16[96,1024]{1,0:T(8,128)(2,1)S(1)}, u32[]{:S(2)}, u32[]{:S(2)}) %collective-permute-start) | collective-permute-done | bytes 196640 | tf_op jit(solution)/shard_map/while/body/eval_jaxpr/ppermute | solution.py:24
  553.8 15.4 %collective-permute-done.1 = bf16[96,1024]{1,0:T(8,128)(2,1)S(1)} collective-permute-done((bf16[96,1024]{1,0:T(8,128)(2,1)}, bf16[96,1024]{1,0:T(8,128)(2,1)S(1)}, u32[]{:S(2)}, u32[]{:S(2)}) %collective-permute-start.1) | collective-permute-done | bytes 196640 | tf_op jit(solution)/shard_map/while/body/eval_jaxpr/ppermute | solution.py:24
  570.7 11.0 %collective-permute-done = bf16[96,1024]{1,0:T(8,128)(2,1)S(1)} collective-permute-done((bf16[96,1024]{1,0:T(8,128)(2,1)S(1)}, bf16[96,1024]{1,0:T(8,128)(2,1)S(1)}, u32[]{:S(2)}, u32[]{:S(2)}) %collective-permute-start) | collective-permute-done | bytes 196640 | tf_op jit(solution)/shard_map/while/body/eval_jaxpr/ppermute | solution.py:24
  593.5 17.1 %collective-permute-done.1 = bf16[96,1024]{1,0:T(8,128)(2,1)S(1)} collective-permute-done((bf16[96,1024]{1,0:T(8,128)(2,1)}, bf16[96,1024]{1,0:T(8,128)(2,1)S(1)}, u32[]{:S(2)}, u32[]{:S(2)}) %collective-permute-start.1) | collective-permute-done | bytes 196640 | tf_op jit(solution)/shard_map/while/body/eval_jaxpr/ppermute | solution.py:24
  612.2 9.4 collective-permute-done
  634.0 15.3 %collective-permute-done.1 = bf16[96,1024]{1,0:T(8,128)(2,1)S(1)} collective-permute-done((bf16[96,1024]{1,0:T(8,128)(2,1)}, bf16[96,1024]{1,0:T(8,128)(2,1)S(1)}, u32[]{:S(2)}, u32[]{:S(2)}) %collective-permute-start.1) | collective-permute-done | bytes 196640 | tf_op jit(solution)/shard_map/while/body/eval_jaxpr/ppermute | solution.py:24
  670.7 13.4 %collective-permute-done.1 = bf16[96,1024]{1,0:T(8,128)(2,1)S(1)} collective-permute-done((bf16[96,1024]{1,0:T(8,128)(2,1)}, bf16[96,1024]{1,0:T(8,128)(2,1)S(1)}, u32[]{:S(2)}, u32[]{:S(2)}) %collective-permute-start.1) | collective-permute-done | bytes 196640 | tf_op jit(solution)/shard_map/while/body/eval_jaxpr/ppermute | solution.py:24
  703.7 11.6 %collective-permute-done.1 = bf16[96,1024]{1,0:T(8,128)(2,1)S(1)} collective-permute-done((bf16[96,1024]{1,0:T(8,128)(2,1)}, bf16[96,1024]{1,0:T(8,128)(2,1)S(1)}, u32[]{:S(2)}, u32[]{:S(2)}) %collective-permute-start.1) | collective-permute-done | bytes 196640 | tf_op jit(solution)/shard_map/while/body/eval_jaxpr/ppermute | solution.py:24
  716.9 8.7 collective-permute-done
  733.7 10.9 %collective-permute-done.1 = bf16[96,1024]{1,0:T(8,128)(2,1)S(1)} collective-permute-done((bf16[96,1024]{1,0:T(8,128)(2,1)}, bf16[96,1024]{1,0:T(8,128)(2,1)S(1)}, u32[]{:S(2)}, u32[]{:S(2)}) %collective-permute-start.1) | collective-permute-done | bytes 196640 | tf_op jit(solution)/shard_map/while/body/eval_jaxpr/ppermute | solution.py:24
  763.0 11.9 %collective-permute-done.1 = bf16[96,1024]{1,0:T(8,128)(2,1)S(1)} collective-permute-done((bf16[96,1024]{1,0:T(8,128)(2,1)}, bf16[96,1024]{1,0:T(8,128)(2,1)S(1)}, u32[]{:S(2)}, u32[]{:S(2)}) %collective-permute-start.1) | collective-permute-done | bytes 196640 | tf_op jit(solution)/shard_map/while/body/eval_jaxpr/ppermute | solution.py:24
  776.4 10.9 %collective-permute-done = bf16[96,1024]{1,0:T(8,128)(2,1)S(1)} collective-permute-done((bf16[96,1024]{1,0:T(8,128)(2,1)S(1)}, bf16[96,1024]{1,0:T(8,128)(2,1)S(1)}, u32[]{:S(2)}, u32[]{:S(2)}) %collective-permute-start) | collective-permute-done | bytes 196640 | tf_op jit(solution)/shard_map/while/body/eval_jaxpr/ppermute | solution.py:24
  795.3 14.0 %collective-permute-done.1 = bf16[96,1024]{1,0:T(8,128)(2,1)S(1)} collective-permute-done((bf16[96,1024]{1,0:T(8,128)(2,1)}, bf16[96,1024]{1,0:T(8,128)(2,1)S(1)}, u32[]{:S(2)}, u32[]{:S(2)}) %collective-permute-start.1) | collective-permute-done | bytes 196640 | tf_op jit(solution)/shard_map/while/body/eval_jaxpr/ppermute | solution.py:24
  810.8 11.2 %collective-permute-done = bf16[96,1024]{1,0:T(8,128)(2,1)S(1)} collective-permute-done((bf16[96,1024]{1,0:T(8,128)(2,1)S(1)}, bf16[96,1024]{1,0:T(8,128)(2,1)S(1)}, u32[]{:S(2)}, u32[]{:S(2)}) %collective-permute-start) | collective-permute-done | bytes 196640 | tf_op jit(solution)/shard_map/while/body/eval_jaxpr/ppermute | solution.py:24
  831.9 16.2 %collective-permute-done.1 = bf16[96,1024]{1,0:T(8,128)(2,1)S(1)} collective-permute-done((bf16[96,1024]{1,0:T(8,128)(2,1)}, bf16[96,1024]{1,0:T(8,128)(2,1)S(1)}, u32[]{:S(2)}, u32[]{:S(2)}) %collective-permute-start.1) | collective-permute-done | bytes 196640 | tf_op jit(solution)/shard_map/while/body/eval_jaxpr/ppermute | solution.py:24
  849.6 11.0 %collective-permute-done = bf16[96,1024]{1,0:T(8,128)(2,1)S(1)} collective-permute-done((bf16[96,1024]{1,0:T(8,128)(2,1)S(1)}, bf16[96,1024]{1,0:T(8,128)(2,1)S(1)}, u32[]{:S(2)}, u32[]{:S(2)}) %collective-permute-start) | collective-permute-done | bytes 196640 | tf_op jit(solution)/shard_map/while/body/eval_jaxpr/ppermute | solution.py:24
  873.0 16.6 %collective-permute-done.1 = bf16[96,1024]{1,0:T(8,128)(2,1)S(1)} collective-permute-done((bf16[96,1024]{1,0:T(8,128)(2,1)}, bf16[96,1024]{1,0:T(8,128)(2,1)S(1)}, u32[]{:S(2)}, u32[]{:S(2)}) %collective-permute-start.1) | collective-permute-done | bytes 196640 | tf_op jit(solution)/shard_map/while/body/eval_jaxpr/ppermute | solution.py:24
  893.9 94.7 %psum.7 = f32[]{:T(128)} all-reduce(f32[]{:T(128)S(6)} %sub.223), channel_id=1, replica_groups=mesh['blk'=32,'inner'=4] {'blk','inner'}, use_global_device_ids=true, to_apply=%region_14.0 | all-reduce | flops 1 | bytes 8 | tf_op jit(solution)/shard_map/psum | solution.py:85
  (423 shorter events, 288.4 us)
Async XLA Ops:
  7.2 98.9 %all-gather.8.cloned.1.call-start = ((), (), s32[]{:S(2)}) async-start(), calls=%async_computation.1 | async-start | bytes 6488064 | tf_op jit(solution)/shard_map/all_gather | solution.py:53
  7.9 982.0 %reduce-scatter.2.cloned.1.call-start = ((), (), s32[]{:S(2)}) async-start(), calls=%async_computation.2 | async-start | bytes 1966080 | tf_op jit(solution)/shard_map/reduce_scatter | solution.py:117
  335.5 16.0 %collective-permute-start.2 = (f32[96,1024]{1,0:T(8,128)S(1)}, f32[96,1024]{1,0:T(8,128)S(1)}, u32[]{:S(2)}, u32[]{:S(2)}) collective-permute-start(f32[96,1024]{1,0:T(8,128)S(1)} %convolution_add_fusion.4), channel_id=1, source_target_pairs={{0,4},{4,8},{8,12},{12,16},{16,20},{20,24},{24,28},{28,32},{32,36}... | collective-permute-start | bytes 1179656 | tf_op jit(solution)/shard_map/while/body/eval_jaxpr/ppermute | solution.py:24
  351.9 19.3 %collective-permute-start.3 = (f32[96,1024]{1,0:T(8,128)S(1)}, f32[96,1024]{1,0:T(8,128)S(1)}, u32[]{:S(2)}, u32[]{:S(2)}) collective-permute-start(f32[96,1024]{1,0:T(8,128)S(1)} %convolution_add_fusion.5), channel_id=1, source_target_pairs={{0,4},{4,8},{8,12},{12,16},{16,20},{20,24},{24,28},{28,32},{32,36}... | collective-permute-start | bytes 1179656 | tf_op jit(solution)/shard_map/while/body/eval_jaxpr/ppermute | solution.py:24
  352.3 18.8 %collective-permute-start.1 = (bf16[96,1024]{1,0:T(8,128)(2,1)}, bf16[96,1024]{1,0:T(8,128)(2,1)S(1)}, u32[]{:S(2)}, u32[]{:S(2)}) collective-permute-start(bf16[96,1024]{1,0:T(8,128)(2,1)} %copy-done.1), channel_id=1, source_target_pairs={{0,4},{4,8},{8,12},{12,16},{16,20},{20,24},{24,28},{28,32},{32,36}... | collective-permute-start | bytes 589832 | tf_op jit(solution)/shard_map/while/body/eval_jaxpr/ppermute | solution.py:24
  372.6 16.8 %collective-permute-start.2 = (f32[96,1024]{1,0:T(8,128)S(1)}, f32[96,1024]{1,0:T(8,128)S(1)}, u32[]{:S(2)}, u32[]{:S(2)}) collective-permute-start(f32[96,1024]{1,0:T(8,128)S(1)} %convolution_add_fusion.4), channel_id=1, source_target_pairs={{0,4},{4,8},{8,12},{12,16},{16,20},{20,24},{24,28},{28,32},{32,36}... | collective-permute-start | bytes 1179656 | tf_op jit(solution)/shard_map/while/body/eval_jaxpr/ppermute | solution.py:24
  389.7 17.4 %collective-permute-start.3 = (f32[96,1024]{1,0:T(8,128)S(1)}, f32[96,1024]{1,0:T(8,128)S(1)}, u32[]{:S(2)}, u32[]{:S(2)}) collective-permute-start(f32[96,1024]{1,0:T(8,128)S(1)} %convolution_add_fusion.5), channel_id=1, source_target_pairs={{0,4},{4,8},{8,12},{12,16},{16,20},{20,24},{24,28},{28,32},{32,36}... | collective-permute-start | bytes 1179656 | tf_op jit(solution)/shard_map/while/body/eval_jaxpr/ppermute | solution.py:24
  390.2 17.0 %collective-permute-start.1 = (bf16[96,1024]{1,0:T(8,128)(2,1)}, bf16[96,1024]{1,0:T(8,128)(2,1)S(1)}, u32[]{:S(2)}, u32[]{:S(2)}) collective-permute-start(bf16[96,1024]{1,0:T(8,128)(2,1)} %copy-done.1), channel_id=1, source_target_pairs={{0,4},{4,8},{8,12},{12,16},{16,20},{20,24},{24,28},{28,32},{32,36}... | collective-permute-start | bytes 589832 | tf_op jit(solution)/shard_map/while/body/eval_jaxpr/ppermute | solution.py:24
  424.0 15.6 %collective-permute-start.3 = (f32[96,1024]{1,0:T(8,128)S(1)}, f32[96,1024]{1,0:T(8,128)S(1)}, u32[]{:S(2)}, u32[]{:S(2)}) collective-permute-start(f32[96,1024]{1,0:T(8,128)S(1)} %convolution_add_fusion.5), channel_id=1, source_target_pairs={{0,4},{4,8},{8,12},{12,16},{16,20},{20,24},{24,28},{28,32},{32,36}... | collective-permute-start | bytes 1179656 | tf_op jit(solution)/shard_map/while/body/eval_jaxpr/ppermute | solution.py:24
  514.7 16.9 %collective-permute-start.3 = (f32[96,1024]{1,0:T(8,128)S(1)}, f32[96,1024]{1,0:T(8,128)S(1)}, u32[]{:S(2)}, u32[]{:S(2)}) collective-permute-start(f32[96,1024]{1,0:T(8,128)S(1)} %convolution_add_fusion.5), channel_id=1, source_target_pairs={{0,4},{4,8},{8,12},{12,16},{16,20},{20,24},{24,28},{28,32},{32,36}... | collective-permute-start | bytes 1179656 | tf_op jit(solution)/shard_map/while/body/eval_jaxpr/ppermute | solution.py:24
  515.2 16.4 %collective-permute-start.1 = (bf16[96,1024]{1,0:T(8,128)(2,1)}, bf16[96,1024]{1,0:T(8,128)(2,1)S(1)}, u32[]{:S(2)}, u32[]{:S(2)}) collective-permute-start(bf16[96,1024]{1,0:T(8,128)(2,1)} %copy-done.1), channel_id=1, source_target_pairs={{0,4},{4,8},{8,12},{12,16},{16,20},{20,24},{24,28},{28,32},{32,36}... | collective-permute-start | bytes 589832 | tf_op jit(solution)/shard_map/while/body/eval_jaxpr/ppermute | solution.py:24
  533.0 16.8 %collective-permute-start.2 = (f32[96,1024]{1,0:T(8,128)S(1)}, f32[96,1024]{1,0:T(8,128)S(1)}, u32[]{:S(2)}, u32[]{:S(2)}) collective-permute-start(f32[96,1024]{1,0:T(8,128)S(1)} %convolution_add_fusion.4), channel_id=1, source_target_pairs={{0,4},{4,8},{8,12},{12,16},{16,20},{20,24},{24,28},{28,32},{32,36}... | collective-permute-start | bytes 1179656 | tf_op jit(solution)/shard_map/while/body/eval_jaxpr/ppermute | solution.py:24
  550.2 19.0 %collective-permute-start.3 = (f32[96,1024]{1,0:T(8,128)S(1)}, f32[96,1024]{1,0:T(8,128)S(1)}, u32[]{:S(2)}, u32[]{:S(2)}) collective-permute-start(f32[96,1024]{1,0:T(8,128)S(1)} %convolution_add_fusion.5), channel_id=1, source_target_pairs={{0,4},{4,8},{8,12},{12,16},{16,20},{20,24},{24,28},{28,32},{32,36}... | collective-permute-start | bytes 1179656 | tf_op jit(solution)/shard_map/while/body/eval_jaxpr/ppermute | solution.py:24
  550.6 18.6 %collective-permute-start.1 = (bf16[96,1024]{1,0:T(8,128)(2,1)}, bf16[96,1024]{1,0:T(8,128)(2,1)S(1)}, u32[]{:S(2)}, u32[]{:S(2)}) collective-permute-start(bf16[96,1024]{1,0:T(8,128)(2,1)} %copy-done.1), channel_id=1, source_target_pairs={{0,4},{4,8},{8,12},{12,16},{16,20},{20,24},{24,28},{28,32},{32,36}... | collective-permute-start | bytes 589832 | tf_op jit(solution)/shard_map/while/body/eval_jaxpr/ppermute | solution.py:24
  570.6 19.0 %collective-permute-start.2 = (f32[96,1024]{1,0:T(8,128)S(1)}, f32[96,1024]{1,0:T(8,128)S(1)}, u32[]{:S(2)}, u32[]{:S(2)}) collective-permute-start(f32[96,1024]{1,0:T(8,128)S(1)} %convolution_add_fusion.4), channel_id=1, source_target_pairs={{0,4},{4,8},{8,12},{12,16},{16,20},{20,24},{24,28},{28,32},{32,36}... | collective-permute-start | bytes 1179656 | tf_op jit(solution)/shard_map/while/body/eval_jaxpr/ppermute | solution.py:24
  589.9 20.7 %collective-permute-start.3 = (f32[96,1024]{1,0:T(8,128)S(1)}, f32[96,1024]{1,0:T(8,128)S(1)}, u32[]{:S(2)}, u32[]{:S(2)}) collective-permute-start(f32[96,1024]{1,0:T(8,128)S(1)} %convolution_add_fusion.5), channel_id=1, source_target_pairs={{0,4},{4,8},{8,12},{12,16},{16,20},{20,24},{24,28},{28,32},{32,36}... | collective-permute-start | bytes 1179656 | tf_op jit(solution)/shard_map/while/body/eval_jaxpr/ppermute | solution.py:24
  590.4 20.3 %collective-permute-start.1 = (bf16[96,1024]{1,0:T(8,128)(2,1)}, bf16[96,1024]{1,0:T(8,128)(2,1)S(1)}, u32[]{:S(2)}, u32[]{:S(2)}) collective-permute-start(bf16[96,1024]{1,0:T(8,128)(2,1)} %copy-done.1), channel_id=1, source_target_pairs={{0,4},{4,8},{8,12},{12,16},{16,20},{20,24},{24,28},{28,32},{32,36}... | collective-permute-start | bytes 589832 | tf_op jit(solution)/shard_map/while/body/eval_jaxpr/ppermute | solution.py:24
  612.1 17.9 %collective-permute-start.2 = (f32[96,1024]{1,0:T(8,128)S(1)}, f32[96,1024]{1,0:T(8,128)S(1)}, u32[]{:S(2)}, u32[]{:S(2)}) collective-permute-start(f32[96,1024]{1,0:T(8,128)S(1)} %convolution_add_fusion.4), channel_id=1, source_target_pairs={{0,4},{4,8},{8,12},{12,16},{16,20},{20,24},{24,28},{28,32},{32,36}... | collective-permute-start | bytes 1179656 | tf_op jit(solution)/shard_map/while/body/eval_jaxpr/ppermute | solution.py:24
  630.4 18.9 %collective-permute-start.3 = (f32[96,1024]{1,0:T(8,128)S(1)}, f32[96,1024]{1,0:T(8,128)S(1)}, u32[]{:S(2)}, u32[]{:S(2)}) collective-permute-start(f32[96,1024]{1,0:T(8,128)S(1)} %convolution_add_fusion.5), channel_id=1, source_target_pairs={{0,4},{4,8},{8,12},{12,16},{16,20},{20,24},{24,28},{28,32},{32,36}... | collective-permute-start | bytes 1179656 | tf_op jit(solution)/shard_map/while/body/eval_jaxpr/ppermute | solution.py:24
  630.8 18.4 %collective-permute-start.1 = (bf16[96,1024]{1,0:T(8,128)(2,1)}, bf16[96,1024]{1,0:T(8,128)(2,1)S(1)}, u32[]{:S(2)}, u32[]{:S(2)}) collective-permute-start(bf16[96,1024]{1,0:T(8,128)(2,1)} %copy-done.1), channel_id=1, source_target_pairs={{0,4},{4,8},{8,12},{12,16},{16,20},{20,24},{24,28},{28,32},{32,36}... | collective-permute-start | bytes 589832 | tf_op jit(solution)/shard_map/while/body/eval_jaxpr/ppermute | solution.py:24
  650.7 16.1 %collective-permute-start.2 = (f32[96,1024]{1,0:T(8,128)S(1)}, f32[96,1024]{1,0:T(8,128)S(1)}, u32[]{:S(2)}, u32[]{:S(2)}) collective-permute-start(f32[96,1024]{1,0:T(8,128)S(1)} %convolution_add_fusion.4), channel_id=1, source_target_pairs={{0,4},{4,8},{8,12},{12,16},{16,20},{20,24},{24,28},{28,32},{32,36}... | collective-permute-start | bytes 1179656 | tf_op jit(solution)/shard_map/while/body/eval_jaxpr/ppermute | solution.py:24
  667.1 17.1 %collective-permute-start.3 = (f32[96,1024]{1,0:T(8,128)S(1)}, f32[96,1024]{1,0:T(8,128)S(1)}, u32[]{:S(2)}, u32[]{:S(2)}) collective-permute-start(f32[96,1024]{1,0:T(8,128)S(1)} %convolution_add_fusion.5), channel_id=1, source_target_pairs={{0,4},{4,8},{8,12},{12,16},{16,20},{20,24},{24,28},{28,32},{32,36}... | collective-permute-start | bytes 1179656 | tf_op jit(solution)/shard_map/while/body/eval_jaxpr/ppermute | solution.py:24
  667.6 16.6 %collective-permute-start.1 = (bf16[96,1024]{1,0:T(8,128)(2,1)}, bf16[96,1024]{1,0:T(8,128)(2,1)S(1)}, u32[]{:S(2)}, u32[]{:S(2)}) collective-permute-start(bf16[96,1024]{1,0:T(8,128)(2,1)} %copy-done.1), channel_id=1, source_target_pairs={{0,4},{4,8},{8,12},{12,16},{16,20},{20,24},{24,28},{28,32},{32,36}... | collective-permute-start | bytes 589832 | tf_op jit(solution)/shard_map/while/body/eval_jaxpr/ppermute | solution.py:24
  759.4 15.5 %collective-permute-start.3 = (f32[96,1024]{1,0:T(8,128)S(1)}, f32[96,1024]{1,0:T(8,128)S(1)}, u32[]{:S(2)}, u32[]{:S(2)}) collective-permute-start(f32[96,1024]{1,0:T(8,128)S(1)} %convolution_add_fusion.5), channel_id=1, source_target_pairs={{0,4},{4,8},{8,12},{12,16},{16,20},{20,24},{24,28},{28,32},{32,36}... | collective-permute-start | bytes 1179656 | tf_op jit(solution)/shard_map/while/body/eval_jaxpr/ppermute | solution.py:24
  791.7 17.6 %collective-permute-start.3 = (f32[96,1024]{1,0:T(8,128)S(1)}, f32[96,1024]{1,0:T(8,128)S(1)}, u32[]{:S(2)}, u32[]{:S(2)}) collective-permute-start(f32[96,1024]{1,0:T(8,128)S(1)} %convolution_add_fusion.5), channel_id=1, source_target_pairs={{0,4},{4,8},{8,12},{12,16},{16,20},{20,24},{24,28},{28,32},{32,36}... | collective-permute-start | bytes 1179656 | tf_op jit(solution)/shard_map/while/body/eval_jaxpr/ppermute | solution.py:24
  792.1 17.2 %collective-permute-start.1 = (bf16[96,1024]{1,0:T(8,128)(2,1)}, bf16[96,1024]{1,0:T(8,128)(2,1)S(1)}, u32[]{:S(2)}, u32[]{:S(2)}) collective-permute-start(bf16[96,1024]{1,0:T(8,128)(2,1)} %copy-done.1), channel_id=1, source_target_pairs={{0,4},{4,8},{8,12},{12,16},{16,20},{20,24},{24,28},{28,32},{32,36}... | collective-permute-start | bytes 589832 | tf_op jit(solution)/shard_map/while/body/eval_jaxpr/ppermute | solution.py:24
  810.8 17.2 %collective-permute-start.2 = (f32[96,1024]{1,0:T(8,128)S(1)}, f32[96,1024]{1,0:T(8,128)S(1)}, u32[]{:S(2)}, u32[]{:S(2)}) collective-permute-start(f32[96,1024]{1,0:T(8,128)S(1)} %convolution_add_fusion.4), channel_id=1, source_target_pairs={{0,4},{4,8},{8,12},{12,16},{16,20},{20,24},{24,28},{28,32},{32,36}... | collective-permute-start | bytes 1179656 | tf_op jit(solution)/shard_map/while/body/eval_jaxpr/ppermute | solution.py:24
  828.3 19.8 %collective-permute-start.3 = (f32[96,1024]{1,0:T(8,128)S(1)}, f32[96,1024]{1,0:T(8,128)S(1)}, u32[]{:S(2)}, u32[]{:S(2)}) collective-permute-start(f32[96,1024]{1,0:T(8,128)S(1)} %convolution_add_fusion.5), channel_id=1, source_target_pairs={{0,4},{4,8},{8,12},{12,16},{16,20},{20,24},{24,28},{28,32},{32,36}... | collective-permute-start | bytes 1179656 | tf_op jit(solution)/shard_map/while/body/eval_jaxpr/ppermute | solution.py:24
  828.7 19.3 %collective-permute-start.1 = (bf16[96,1024]{1,0:T(8,128)(2,1)}, bf16[96,1024]{1,0:T(8,128)(2,1)S(1)}, u32[]{:S(2)}, u32[]{:S(2)}) collective-permute-start(bf16[96,1024]{1,0:T(8,128)(2,1)} %copy-done.1), channel_id=1, source_target_pairs={{0,4},{4,8},{8,12},{12,16},{16,20},{20,24},{24,28},{28,32},{32,36}... | collective-permute-start | bytes 589832 | tf_op jit(solution)/shard_map/while/body/eval_jaxpr/ppermute | solution.py:24
  849.5 19.5 %collective-permute-start.2 = (f32[96,1024]{1,0:T(8,128)S(1)}, f32[96,1024]{1,0:T(8,128)S(1)}, u32[]{:S(2)}, u32[]{:S(2)}) collective-permute-start(f32[96,1024]{1,0:T(8,128)S(1)} %convolution_add_fusion.4), channel_id=1, source_target_pairs={{0,4},{4,8},{8,12},{12,16},{16,20},{20,24},{24,28},{28,32},{32,36}... | collective-permute-start | bytes 1179656 | tf_op jit(solution)/shard_map/while/body/eval_jaxpr/ppermute | solution.py:24
  869.4 20.2 %collective-permute-start.3 = (f32[96,1024]{1,0:T(8,128)S(1)}, f32[96,1024]{1,0:T(8,128)S(1)}, u32[]{:S(2)}, u32[]{:S(2)}) collective-permute-start(f32[96,1024]{1,0:T(8,128)S(1)} %convolution_add_fusion.5), channel_id=1, source_target_pairs={{0,4},{4,8},{8,12},{12,16},{16,20},{20,24},{24,28},{28,32},{32,36}... | collective-permute-start | bytes 1179656 | tf_op jit(solution)/shard_map/while/body/eval_jaxpr/ppermute | solution.py:24
  869.8 19.7 %collective-permute-start.1 = (bf16[96,1024]{1,0:T(8,128)(2,1)}, bf16[96,1024]{1,0:T(8,128)(2,1)S(1)}, u32[]{:S(2)}, u32[]{:S(2)}) collective-permute-start(bf16[96,1024]{1,0:T(8,128)(2,1)} %copy-done.1), channel_id=1, source_target_pairs={{0,4},{4,8},{8,12},{12,16},{16,20},{20,24},{24,28},{28,32},{32,36}... | collective-permute-start | bytes 589832 | tf_op jit(solution)/shard_map/while/body/eval_jaxpr/ppermute | solution.py:24
  (52 other events, 657.4 us)
Sparse Core Ops, SparseCore 0:
  11.1 94.9 all-gather.7
  889.7 51.4 reduce-scatter.1
where the time goes:
time: 1000 us
  waiting for transfers between devices  550 us (55%)
  blocking collectives  288 us (29%)
  matrix products  119 us (12%)
  between operations  18.6 us (2%)
    ppermute x64, waiting for transfers between devices, from_behind(): return lax.ppermute(value, axis, pairs)  452 us
    all_gather x4, blocking collectives, joined(): everything = jax.tree.map(lambda part: lax.all_gather(part, axis), value)  194 us
    all_gather x1, waiting for transfers between devices, on_device(): piece = lax.all_gather(text, 'blk', axis=0, tiled=True)  97.2 us
    psum x1, blocking collectives, on_device(): summed = lax.psum(local_terms, ('blk', 'inner'))  94.7 us
    dot_general x40, matrix products, scores(): return scale * jnp.dot(image, tile.T, preferred_element_type=jnp.float32)  55 us
    dot_general x32, matrix products, grad_tile(): grad_rows = grad_rows + jnp.dot(g, tile, preferred_element_type=jnp.float32)  54.5 us
  transfers between devices with their start and end apart: 66, of which 49 were waited for; matrix products, arithmetic and copies ran while one was open for 10% of the time, Pallas kernels for 0%

commit v1 on v0

v1 whole, which is shorter than its diff:
```python
import functools

import jax
import jax.numpy as jnp
from jax import lax
from jax.experimental import pallas as pl
from jax.experimental.pallas import tpu as pltpu
from jax.sharding import Mesh, PartitionSpec as P

AXES = ("x", "z", "yh", "yl", "c")
SIZES = (4, 4, 2, 2, 2)
PIECE = 96
CHIP = 2 * PIECE
KIND = 4 * CHIP
TILE = KIND // 2
WIDTH = 1024
EXTRA = 16
VMEM_LIMIT = 16 * 1024 * 1024

F32 = jnp.float32
BF16 = jnp.bfloat16
VMEM = pl.BlockSpec(memory_space=pltpu.VMEM)
SMEM = pl.BlockSpec(memory_space=pltpu.SMEM)


def pairs_of(move):
    def index(x, z, yh, yl, c):
        return (((x * 4 + z) * 2 + yh) * 2 + yl) * 2 + c

    return [
        (index(x, z, yh, yl, c), index(*move(x, z, yh, yl, c)))
        for x in range(4) for z in range(4) for yh in range(2) for yl in range(2) for c in range(2)
    ]


def on_ring(turn):
    return lambda x, z, yh, yl, c: (turn(x), z, yh, yl, c) if c == 0 else (x, turn(z), yh, yl, c)


AHEAD = [pairs_of(on_ring(lambda r, d=d: (r + d) % 4)) for d in range(4)]
PAIR_A = pairs_of(on_ring(lambda r: r ^ 1))
PAIR_B = pairs_of(on_ring(lambda r: r ^ 3))
flip_y = lambda x, z, yh, yl, c: (x, z, yh, 1 - yl, c) if c == 0 else (x, z, 1 - yh, yl, c)
FLIP_Y = pairs_of(flip_y)
CROSS_Y = pairs_of(lambda x, z, yh, yl, c: (*flip_y(x, z, yh, yl, c)[:4], 1 - c))
FLIP_YH = [(a, b) for a, b in FLIP_Y if a % 2 == 1]
FLIP_C = pairs_of(lambda x, z, yh, yl, c: (x, z, yh, yl, 1 - c))


def move(value, pairs):
    return lax.ppermute(value, AXES, pairs)


def call(body, out_shape, specs, scratch=(), flops=0, bytes_accessed=0, out_specs=None):
    return pl.pallas_call(
        body,
        out_shape=out_shape,
        in_specs=specs,
        out_specs=out_specs or jax.tree.map(lambda _: VMEM, out_shape),
        scratch_shapes=list(scratch),
        compiler_params=pltpu.CompilerParams(vmem_limit_bytes=VMEM_LIMIT),
        cost_estimate=pl.CostEstimate(flops=flops, bytes_accessed=bytes_accessed, transcendentals=0),
    )


def shape(*dims, dtype=F32):
    return jax.ShapeDtypeStruct(dims, dtype)


def lanes_of(s, combine):
    part = s[:, :128]
    for j in range(1, KIND // 128):
        part = combine(part, s[:, j * 128 : (j + 1) * 128])
    return part


def on_diagonal(j):
    row = lax.broadcasted_iota(jnp.int32, (TILE, 128), 0)
    return (row == lax.broadcasted_iota(jnp.int32, (TILE, 128), 1) + j * 128) & (row < CHIP)


def score_tiles(factor, rows, cols, s_ref, row_ref, col_max, col_sum):
    for r in range(2):
        part = slice(r * TILE, (r + 1) * TILE)
        s = factor * lax.dot_general(rows(part), cols(slice(None)), (((1,), (1,)), ((), ())), preferred_element_type=F32)
        s_ref[part, :] = s
        top = lanes_of(s, jnp.maximum)
        row_ref[0:1, part] = jnp.max(top.T, axis=0, keepdims=True)
        e = jnp.exp(s - jnp.max(top, axis=1, keepdims=True))
        row_ref[1:2, part] = jnp.sum(lanes_of(e, jnp.add).T, axis=0, keepdims=True)
        new_max = jnp.maximum(col_max, jnp.max(s, axis=0, keepdims=True))
        col_sum = col_sum * jnp.exp(col_max - new_max) + jnp.sum(jnp.exp(s - new_max), axis=0, keepdims=True)
        col_max = new_max
    return col_max, col_sum


def prepare(core, odd, image, text, text_c, first_ref, peer_ref):
    @pl.when(core[0] == 0)
    def _():
        first_ref[...] = image[...]
        peer_ref[:PIECE, :] = text[...]
        peer_ref[PIECE:, :] = text_c[...]

    @pl.when(core[0] == 1)
    def _():
        peer_ref[...] = image[...]
        first_ref[:PIECE, :] = text_c[...]
        first_ref[PIECE:, :] = text[...]


def scores_first(core, scale, *refs):
    a1, a2, b1 = refs[0:4], refs[4:8], refs[8:12]
    s_ref, x_ref, st_ref = refs[12:]
    me = core[0]
    for slot in range(4):
        at = slice(slot * CHIP, (slot + 1) * CHIP)
        x_ref[0, at, :] = b1[slot][...]

        @pl.when(me == 0)
        def _():
            x_ref[1, at, :] = a1[slot][...]

        @pl.when(me == 1)
        def _():
            x_ref[1, at, :] = a2[slot][...]

    st_ref[...] = jnp.ones((8, KIND), F32)
    col_max, col_sum = score_tiles(
        scale[0],
        lambda part: x_ref[1 - me, part, :],
        lambda part: x_ref[me, part, :],
        s_ref,
        st_ref,
        jnp.full((1, KIND), -1e30, F32),
        jnp.zeros((1, KIND), F32),
    )
    st_ref[4:5, :] = col_max
    st_ref[5:6, :] = col_sum
    total = jnp.zeros((1, 1), F32)
    for j in range(2):
        here = jnp.where(on_diagonal(j), s_ref[:TILE, j * 128 : (j + 1) * 128], 0.0)
        total += jnp.sum(jnp.sum(here, axis=0, keepdims=True), axis=1, keepdims=True)
    st_ref[6:7, :] = jnp.broadcast_to(total, (1, KIND))


def scores_second(core, scale, x_ref, st1, *refs):
    a2, text0, b2 = refs[0:4], refs[4], refs[5:8]
    s_ref, y_ref, st_ref, line = refs[8:]
    me = core[0]

    @pl.when(me == 0)
    def _():
        y_ref[0, :CHIP, :] = text0[...]
        for slot in range(4):
            y_ref[1, slot * CHIP : (slot + 1) * CHIP, :] = a2[slot][...]

    @pl.when(me == 1)
    def _():
        y_ref[0, :CHIP, :] = a2[0][...]

    for slot in range(1, 4):
        y_ref[0, slot * CHIP : (slot + 1) * CHIP, :] = b2[slot - 1][...]

    col_max, col_sum = score_tiles(
        scale[0],
        lambda part: y_ref[1 - me, part, :],
        lambda part: x_ref[me, part, :],
        s_ref,
        line,
        st1[4:5, :],
        st1[5:6, :],
    )
    st_ref[...] = jnp.concatenate(
        [st1[0:1, :], line[0:1, :], st1[1:2, :], line[1:2, :], col_max, col_sum, st1[6:8, :]], axis=0
    )


def join(a, b):
    top = jnp.maximum(a[0:2], b[0:2])
    total = a[2:4] * jnp.exp(a[0:2] - top) + b[2:4] * jnp.exp(b[0:2] - top)
    return jnp.concatenate([top, total, a[4:5] + b[4:5], jnp.ones((3, KIND), F32)], axis=0)


def join_cores(core, mine_ref, peer_ref, *refs):
    o_ref = refs[-1]
    a, b = mine_ref[...], peer_ref[...]
    rows = join(a[0:5], b[0:5])
    rows = jnp.concatenate([rows[0:4], a[6:7], rows[5:8]], axis=0)
    cols = jnp.concatenate([b[4:5], a[4:5], b[5:6], a[5:6], jnp.zeros((1, KIND), F32), rows[5:8]], axis=0)
    o_ref[...] = jnp.where(core[0] == 0, rows, cols)


def join_pair(a_ref, b_ref, *refs):
    o_ref = refs[-1]
    b = b_ref[...]
    o_ref[...] = join(a_ref[...], jnp.concatenate([b[1:2], b[0:1], b[3:4], b[2:3], b[4:8]], axis=0))


def join_ring(last, odd, a_ref, b_ref, *refs):
    o_ref = refs[-1]
    b = b_ref[...]
    one = jnp.concatenate([b[:, KIND - CHIP :], b[:, : KIND - CHIP]], axis=1)
    three = jnp.concatenate([b[:, CHIP:], b[:, :CHIP]], axis=1)
    out = join(a_ref[...], jnp.where((odd[0] == 1) == last, one, three))
    if last:
        out = jnp.concatenate([out[0:2] + jnp.log(out[2:4]), out[2:8]], axis=0)
    o_ref[...] = out


def grad_weights(kind, core, s_ref, mine_ref, peer_ref, g_ref):
    image = core[0] == 0
    rows = jnp.where(image, mine_ref[kind : kind + 1, :], peer_ref[kind : kind + 1, :])
    cols = jnp.where(image, peer_ref[0:1, :], mine_ref[1:2, :])
    for r in range(2):
        lse = jnp.broadcast_to(rows[:, r * TILE : (r + 1) * TILE], (128, TILE)).T
        for j in range(KIND // 128):
            at = slice(j * 128, (j + 1) * 128)
            s = s_ref[r * TILE : (r + 1) * TILE, at]
            g = 0.5 * (jnp.exp(s - lse) + jnp.exp(s - cols[:, at]))
            if kind == 0 and r == 0 and j < 2:
                g = g - jnp.where(on_diagonal(j) & image, 1.0, 0.0)
            g_ref[r * TILE : (r + 1) * TILE, at] = g.astype(BF16)


def spread(value):
    high = value.astype(BF16).astype(F32)
    middle = (value - high).astype(BF16).astype(F32)
    low = value - high - middle
    lane = lax.broadcasted_iota(jnp.int32, (EXTRA, WIDTH), 1)
    out = jnp.where(lane < 128, high, jnp.where(lane < 256, middle, low))
    return out.astype(BF16)


def gathered(rows):
    rows = rows[0:1, :].astype(F32)
    return rows[:, 0:1] + rows[:, 128:129] + rows[:, 256:257]


def product(core, half, left, left_t, first, second, outs):
    at = slice(half * TILE, (half + 1) * TILE)

    def write(out):
        for k in range(2):
            value = out[k * CHIP : (k + 1) * CHIP, :]
            outs[k][0:CHIP, :] = value if (half, k) == (0, 0) else value.astype(BF16)

    @pl.when(core[0] == 0)
    def _():
        out = jnp.dot(left[0][at, :], first[0], preferred_element_type=F32)
        write(out + jnp.dot(left[1][at, :], second[0], preferred_element_type=F32))

    @pl.when(core[0] == 1)
    def _():
        over = (((0,), (0,)), ((), ()))
        out = lax.dot_general(left_t[0][:, at], first[0], over, preferred_element_type=F32)
        write(out + lax.dot_general(left_t[1][:, at], second[0], over, preferred_element_type=F32))


def grads_other(half, core, g1, g2, r2, x_ref, y_ref, mine_ref, peer_ref, *outs):
    product(core, half, (g2, r2), (g1, g2), x_ref, y_ref, outs)
    peer = peer_ref[...]
    term = jnp.sum(jnp.sum(peer[0:2], axis=0, keepdims=True), axis=1, keepdims=True)
    term = term - jnp.where(core[0] == 0, 0.0, 2.0 * peer[4:5, 0:1])
    if half == 0:
        outs[2][...] = jnp.broadcast_to(term, (8, 128))
    for out in outs[1 - half : 2]:
        out[CHIP:, :] = spread(term)


def grads_own(half, core, g1, r1, r2, x_ref, y_ref, *outs):
    product(core, half, (g1, r1), (r1, r2), x_ref, y_ref, outs)


def sum_other(core, acc, r1, r2, r3, term, *refs):
    same_ref, cross_ref, total_ref = refs[-3:]
    out = acc[...]
    total = term[0:1, 0:1]
    for r in (r1, r2, r3):
        out = out + r[0:CHIP, :].astype(F32)
        total = total + gathered(r[CHIP:, :])
    low, high = out[:PIECE].astype(BF16), out[PIECE:].astype(BF16)
    image = core[0] == 0
    same_ref[...] = jnp.where(image, low, high)
    cross_ref[...] = jnp.where(image, high, low)
    total_ref[...] = jnp.broadcast_to(total, (8, 128))


def sum_own(core, acc, r1, r2, r3, total, pair_total, keep_ref, give_a_ref, give_b_ref, total_ref):
    out = acc[...]
    for r in (r1, r2, r3):
        out = out + r[...].astype(F32)
    low, high = out[:PIECE], out[PIECE:]
    image = core[0] == 0
    keep_ref[...] = jnp.where(image, low, high)
    give = jnp.where(image, high, low).astype(BF16)
    whole = total[...] + pair_total[...]
    give_a_ref[0 : PIECE // 2, :] = give[: PIECE // 2]
    give_a_ref[PIECE // 2 :, :] = spread(whole[0:1, 0:1])
    give_b_ref[...] = give[PIECE // 2 :]
    total_ref[...] = whole


def finish(core, scale, keep, got_a, got_b, same, cross, total, image_ref, text_ref, loss_ref):
    mine = (scale[0] * (keep[...] + same[...].astype(F32))).astype(BF16)
    got = jnp.concatenate([got_a[: PIECE // 2, :], got_b[...]], axis=0)
    other = (scale[0] * (got.astype(F32) + cross[...].astype(F32))).astype(BF16)
    image = core[0] == 0
    image_ref[...] = jnp.where(image, mine, other)
    text_ref[...] = jnp.where(image, other, mine)
    loss = total[0:1, 0:1] + gathered(got_a[PIECE // 2 :, :])
    loss_ref[0] = loss[0, 0] / (16.0 * 2 * KIND)


def on_device(image, text, logit_scale):
    c = lax.axis_index("c")
    yl = lax.axis_index("yl")
    is_image = c == 0
    ring = jnp.where(is_image, lax.axis_index("x"), lax.axis_index("z"))
    core = c.reshape(1)
    odd = (ring & 1).reshape(1)
    mat = functools.partial(shape, dtype=BF16)

    chip = mat(CHIP, WIDTH)
    image_own = lax.dynamic_slice_in_dim(image, yl * CHIP, CHIP, 0)
    image_other = lax.dynamic_slice_in_dim(image, (1 - yl) * CHIP, CHIP, 0)
    image_own, image_other = lax.optimization_barrier((image_own, image_other))
    first, peer_first = call(prepare, (chip, chip), [SMEM] * 2 + [VMEM] * 3)(core, odd, image_own, text, move(text, FLIP_C))
    text_y = move(first, FLIP_YH)
    ring1 = [move(first, AHEAD[4 - slot]) for slot in (1, 2, 3)]
    second = jnp.where(is_image, image_other, text_y)
    ring2 = [move(second, AHEAD[4 - slot]) for slot in (1, 2, 3)]
    peer1 = [move(v, FLIP_C) for v in ring1]
    text_yc = move(text_y, FLIP_C)
    peer2 = [move(v, FLIP_C) for v in ring2]

    half = 2 * KIND * KIND * WIDTH
    s1, x, st1 = call(
        scores_first,
        (shape(KIND, KIND), mat(2, KIND, WIDTH), shape(8, KIND)),
        [SMEM] * 2 + [VMEM] * 12,
        flops=half,
        bytes_accessed=KIND * KIND * 4,
    )(core, logit_scale, first, *ring1, second, *ring2, peer_first, *peer1)
    s2, y, st = call(
        scores_second,
        (shape(KIND, KIND), mat(2, KIND, WIDTH), shape(8, KIND)),
        [SMEM] * 2 + [VMEM] * 10,
        scratch=[pltpu.VMEM((8, KIND), F32)],
        flops=half,
        bytes_accessed=KIND * KIND * 4,
    )(core, logit_scale, x, st1, image_other, *ring2, text_yc, *peer2)

    stats = shape(8, KIND)
    held = (s1, s2, x, y)
    side = call(join_cores, stats, [SMEM] + [VMEM] * 6)(core, st, move(st, FLIP_C), *held)
    side = call(join_pair, stats, [VMEM] * 6)(side, move(side, FLIP_Y), *held)
    side = call(functools.partial(join_ring, False), stats, [SMEM] + [VMEM] * 6)(odd, side, move(side, PAIR_A), *held)
    side = call(functools.partial(join_ring, True), stats, [SMEM] + [VMEM] * 6)(odd, side, move(side, PAIR_B), *held)
    peer = move(side, FLIP_C)

    weights = lambda kind, s: call(functools.partial(grad_weights, kind), mat(KIND, KIND), [SMEM] + [VMEM] * 3)(
        core, s, side, peer
    )
    g2 = weights(1, s2)
    r2 = move(g2, FLIP_C)
    g1 = weights(0, s1)
    r1 = move(g1, FLIP_C)
    long, own, small = mat(CHIP + EXTRA, WIDTH), shape(CHIP, WIDTH), shape(8, 128)

    def grads(body, out_shape, *operands):
        return call(body, out_shape, [SMEM] + [VMEM] * len(operands), flops=half)(core, *operands)

    send_2, send_3 = grads(functools.partial(grads_other, 1), (long, long), g1, g2, r2, x, y, side, peer)
    acc2, send_1, term = grads(functools.partial(grads_other, 0), (own, long, small), g1, g2, r2, x, y, side, peer)
    got2 = [move(v, AHEAD[k + 1]) for k, v in enumerate((send_1, send_2, send_3))]
    send_2, send_3 = grads(functools.partial(grads_own, 1), (chip, chip), g1, r1, r2, x, y)
    acc1, send_1 = grads(functools.partial(grads_own, 0), (own, chip), g1, r1, r2, x, y)
    got1 = [move(v, AHEAD[k + 1]) for k, v in enumerate((send_1, send_2, send_3))]
    piece, part = mat(PIECE, WIDTH), mat(PIECE // 2, WIDTH)
    same, cross, total = call(sum_other, (piece, piece, small), [SMEM] + [VMEM] * 7)(core, acc2, *got2, term, send_2, acc1)
    pair_total = move(total, FLIP_Y)
    same, cross = move(same, FLIP_Y), move(cross, CROSS_Y)
    keep, give_a, give_b, total = call(
        sum_own, (shape(PIECE, WIDTH), mat(PIECE // 2 + EXTRA, WIDTH), part, small), [SMEM] + [VMEM] * 6
    )(core, acc1, *got1, total, pair_total)
    grad_image, grad_text, loss = call(
        finish, (piece, piece, shape(1)), [SMEM] * 2 + [VMEM] * 6, out_specs=(VMEM, VMEM, SMEM)
    )(core, logit_scale, keep, move(give_a, FLIP_C), move(give_b, FLIP_C), same, cross, total)
    return loss, grad_image, grad_text


def solution(mesh):
    fine = Mesh(mesh.devices.reshape(SIZES), AXES)
    every = P(AXES, None)
    return jax.shard_map(
        on_device,
        mesh=fine,
        in_specs=(P(("x", "z", "yh"), None), every, P()),
        out_specs=(P(), every, every),
        check_vma=False,
    )
```

time: 1000 us -> 88.8 us (0.09)
  waiting for transfers between devices: 550 us -> 33.5 us
  blocking collectives: 288 us -> 0 us
  matrix products: 119 us -> 0 us
  starting transfers between devices: 6.89 us -> 37.4 us
  between operations: 18.6 us -> 1.64 us
  Pallas kernels: 0 us -> 14 us
    ppermute x64 -> x33, waiting for transfers between devices: 452 us -> 33.5 us  [move(): return lax.ppermute(value, AXES, pairs)]
    all_gather x4 -> x0, blocking collectives: 194 us -> none  [joined(): everything = jax.tree.map(lambda part: lax.all_gather(part, axis), value)]
    dot_general x104 -> x0, matrix products: 119 us -> none  [the longest x40 55 us: scores(): return scale * jnp.dot(image, tile.T, preferred_element_type=jnp.float32)]
    all_gather x1 -> x0, waiting for transfers between devices: 97.2 us -> none  [on_device(): piece = lax.all_gather(text, 'blk', axis=0, tiled=True)]
    psum x1 -> x0, blocking collectives: 94.7 us -> none  [on_device(): summed = lax.psum(local_terms, ('blk', 'inner'))]
    ppermute x64 -> x33, starting transfers between devices: 6.81 us -> 37.4 us  [move(): return lax.ppermute(value, AXES, pairs)]
    pallas_call x0 -> x16, Pallas kernels: none -> 14 us  [the longest x4 5.94 us: grads(): call(body, out_shape, [SMEM] + [VMEM] * len(operands), flops=half)]
  transfers between devices with their start and end apart: 66 -> 33, of which waited for: 49 -> 15; matrix products, arithmetic and copies ran while one was open for 10% -> 1% of each run, Pallas kernels for 0% -> 11%
where the time goes in v1:
time: 88.8 us; the launch traced here: 88.7 us
  starting transfers between devices  37.4 us (42%)
  waiting for transfers between devices  33.5 us (38%)
  Pallas kernels  14 us (16%)
  local copies, waits for them, and re-layouts  2.09 us (2%)
  between operations  1.64 us (2%)
    ppermute x33, starting transfers between devices, move(): return lax.ppermute(value, AXES, pairs)  37.4 us
    ppermute x33, waiting for transfers between devices, move(): return lax.ppermute(value, AXES, pairs)  33.5 us
    pallas_call x4, Pallas kernels, grads(): call(body, out_shape, [SMEM] + [VMEM] * len(operands), flops=half)  5.94 us
    pallas_call x1, Pallas kernels, on_device(): call(scores_first, (shape(KIND, KIND), mat(2, KIND, WIDTH), shape(8, KIND...  2.33 us
    pallas_call x1, Pallas kernels, on_device(): call(scores_second, (shape(KIND, KIND), mat(2, KIND, WIDTH), shape(8, KIN...  2.31 us
  transfers between devices with their start and end apart: 33, of which 15 were waited for; matrix products, arithmetic and copies ran while one was open for 1% of the time, Pallas kernels for 11%

profile of v1, /device:TPU:1, one launch (start us, length us, event | category | flops | bytes accessed | tf_op | source)
XLA Modules:
  0.0 88.7 jit_solution(14070142944656768101)
XLA Ops:
  0.6 1.5 %collective-permute-start = (bf16[96,1024]{1,0:T(8,128)(2,1)}, bf16[96,1024]{1,0:T(8,128)(2,1)S(1)}, u32[]{:S(2)}, u32[]{:S(2)}) collective-permute-start(bf16[96,1024]{1,0:T(8,128)(2,1)} %text.1), channel_id=1, source_target_pairs={{0,1},{1,0},{2,3},{3,2},{4,5},{5,4},{6,7},{7,6},{8,9},{9,8},{10,11... | collective-permute-start | bytes 589832 | tf_op jit(solution)/shard_map/ppermute | solution.py:51
  2.1 1.2 %constant_dynamic-slice_fusion = (bf16[192,1024]{1,0:T(8,128)(2,1)S(1)}, bf16[192,1024]{1,0:T(8,128)(2,1)S(1)}) fusion(bf16[384,1024]{1,0:T(8,128)(2,1)} %param.3, s32[]{:T(128)S(6)} %select_n.20, s32[]{:T(128)S(6)} %select_n.19), kind=kLoop, calls=%fused_computation.1 | loop fusion | bytes 1572872 | tf_op jit(solution)/shard_map/dynamic_slice | solution.py:325
  4.4 4.9 %collective-permute-start.4 = (bf16[192,1024]{1,0:T(8,128)(2,1)S(1)}, bf16[192,1024]{1,0:T(8,128)(2,1)S(1)}, u32[]{:S(2)}, u32[]{:S(2)}) collective-permute-start(bf16[192,1024]{1,0:T(8,128)(2,1)S(1)} %get-tuple-element.33.refs_0_), channel_id=1, source_target_pairs={{1,5},{3,7},{5,1},{7,3},{9,13},{11,15},{13,9},{15,11},{17,21},{19,... | collective-permute-start | bytes 1179656 | tf_op jit(solution)/shard_map/ppermute | solution.py:51
  9.3 1.7 %collective-permute-start.3 = (bf16[192,1024]{1,0:T(8,128)(2,1)S(1)}, bf16[192,1024]{1,0:T(8,128)(2,1)S(1)}, u32[]{:S(2)}, u32[]{:S(2)}) collective-permute-start(bf16[192,1024]{1,0:T(8,128)(2,1)S(1)} %get-tuple-element.33.refs_0_), channel_id=1, source_target_pairs={{0,32},{1,9},{2,34},{3,11},{4,36},{5,13},{6,38},{7,15},{8,40},{9,1... | collective-permute-start | bytes 1179656 | tf_op jit(solution)/shard_map/ppermute | solution.py:51
  11.0 3.3 %collective-permute-start.2 = (bf16[192,1024]{1,0:T(8,128)(2,1)S(1)}, bf16[192,1024]{1,0:T(8,128)(2,1)S(1)}, u32[]{:S(2)}, u32[]{:S(2)}) collective-permute-start(bf16[192,1024]{1,0:T(8,128)(2,1)S(1)} %get-tuple-element.33.refs_0_), channel_id=1, source_target_pairs={{0,64},{1,17},{2,66},{3,19},{4,68},{5,21},{6,70},{7,23},{8,72},{9,... | collective-permute-start | bytes 1179656 | tf_op jit(solution)/shard_map/ppermute | solution.py:51
  15.1 1.2 %collective-permute-start.7 = (bf16[192,1024]{1,0:T(8,128)(2,1)S(1)}, bf16[192,1024]{1,0:T(8,128)(2,1)S(1)}, u32[]{:S(2)}, u32[]{:S(2)}) collective-permute-start(bf16[192,1024]{1,0:T(8,128)(2,1)S(1)} %broadcast_select_fusion.refs_4_), channel_id=1, source_target_pairs={{0,32},{1,9},{2,34},{3,11},{4,36},{5,13},{6,38},{7,15},{8,40},{9,1... | collective-permute-start | bytes 1179656 | tf_op jit(solution)/shard_map/ppermute | solution.py:51
  16.3 3.3 %collective-permute-start.6 = (bf16[192,1024]{1,0:T(8,128)(2,1)S(1)}, bf16[192,1024]{1,0:T(8,128)(2,1)S(1)}, u32[]{:S(2)}, u32[]{:S(2)}) collective-permute-start(bf16[192,1024]{1,0:T(8,128)(2,1)S(1)} %broadcast_select_fusion.refs_4_), channel_id=1, source_target_pairs={{0,64},{1,17},{2,66},{3,19},{4,68},{5,21},{6,70},{7,23},{8,72},{9,... | collective-permute-start | bytes 1179656 | tf_op jit(solution)/shard_map/ppermute | solution.py:51
  20.3 3.7 %collective-permute-done.2.refs_2_ = bf16[192,1024]{1,0:T(8,128)(2,1)S(1)} collective-permute-done((bf16[192,1024]{1,0:T(8,128)(2,1)S(1)}, bf16[192,1024]{1,0:T(8,128)(2,1)S(1)}, u32[]{:S(2)}, u32[]{:S(2)}) %collective-permute-start.2) | collective-permute-done | bytes 393248 | tf_op jit(solution)/shard_map/ppermute | solution.py:51
  24.5 3.3 %collective-permute-done.7.refs_7_.refs_3_ = bf16[192,1024]{1,0:T(8,128)(2,1)S(1)} collective-permute-done((bf16[192,1024]{1,0:T(8,128)(2,1)S(1)}, bf16[192,1024]{1,0:T(8,128)(2,1)S(1)}, u32[]{:S(2)}, u32[]{:S(2)}) %collective-permute-start.7) | collective-permute-done | bytes 393248 | tf_op jit(solution)/shard_map/ppermute | solution.py:51
  27.9 4.3 %collective-permute-done.6.refs_6_.refs_2_ = bf16[192,1024]{1,0:T(8,128)(2,1)S(1)} collective-permute-done((bf16[192,1024]{1,0:T(8,128)(2,1)S(1)}, bf16[192,1024]{1,0:T(8,128)(2,1)S(1)}, u32[]{:S(2)}, u32[]{:S(2)}) %collective-permute-start.6) | collective-permute-done | bytes 393248 | tf_op jit(solution)/shard_map/ppermute | solution.py:51
  33.9 2.3 %shard_map.59 = (f32[768,768]{1,0:T(8,128)S(1)}, bf16[2,768,1024]{2,1,0:T(8,128)(2,1)S(1)}, f32[8,768]{1,0:T(8,128)S(1)}) custom-call(s32[1]{0:T(128)} %bitcast.core, f32[1]{0:T(128)S(6)} %copy.6.scale, bf16[192,1024]{1,0:T(8,128)(2,1)S(1)} %get-tuple-element.33.refs_0_, bf16[192,1024]{1,0:T(8,128)(2,1)S(1)} %collective-permute-done.1.refs_1_, ...), custom_call_target="tpu_custom_call" | custom-call | flops 1207959552 | bytes 2359296 | tf_op jit(solution)/shard_map/pallas_call | solution.py:337
  36.2 2.3 %shard_map.60 = (f32[768,768]{1,0:T(8,128)S(1)}, bf16[2,768,1024]{2,1,0:T(8,128)(2,1)S(1)}, f32[8,768]{1,0:T(8,128)S(1)}) custom-call(s32[1]{0:T(128)} %bitcast.core, f32[1]{0:T(128)S(6)} %copy.6.scale, bf16[2,768,1024]{2,1,0:T(8,128)(2,1)S(1)} %get-tuple-element.37.x_ref.refs_2_, f32[8,768]{1,0:T(8,128)S(1)} %get-tuple-element.38.st1, ...), custom_call_target="tpu_custom_call" | custom-call | flops 1207959552 | bytes 2359296 | tf_op jit(solution)/shard_map/pallas_call | solution.py:344
  38.8 1.0 %collective-permute-done.15.peer_ref = f32[8,768]{1,0:T(8,128)S(1)} collective-permute-done((f32[8,768]{1,0:T(8,128)S(1)}, f32[8,768]{1,0:T(8,128)S(1)}, u32[]{:S(2)}, u32[]{:S(2)}) %collective-permute-start.15) | collective-permute-done | bytes 24608 | tf_op jit(solution)/shard_map/ppermute | solution.py:51
  39.9 4.2 %collective-permute-done.16.b_ref = f32[8,768]{1,0:T(8,128)S(1)} collective-permute-done((f32[8,768]{1,0:T(8,128)S(1)}, f32[8,768]{1,0:T(8,128)S(1)}, u32[]{:S(2)}, u32[]{:S(2)}) %collective-permute-start.16) | collective-permute-done | bytes 24608 | tf_op jit(solution)/shard_map/ppermute | solution.py:51
  45.1 1.8 %collective-permute-done.17.b_ref = f32[8,768]{1,0:T(8,128)S(1)} collective-permute-done((f32[8,768]{1,0:T(8,128)S(1)}, f32[8,768]{1,0:T(8,128)S(1)}, u32[]{:S(2)}, u32[]{:S(2)}) %collective-permute-start.17) | collective-permute-done | bytes 24608 | tf_op jit(solution)/shard_map/ppermute | solution.py:51
  47.0 1.8 %collective-permute-start.18 = (f32[8,768]{1,0:T(8,128)S(1)}, f32[8,768]{1,0:T(8,128)S(1)}, u32[]{:S(2)}, u32[]{:S(2)}) collective-permute-start(f32[8,768]{1,0:T(8,128)S(1)} %shard_map.63.a_ref), channel_id=1, source_target_pairs={{0,96},{1,25},{2,98},{3,27},{4,100},{5,29},{6,102},{7,31},{8,104},... | collective-permute-start | bytes 73736 | tf_op jit(solution)/shard_map/ppermute | solution.py:51
  48.8 2.2 %collective-permute-done.18.b_ref = f32[8,768]{1,0:T(8,128)S(1)} collective-permute-done((f32[8,768]{1,0:T(8,128)S(1)}, f32[8,768]{1,0:T(8,128)S(1)}, u32[]{:S(2)}, u32[]{:S(2)}) %collective-permute-start.18) | collective-permute-done | bytes 24608 | tf_op jit(solution)/shard_map/ppermute | solution.py:51
  51.1 2.2 %collective-permute-start.19 = (f32[8,768]{1,0:T(8,128)S(1)}, f32[8,768]{1,0:T(8,128)S(1)}, u32[]{:S(2)}, u32[]{:S(2)}) collective-permute-start(f32[8,768]{1,0:T(8,128)S(1)} %shard_map.64.mine_ref), channel_id=1, source_target_pairs={{0,1},{1,0},{2,3},{3,2},{4,5},{5,4},{6,7},{7,6},{8,9},{9,8},{10,11... | collective-permute-start | bytes 73736 | tf_op jit(solution)/shard_map/ppermute | solution.py:51
  56.5 1.5 %collective-permute-done.21.r2 = bf16[768,768]{1,0:T(8,128)(2,1)S(1)} collective-permute-done((bf16[768,768]{1,0:T(8,128)(2,1)S(1)}, bf16[768,768]{1,0:T(8,128)(2,1)S(1)}, u32[]{:S(2)}, u32[]{:S(2)}) %collective-permute-start.21) | collective-permute-done | bytes 1179680 | tf_op jit(solution)/shard_map/ppermute | solution.py:51
  58.0 1.6 %shard_map.70 = (bf16[208,1024]{1,0:T(8,128)(2,1)S(1)}, bf16[208,1024]{1,0:T(8,128)(2,1)S(1)}) custom-call(s32[1]{0:T(128)} %bitcast.core, bf16[768,768]{1,0:T(8,128)(2,1)S(1)} %shard_map.65.g1, bf16[768,768]{1,0:T(8,128)(2,1)S(1)} %shard_map.66.g2, bf16[768,768]{1,0:T(8,128)(2,1)S(1)} %collective-permute-done.21.r2, ...), custom_call_target="tpu_custom_call" | custom-call | flops 1207959552 | tf_op jit(solution)/shard_map/pallas_call | solution.py:371
  59.6 2.0 %collective-permute-start.26 = (bf16[208,1024]{1,0:T(8,128)(2,1)S(1)}, bf16[208,1024]{1,0:T(8,128)(2,1)S(1)}, u32[]{:S(2)}, u32[]{:S(2)}) collective-permute-start(bf16[208,1024]{1,0:T(8,128)(2,1)S(1)} %get-tuple-element.48), channel_id=1, source_target_pairs={{0,64},{1,17},{2,66},{3,19},{4,68},{5,21},{6,70},{7,23},{8,72},{9,... | collective-permute-start | bytes 1277960 | tf_op jit(solution)/shard_map/ppermute | solution.py:51
  61.5 1.4 %collective-permute-start.27 = (bf16[208,1024]{1,0:T(8,128)(2,1)S(1)}, bf16[208,1024]{1,0:T(8,128)(2,1)S(1)}, u32[]{:S(2)}, u32[]{:S(2)}) collective-permute-start(bf16[208,1024]{1,0:T(8,128)(2,1)S(1)} %get-tuple-element.49), channel_id=1, source_target_pairs={{0,96},{1,25},{2,98},{3,27},{4,100},{5,29},{6,102},{7,31},{8,104},... | collective-permute-start | bytes 1277960 | tf_op jit(solution)/shard_map/ppermute | solution.py:51
  62.9 1.6 %shard_map.69 = (f32[192,1024]{1,0:T(8,128)S(1)}, bf16[208,1024]{1,0:T(8,128)(2,1)S(1)}, f32[8,128]{1,0:T(8,128)S(1)}) custom-call(s32[1]{0:T(128)} %bitcast.core, bf16[768,768]{1,0:T(8,128)(2,1)S(1)} %shard_map.65.g1, bf16[768,768]{1,0:T(8,128)(2,1)S(1)} %shard_map.66.g2, bf16[768,768]{1,0:T(8,128)(2,1)S(1)} %collective-permute-done.21.r2, ...), custom_call_target="tpu_custom_call" | custom-call | flops 1207959552 | tf_op jit(solution)/shard_map/pallas_call | solution.py:371
  64.6 1.4 %shard_map.68 = (bf16[192,1024]{1,0:T(8,128)(2,1)S(1)}, bf16[192,1024]{1,0:T(8,128)(2,1)S(1)}) custom-call(s32[1]{0:T(128)} %bitcast.core, bf16[768,768]{1,0:T(8,128)(2,1)S(1)} %shard_map.65.g1, bf16[768,768]{1,0:T(8,128)(2,1)S(1)} %collective-permute-done.20.r1, bf16[768,768]{1,0:T(8,128)(2,1)S(1)} %collective-permute-done.21.r2, ...), custom_call_target="tpu_custom_call" | custom-call | flops 1207959552 | tf_op jit(solution)/shard_map/pallas_call | solution.py:371
  66.0 2.7 %collective-permute-start.24 = (bf16[192,1024]{1,0:T(8,128)(2,1)S(1)}, bf16[192,1024]{1,0:T(8,128)(2,1)S(1)}, u32[]{:S(2)}, u32[]{:S(2)}) collective-permute-start(bf16[192,1024]{1,0:T(8,128)(2,1)S(1)} %get-tuple-element.45), channel_id=1, source_target_pairs={{0,96},{1,25},{2,98},{3,27},{4,100},{5,29},{6,102},{7,31},{8,104},... | collective-permute-start | bytes 1179656 | tf_op jit(solution)/shard_map/ppermute | solution.py:51
  68.8 1.4 %shard_map.67 = (f32[192,1024]{1,0:T(8,128)S(1)}, bf16[192,1024]{1,0:T(8,128)(2,1)S(1)}) custom-call(s32[1]{0:T(128)} %bitcast.core, bf16[768,768]{1,0:T(8,128)(2,1)S(1)} %shard_map.65.g1, bf16[768,768]{1,0:T(8,128)(2,1)S(1)} %collective-permute-done.20.r1, bf16[768,768]{1,0:T(8,128)(2,1)S(1)} %collective-permute-done.21.r2, ...), custom_call_target="tpu_custom_call" | custom-call | flops 1207959552 | tf_op jit(solution)/shard_map/pallas_call | solution.py:371
  70.9 1.5 %collective-permute-done.27.r3 = bf16[208,1024]{1,0:T(8,128)(2,1)S(1)} collective-permute-done((bf16[208,1024]{1,0:T(8,128)(2,1)S(1)}, bf16[208,1024]{1,0:T(8,128)(2,1)S(1)}, u32[]{:S(2)}, u32[]{:S(2)}) %collective-permute-start.27) | collective-permute-done | bytes 426016 | tf_op jit(solution)/shard_map/ppermute | solution.py:51
  73.8 3.1 %collective-permute-start.32 = (bf16[96,1024]{1,0:T(8,128)(2,1)S(1)}, bf16[96,1024]{1,0:T(8,128)(2,1)S(1)}, u32[]{:S(2)}, u32[]{:S(2)}) collective-permute-start(bf16[96,1024]{1,0:T(8,128)(2,1)S(1)} %get-tuple-element.56), channel_id=1, source_target_pairs={{0,3},{1,4},{2,1},{3,6},{4,7},{5,0},{6,5},{7,2},{8,11},{9,12},{10,... | collective-permute-start | bytes 589832 | tf_op jit(solution)/shard_map/ppermute | solution.py:51
  76.9 1.4 %collective-permute-start.28 = (f32[8,128]{1,0:T(8,128)S(1)}, f32[8,128]{1,0:T(8,128)S(1)}, u32[]{:S(2)}, u32[]{:S(2)}) collective-permute-start(f32[8,128]{1,0:T(8,128)S(1)} %get-tuple-element.51.total), channel_id=1, source_target_pairs={{0,2},{1,5},{2,0},{3,7},{4,6},{5,1},{6,4},{7,3},{8,10},{9,13},{10,... | collective-permute-start | bytes 12296 | tf_op jit(solution)/shard_map/ppermute | solution.py:51
  78.3 3.2 %collective-permute-done.22.r1 = bf16[192,1024]{1,0:T(8,128)(2,1)S(1)} collective-permute-done((bf16[192,1024]{1,0:T(8,128)(2,1)S(1)}, bf16[192,1024]{1,0:T(8,128)(2,1)S(1)}, u32[]{:S(2)}, u32[]{:S(2)}) %collective-permute-start.22) | collective-permute-done | bytes 393248 | tf_op jit(solution)/shard_map/ppermute | solution.py:51
  81.5 4.1 %collective-permute-done.28.pair_total = f32[8,128]{1,0:T(8,128)S(1)} collective-permute-done((f32[8,128]{1,0:T(8,128)S(1)}, f32[8,128]{1,0:T(8,128)S(1)}, u32[]{:S(2)}, u32[]{:S(2)}) %collective-permute-start.28) | collective-permute-done | bytes 4128 | tf_op jit(solution)/shard_map/ppermute | solution.py:51
  86.6 1.0 %collective-permute-done.30.got_b = bf16[48,1024]{1,0:T(8,128)(2,1)S(1)} collective-permute-done((bf16[48,1024]{1,0:T(8,128)(2,1)S(1)}, bf16[48,1024]{1,0:T(8,128)(2,1)S(1)}, u32[]{:S(2)}, u32[]{:S(2)}) %collective-permute-start.30) | collective-permute-done | bytes 98336 | tf_op jit(solution)/shard_map/ppermute | solution.py:51
  (54 shorter events, 13.0 us)
Async XLA Ops:
  0.6 2.8 %collective-permute-start = (bf16[96,1024]{1,0:T(8,128)(2,1)}, bf16[96,1024]{1,0:T(8,128)(2,1)S(1)}, u32[]{:S(2)}, u32[]{:S(2)}) collective-permute-start(bf16[96,1024]{1,0:T(8,128)(2,1)} %text.1), channel_id=1, source_target_pairs={{0,1},{1,0},{2,3},{3,2},{4,5},{5,4},{6,7},{7,6},{8,9},{9,8},{10,11... | collective-permute-start | bytes 589832 | tf_op jit(solution)/shard_map/ppermute | solution.py:51
  4.4 10.7 %collective-permute-start.4 = (bf16[192,1024]{1,0:T(8,128)(2,1)S(1)}, bf16[192,1024]{1,0:T(8,128)(2,1)S(1)}, u32[]{:S(2)}, u32[]{:S(2)}) collective-permute-start(bf16[192,1024]{1,0:T(8,128)(2,1)S(1)} %get-tuple-element.33.refs_0_), channel_id=1, source_target_pairs={{1,5},{3,7},{5,1},{7,3},{9,13},{11,15},{13,9},{15,11},{17,21},{19,... | collective-permute-start | bytes 1179656 | tf_op jit(solution)/shard_map/ppermute | solution.py:51
  9.3 10.3 %collective-permute-start.3 = (bf16[192,1024]{1,0:T(8,128)(2,1)S(1)}, bf16[192,1024]{1,0:T(8,128)(2,1)S(1)}, u32[]{:S(2)}, u32[]{:S(2)}) collective-permute-start(bf16[192,1024]{1,0:T(8,128)(2,1)S(1)} %get-tuple-element.33.refs_0_), channel_id=1, source_target_pairs={{0,32},{1,9},{2,34},{3,11},{4,36},{5,13},{6,38},{7,15},{8,40},{9,1... | collective-permute-start | bytes 1179656 | tf_op jit(solution)/shard_map/ppermute | solution.py:51
  11.0 13.0 %collective-permute-start.2 = (bf16[192,1024]{1,0:T(8,128)(2,1)S(1)}, bf16[192,1024]{1,0:T(8,128)(2,1)S(1)}, u32[]{:S(2)}, u32[]{:S(2)}) collective-permute-start(bf16[192,1024]{1,0:T(8,128)(2,1)S(1)} %get-tuple-element.33.refs_0_), channel_id=1, source_target_pairs={{0,64},{1,17},{2,66},{3,19},{4,68},{5,21},{6,70},{7,23},{8,72},{9,... | collective-permute-start | bytes 1179656 | tf_op jit(solution)/shard_map/ppermute | solution.py:51
  14.3 9.7 %collective-permute-start.1 = (bf16[192,1024]{1,0:T(8,128)(2,1)S(1)}, bf16[192,1024]{1,0:T(8,128)(2,1)S(1)}, u32[]{:S(2)}, u32[]{:S(2)}) collective-permute-start(bf16[192,1024]{1,0:T(8,128)(2,1)S(1)} %get-tuple-element.33.refs_0_), channel_id=1, source_target_pairs={{0,96},{1,25},{2,98},{3,27},{4,100},{5,29},{6,102},{7,31},{8,104},... | collective-permute-start | bytes 1179656 | tf_op jit(solution)/shard_map/ppermute | solution.py:51
  15.1 12.8 %collective-permute-start.7 = (bf16[192,1024]{1,0:T(8,128)(2,1)S(1)}, bf16[192,1024]{1,0:T(8,128)(2,1)S(1)}, u32[]{:S(2)}, u32[]{:S(2)}) collective-permute-start(bf16[192,1024]{1,0:T(8,128)(2,1)S(1)} %broadcast_select_fusion.refs_4_), channel_id=1, source_target_pairs={{0,32},{1,9},{2,34},{3,11},{4,36},{5,13},{6,38},{7,15},{8,40},{9,1... | collective-permute-start | bytes 1179656 | tf_op jit(solution)/shard_map/ppermute | solution.py:51
  16.3 15.9 %collective-permute-start.6 = (bf16[192,1024]{1,0:T(8,128)(2,1)S(1)}, bf16[192,1024]{1,0:T(8,128)(2,1)S(1)}, u32[]{:S(2)}, u32[]{:S(2)}) collective-permute-start(bf16[192,1024]{1,0:T(8,128)(2,1)S(1)} %broadcast_select_fusion.refs_4_), channel_id=1, source_target_pairs={{0,64},{1,17},{2,66},{3,19},{4,68},{5,21},{6,70},{7,23},{8,72},{9,... | collective-permute-start | bytes 1179656 | tf_op jit(solution)/shard_map/ppermute | solution.py:51
  19.6 12.6 %collective-permute-start.5 = (bf16[192,1024]{1,0:T(8,128)(2,1)S(1)}, bf16[192,1024]{1,0:T(8,128)(2,1)S(1)}, u32[]{:S(2)}, u32[]{:S(2)}) collective-permute-start(bf16[192,1024]{1,0:T(8,128)(2,1)S(1)} %broadcast_select_fusion.refs_4_), channel_id=1, source_target_pairs={{0,96},{1,25},{2,98},{3,27},{4,100},{5,29},{6,102},{7,31},{8,104},... | collective-permute-start | bytes 1179656 | tf_op jit(solution)/shard_map/ppermute | solution.py:51
  24.0 8.6 %collective-permute-start.10 = (bf16[192,1024]{1,0:T(8,128)(2,1)S(1)}, bf16[192,1024]{1,0:T(8,128)(2,1)S(1)}, u32[]{:S(2)}, u32[]{:S(2)}) collective-permute-start(bf16[192,1024]{1,0:T(8,128)(2,1)S(1)} %collective-permute-done.3.refs_3_), channel_id=1, source_target_pairs={{0,1},{1,0},{2,3},{3,2},{4,5},{5,4},{6,7},{7,6},{8,9},{9,8},{10,11... | collective-permute-start | bytes 1179656 | tf_op jit(solution)/shard_map/ppermute | solution.py:51
  24.0 8.7 %collective-permute-start.9 = (bf16[192,1024]{1,0:T(8,128)(2,1)S(1)}, bf16[192,1024]{1,0:T(8,128)(2,1)S(1)}, u32[]{:S(2)}, u32[]{:S(2)}) collective-permute-start(bf16[192,1024]{1,0:T(8,128)(2,1)S(1)} %collective-permute-done.2.refs_2_), channel_id=1, source_target_pairs={{0,1},{1,0},{2,3},{3,2},{4,5},{5,4},{6,7},{7,6},{8,9},{9,8},{10,11... | collective-permute-start | bytes 1179656 | tf_op jit(solution)/shard_map/ppermute | solution.py:51
  27.9 6.0 %collective-permute-start.8 = (bf16[192,1024]{1,0:T(8,128)(2,1)S(1)}, bf16[192,1024]{1,0:T(8,128)(2,1)S(1)}, u32[]{:S(2)}, u32[]{:S(2)}) collective-permute-start(bf16[192,1024]{1,0:T(8,128)(2,1)S(1)} %collective-permute-done.1.refs_1_), channel_id=1, source_target_pairs={{0,1},{1,0},{2,3},{3,2},{4,5},{5,4},{6,7},{7,6},{8,9},{9,8},{10,11... | collective-permute-start | bytes 1179656 | tf_op jit(solution)/shard_map/ppermute | solution.py:51
  32.2 4.0 %collective-permute-start.11 = (bf16[192,1024]{1,0:T(8,128)(2,1)S(1)}, bf16[192,1024]{1,0:T(8,128)(2,1)S(1)}, u32[]{:S(2)}, u32[]{:S(2)}) collective-permute-start(bf16[192,1024]{1,0:T(8,128)(2,1)S(1)} %collective-permute-done.4), channel_id=1, source_target_pairs={{0,1},{1,0},{2,3},{3,2},{4,5},{5,4},{6,7},{7,6},{8,9},{9,8},{10,11... | collective-permute-start | bytes 1179656 | tf_op jit(solution)/shard_map/ppermute | solution.py:51
  32.2 4.0 %collective-permute-start.14 = (bf16[192,1024]{1,0:T(8,128)(2,1)S(1)}, bf16[192,1024]{1,0:T(8,128)(2,1)S(1)}, u32[]{:S(2)}, u32[]{:S(2)}) collective-permute-start(bf16[192,1024]{1,0:T(8,128)(2,1)S(1)} %collective-permute-done.7.refs_7_.refs_3_), channel_id=1, source_target_pairs={{0,1},{1,0},{2,3},{3,2},{4,5},{5,4},{6,7},{7,6},{8,9},{9,8},{10,11... | collective-permute-start | bytes 1179656 | tf_op jit(solution)/shard_map/ppermute | solution.py:51
  32.7 3.5 %collective-permute-start.13 = (bf16[192,1024]{1,0:T(8,128)(2,1)S(1)}, bf16[192,1024]{1,0:T(8,128)(2,1)S(1)}, u32[]{:S(2)}, u32[]{:S(2)}) collective-permute-start(bf16[192,1024]{1,0:T(8,128)(2,1)S(1)} %collective-permute-done.6.refs_6_.refs_2_), channel_id=1, source_target_pairs={{0,1},{1,0},{2,3},{3,2},{4,5},{5,4},{6,7},{7,6},{8,9},{9,8},{10,11... | collective-permute-start | bytes 1179656 | tf_op jit(solution)/shard_map/ppermute | solution.py:51
  32.8 3.5 %collective-permute-start.12 = (bf16[192,1024]{1,0:T(8,128)(2,1)S(1)}, bf16[192,1024]{1,0:T(8,128)(2,1)S(1)}, u32[]{:S(2)}, u32[]{:S(2)}) collective-permute-start(bf16[192,1024]{1,0:T(8,128)(2,1)S(1)} %collective-permute-done.5.refs_5_.refs_1_), channel_id=1, source_target_pairs={{0,1},{1,0},{2,3},{3,2},{4,5},{5,4},{6,7},{7,6},{8,9},{9,8},{10,11... | collective-permute-start | bytes 1179656 | tf_op jit(solution)/shard_map/ppermute | solution.py:51
  39.9 4.3 %collective-permute-start.16 = (f32[8,768]{1,0:T(8,128)S(1)}, f32[8,768]{1,0:T(8,128)S(1)}, u32[]{:S(2)}, u32[]{:S(2)}) collective-permute-start(f32[8,768]{1,0:T(8,128)S(1)} %shard_map.61.a_ref), channel_id=1, source_target_pairs={{0,2},{1,5},{2,0},{3,7},{4,6},{5,1},{6,4},{7,3},{8,10},{9,13},{10,... | collective-permute-start | bytes 73736 | tf_op jit(solution)/shard_map/ppermute | solution.py:51
  44.1 2.8 %collective-permute-start.17 = (f32[8,768]{1,0:T(8,128)S(1)}, f32[8,768]{1,0:T(8,128)S(1)}, u32[]{:S(2)}, u32[]{:S(2)}) collective-permute-start(f32[8,768]{1,0:T(8,128)S(1)} %shard_map.62.a_ref), channel_id=1, source_target_pairs={{0,32},{1,9},{2,34},{3,11},{4,36},{5,13},{6,38},{7,15},{8,40},{9,1... | collective-permute-start | bytes 73736 | tf_op jit(solution)/shard_map/ppermute | solution.py:51
  47.0 4.0 %collective-permute-start.18 = (f32[8,768]{1,0:T(8,128)S(1)}, f32[8,768]{1,0:T(8,128)S(1)}, u32[]{:S(2)}, u32[]{:S(2)}) collective-permute-start(f32[8,768]{1,0:T(8,128)S(1)} %shard_map.63.a_ref), channel_id=1, source_target_pairs={{0,96},{1,25},{2,98},{3,27},{4,100},{5,29},{6,102},{7,31},{8,104},... | collective-permute-start | bytes 73736 | tf_op jit(solution)/shard_map/ppermute | solution.py:51
  51.1 3.1 %collective-permute-start.19 = (f32[8,768]{1,0:T(8,128)S(1)}, f32[8,768]{1,0:T(8,128)S(1)}, u32[]{:S(2)}, u32[]{:S(2)}) collective-permute-start(f32[8,768]{1,0:T(8,128)S(1)} %shard_map.64.mine_ref), channel_id=1, source_target_pairs={{0,1},{1,0},{2,3},{3,2},{4,5},{5,4},{6,7},{7,6},{8,9},{9,8},{10,11... | collective-permute-start | bytes 73736 | tf_op jit(solution)/shard_map/ppermute | solution.py:51
  54.9 3.1 %collective-permute-start.21 = (bf16[768,768]{1,0:T(8,128)(2,1)S(1)}, bf16[768,768]{1,0:T(8,128)(2,1)S(1)}, u32[]{:S(2)}, u32[]{:S(2)}) collective-permute-start(bf16[768,768]{1,0:T(8,128)(2,1)S(1)} %shard_map.66.g2), channel_id=1, source_target_pairs={{0,1},{1,0},{2,3},{3,2},{4,5},{5,4},{6,7},{7,6},{8,9},{9,8},{10,11... | collective-permute-start | bytes 3538952 | tf_op jit(solution)/shard_map/ppermute | solution.py:51
  56.2 8.4 %collective-permute-start.20 = (bf16[768,768]{1,0:T(8,128)(2,1)S(1)}, bf16[768,768]{1,0:T(8,128)(2,1)S(1)}, u32[]{:S(2)}, u32[]{:S(2)}) collective-permute-start(bf16[768,768]{1,0:T(8,128)(2,1)S(1)} %shard_map.65.g1), channel_id=1, source_target_pairs={{0,1},{1,0},{2,3},{3,2},{4,5},{5,4},{6,7},{7,6},{8,9},{9,8},{10,11... | collective-permute-start | bytes 3538952 | tf_op jit(solution)/shard_map/ppermute | solution.py:51
  59.6 10.6 %collective-permute-start.26 = (bf16[208,1024]{1,0:T(8,128)(2,1)S(1)}, bf16[208,1024]{1,0:T(8,128)(2,1)S(1)}, u32[]{:S(2)}, u32[]{:S(2)}) collective-permute-start(bf16[208,1024]{1,0:T(8,128)(2,1)S(1)} %get-tuple-element.48), channel_id=1, source_target_pairs={{0,64},{1,17},{2,66},{3,19},{4,68},{5,21},{6,70},{7,23},{8,72},{9,... | collective-permute-start | bytes 1277960 | tf_op jit(solution)/shard_map/ppermute | solution.py:51
  61.5 10.9 %collective-permute-start.27 = (bf16[208,1024]{1,0:T(8,128)(2,1)S(1)}, bf16[208,1024]{1,0:T(8,128)(2,1)S(1)}, u32[]{:S(2)}, u32[]{:S(2)}) collective-permute-start(bf16[208,1024]{1,0:T(8,128)(2,1)S(1)} %get-tuple-element.49), channel_id=1, source_target_pairs={{0,96},{1,25},{2,98},{3,27},{4,100},{5,29},{6,102},{7,31},{8,104},... | collective-permute-start | bytes 1277960 | tf_op jit(solution)/shard_map/ppermute | solution.py:51
  64.5 8.6 %collective-permute-start.25 = (bf16[208,1024]{1,0:T(8,128)(2,1)S(1)}, bf16[208,1024]{1,0:T(8,128)(2,1)S(1)}, u32[]{:S(2)}, u32[]{:S(2)}) collective-permute-start(bf16[208,1024]{1,0:T(8,128)(2,1)S(1)} %get-tuple-element.47), channel_id=1, source_target_pairs={{0,32},{1,9},{2,34},{3,11},{4,36},{5,13},{6,38},{7,15},{8,40},{9,1... | collective-permute-start | bytes 1277960 | tf_op jit(solution)/shard_map/ppermute | solution.py:51
  66.0 10.8 %collective-permute-start.24 = (bf16[192,1024]{1,0:T(8,128)(2,1)S(1)}, bf16[192,1024]{1,0:T(8,128)(2,1)S(1)}, u32[]{:S(2)}, u32[]{:S(2)}) collective-permute-start(bf16[192,1024]{1,0:T(8,128)(2,1)S(1)} %get-tuple-element.45), channel_id=1, source_target_pairs={{0,96},{1,25},{2,98},{3,27},{4,100},{5,29},{6,102},{7,31},{8,104},... | collective-permute-start | bytes 1179656 | tf_op jit(solution)/shard_map/ppermute | solution.py:51
  68.8 9.5 %collective-permute-start.23 = (bf16[192,1024]{1,0:T(8,128)(2,1)S(1)}, bf16[192,1024]{1,0:T(8,128)(2,1)S(1)}, u32[]{:S(2)}, u32[]{:S(2)}) collective-permute-start(bf16[192,1024]{1,0:T(8,128)(2,1)S(1)} %get-tuple-element.44.refs_0_), channel_id=1, source_target_pairs={{0,64},{1,17},{2,66},{3,19},{4,68},{5,21},{6,70},{7,23},{8,72},{9,... | collective-permute-start | bytes 1179656 | tf_op jit(solution)/shard_map/ppermute | solution.py:51
  70.2 11.3 %collective-permute-start.22 = (bf16[192,1024]{1,0:T(8,128)(2,1)S(1)}, bf16[192,1024]{1,0:T(8,128)(2,1)S(1)}, u32[]{:S(2)}, u32[]{:S(2)}) collective-permute-start(bf16[192,1024]{1,0:T(8,128)(2,1)S(1)} %get-tuple-element.43), channel_id=1, source_target_pairs={{0,32},{1,9},{2,34},{3,11},{4,36},{5,13},{6,38},{7,15},{8,40},{9,1... | collective-permute-start | bytes 1179656 | tf_op jit(solution)/shard_map/ppermute | solution.py:51
  73.4 14.1 %collective-permute-start.31 = (bf16[96,1024]{1,0:T(8,128)(2,1)S(1)}, bf16[96,1024]{1,0:T(8,128)(2,1)S(1)}, u32[]{:S(2)}, u32[]{:S(2)}) collective-permute-start(bf16[96,1024]{1,0:T(8,128)(2,1)S(1)} %get-tuple-element.55), channel_id=1, source_target_pairs={{0,2},{1,5},{2,0},{3,7},{4,6},{5,1},{6,4},{7,3},{8,10},{9,13},{10,... | collective-permute-start | bytes 589832 | tf_op jit(solution)/shard_map/ppermute | solution.py:51
  73.8 13.8 %collective-permute-start.32 = (bf16[96,1024]{1,0:T(8,128)(2,1)S(1)}, bf16[96,1024]{1,0:T(8,128)(2,1)S(1)}, u32[]{:S(2)}, u32[]{:S(2)}) collective-permute-start(bf16[96,1024]{1,0:T(8,128)(2,1)S(1)} %get-tuple-element.56), channel_id=1, source_target_pairs={{0,3},{1,4},{2,1},{3,6},{4,7},{5,0},{6,5},{7,2},{8,11},{9,12},{10,... | collective-permute-start | bytes 589832 | tf_op jit(solution)/shard_map/ppermute | solution.py:51
  76.9 8.7 %collective-permute-start.28 = (f32[8,128]{1,0:T(8,128)S(1)}, f32[8,128]{1,0:T(8,128)S(1)}, u32[]{:S(2)}, u32[]{:S(2)}) collective-permute-start(f32[8,128]{1,0:T(8,128)S(1)} %get-tuple-element.51.total), channel_id=1, source_target_pairs={{0,2},{1,5},{2,0},{3,7},{4,6},{5,1},{6,4},{7,3},{8,10},{9,13},{10,... | collective-permute-start | bytes 12296 | tf_op jit(solution)/shard_map/ppermute | solution.py:51
  86.0 1.6 %collective-permute-start.29 = (bf16[64,1024]{1,0:T(8,128)(2,1)S(1)}, bf16[64,1024]{1,0:T(8,128)(2,1)S(1)}, u32[]{:S(2)}, u32[]{:S(2)}) collective-permute-start(bf16[64,1024]{1,0:T(8,128)(2,1)S(1)} %get-tuple-element.53), channel_id=1, source_target_pairs={{0,1},{1,0},{2,3},{3,2},{4,5},{5,4},{6,7},{7,6},{8,9},{9,8},{10,11... | collective-permute-start | bytes 393224 | tf_op jit(solution)/shard_map/ppermute | solution.py:51
  86.1 1.5 %collective-permute-start.30 = (bf16[48,1024]{1,0:T(8,128)(2,1)S(1)}, bf16[48,1024]{1,0:T(8,128)(2,1)S(1)}, u32[]{:S(2)}, u32[]{:S(2)}) collective-permute-start(bf16[48,1024]{1,0:T(8,128)(2,1)S(1)} %get-tuple-element.54), channel_id=1, source_target_pairs={{0,1},{1,0},{2,3},{3,2},{4,5},{5,4},{6,7},{7,6},{8,9},{9,8},{10,11... | collective-permute-start | bytes 294920 | tf_op jit(solution)/shard_map/ppermute | solution.py:51
  (2 other events, 2.2 us)

commit v2 on v1

--- a/solution.py
+++ b/solution.py
@@ -40,7 +40,7 @@
 AHEAD = [pairs_of(on_ring(lambda r, d=d: (r + d) % 4)) for d in range(4)]
 PAIR_A = pairs_of(on_ring(lambda r: r ^ 1))
 PAIR_B = pairs_of(on_ring(lambda r: r ^ 3))
-flip_y = lambda x, z, yh, yl, c: (x, z, yh, 1 - yl, c) if c == 0 else (x, z, 1 - yh, yl, c)
+flip_y = lambda x, z, yh, yl, c: (x, z, yh, 1 - yl, c) if c == 0 else (x, z, 1 - yh, 1 - yl, c)
 FLIP_Y = pairs_of(flip_y)
 CROSS_Y = pairs_of(lambda x, z, yh, yl, c: (*flip_y(x, z, yh, yl, c)[:4], 1 - c))
 FLIP_YH = [(a, b) for a, b in FLIP_Y if a % 2 == 1]
@@ -196,15 +196,12 @@
     o_ref[...] = join(a_ref[...], jnp.concatenate([b[1:2], b[0:1], b[3:4], b[2:3], b[4:8]], axis=0))
 
 
-def join_ring(last, odd, a_ref, b_ref, *refs):
-    o_ref = refs[-1]
-    b = b_ref[...]
-    one = jnp.concatenate([b[:, KIND - CHIP :], b[:, : KIND - CHIP]], axis=1)
-    three = jnp.concatenate([b[:, CHIP:], b[:, :CHIP]], axis=1)
-    out = join(a_ref[...], jnp.where((odd[0] == 1) == last, one, three))
-    if last:
-        out = jnp.concatenate([out[0:2] + jnp.log(out[2:4]), out[2:8]], axis=0)
-    o_ref[...] = out
+def join_ring(a_ref, b1_ref, b2_ref, b3_ref, *refs):
+    out = a_ref[...]
+    for k, b_ref in enumerate((b1_ref, b2_ref, b3_ref)):
+        b, cut = b_ref[...], KIND - (k + 1) * CHIP
+        out = join(out, jnp.concatenate([b[:, cut:], b[:, :cut]], axis=1))
+    refs[-1][...] = jnp.concatenate([out[0:2] + jnp.log(out[2:4]), out[2:8]], axis=0)
 
 
 def grad_weights(kind, core, s_ref, mine_ref, peer_ref, g_ref):
@@ -328,7 +325,8 @@
     text_y = move(first, FLIP_YH)
     ring1 = [move(first, AHEAD[4 - slot]) for slot in (1, 2, 3)]
     second = jnp.where(is_image, image_other, text_y)
-    ring2 = [move(second, AHEAD[4 - slot]) for slot in (1, 2, 3)]
+    ring2 = [move(second, AHEAD[3]), move(ring1[1], FLIP_Y), move(second, AHEAD[1])]
+    ring1[0], ring1[1], ring1[2], ring2[1] = lax.optimization_barrier((*ring1, ring2[1]))
     peer1 = [move(v, FLIP_C) for v in ring1]
     text_yc = move(text_y, FLIP_C)
     peer2 = [move(v, FLIP_C) for v in ring2]
@@ -354,8 +352,8 @@
     held = (s1, s2, x, y)
     side = call(join_cores, stats, [SMEM] + [VMEM] * 6)(core, st, move(st, FLIP_C), *held)
     side = call(join_pair, stats, [VMEM] * 6)(side, move(side, FLIP_Y), *held)
-    side = call(functools.partial(join_ring, False), stats, [SMEM] + [VMEM] * 6)(odd, side, move(side, PAIR_A), *held)
-    side = call(functools.partial(join_ring, True), stats, [SMEM] + [VMEM] * 6)(odd, side, move(side, PAIR_B), *held)
+    others = [move(side, AHEAD[4 - k]) for k in (1, 2, 3)]
+    side = call(join_ring, stats, [VMEM] * 8)(side, *others, *held)
     peer = move(side, FLIP_C)
 
     weights = lambda kind, s: call(functools.partial(grad_weights, kind), mat(KIND, KIND), [SMEM] + [VMEM] * 3)(

time: 88.8 us -> 78.5 us (0.88)
  waiting for transfers between devices: 33.5 us -> 18.8 us
  starting transfers between devices: 37.4 us -> 41.8 us
    ppermute x33 -> x34, waiting for transfers between devices: 33.5 us -> 18.8 us  [move(): return lax.ppermute(value, AXES, pairs)]
    ppermute x33 -> x34, starting transfers between devices: 37.4 us -> 41.8 us  [move(): return lax.ppermute(value, AXES, pairs)]
  transfers between devices with their start and end apart: 33 -> 34, of which waited for: 15 -> 16; matrix products, arithmetic and copies ran while one was open for 1% -> 2% of each run, Pallas kernels for 11% -> 12%
where the time goes in v2:
time: 78.5 us; the launch traced here: 78.3 us
  starting transfers between devices  41.8 us (53%)
  waiting for transfers between devices  18.8 us (24%)
  Pallas kernels  13.9 us (18%)
  local copies, waits for them, and re-layouts  2.09 us (3%)
  between operations  1.63 us (2%)
    ppermute x34, starting transfers between devices, move(): return lax.ppermute(value, AXES, pairs)  41.8 us
    ppermute x34, waiting for transfers between devices, move(): return lax.ppermute(value, AXES, pairs)  18.8 us
    pallas_call x4, Pallas kernels, grads(): call(body, out_shape, [SMEM] + [VMEM] * len(operands), flops=half)  5.94 us
    pallas_call x1, Pallas kernels, on_device(): call(scores_first, (shape(KIND, KIND), mat(2, KIND, WIDTH), shape(8, KIND...  2.33 us
    pallas_call x1, Pallas kernels, on_device(): call(scores_second, (shape(KIND, KIND), mat(2, KIND, WIDTH), shape(8, KIN...  2.26 us
  transfers between devices with their start and end apart: 34, of which 16 were waited for; matrix products, arithmetic and copies ran while one was open for 2% of the time, Pallas kernels for 12%

profile of v2, /device:TPU:1, one launch (start us, length us, event | category | flops | bytes accessed | tf_op | source)
XLA Modules:
  0.0 78.3 jit_solution(14628482810110342965)
XLA Ops:
  0.6 1.5 %collective-permute-start = (bf16[96,1024]{1,0:T(8,128)(2,1)}, bf16[96,1024]{1,0:T(8,128)(2,1)S(1)}, u32[]{:S(2)}, u32[]{:S(2)}) collective-permute-start(bf16[96,1024]{1,0:T(8,128)(2,1)} %text.1), channel_id=1, source_target_pairs={{0,1},{1,0},{2,3},{3,2},{4,5},{5,4},{6,7},{7,6},{8,9},{9,8},{10,11... | collective-permute-start | bytes 589832 | tf_op jit(solution)/shard_map/ppermute | solution.py:51
  2.1 1.2 %constant_dynamic-slice_fusion = (bf16[192,1024]{1,0:T(8,128)(2,1)S(1)}, bf16[192,1024]{1,0:T(8,128)(2,1)S(1)}) fusion(bf16[384,1024]{1,0:T(8,128)(2,1)} %param.3, s32[]{:T(128)S(6)} %select_n.20, s32[]{:T(128)S(6)} %select_n.19), kind=kLoop, calls=%fused_computation.1 | loop fusion | bytes 1572872 | tf_op jit(solution)/shard_map/dynamic_slice | solution.py:322
  4.4 3.8 %collective-permute-start.2 = (bf16[192,1024]{1,0:T(8,128)(2,1)S(1)}, bf16[192,1024]{1,0:T(8,128)(2,1)S(1)}, u32[]{:S(2)}, u32[]{:S(2)}) collective-permute-start(bf16[192,1024]{1,0:T(8,128)(2,1)S(1)} %get-tuple-element.37.refs_0_), channel_id=1, source_target_pairs={{0,64},{1,17},{2,66},{3,19},{4,68},{5,21},{6,70},{7,23},{8,72},{9,... | collective-permute-start | bytes 1179656 | tf_op jit(solution)/shard_map/ppermute | solution.py:51
  8.2 4.6 %collective-permute-start.5 = (bf16[192,1024]{1,0:T(8,128)(2,1)S(1)}, bf16[192,1024]{1,0:T(8,128)(2,1)S(1)}, u32[]{:S(2)}, u32[]{:S(2)}) collective-permute-start(bf16[192,1024]{1,0:T(8,128)(2,1)S(1)} %get-tuple-element.37.refs_0_), channel_id=1, source_target_pairs={{1,7},{3,5},{5,3},{7,1},{9,15},{11,13},{13,11},{15,9},{17,23},{19,... | collective-permute-start | bytes 1179656 | tf_op jit(solution)/shard_map/ppermute | solution.py:51
  13.6 1.9 %collective-permute-start.1 = (bf16[192,1024]{1,0:T(8,128)(2,1)S(1)}, bf16[192,1024]{1,0:T(8,128)(2,1)S(1)}, u32[]{:S(2)}, u32[]{:S(2)}) collective-permute-start(bf16[192,1024]{1,0:T(8,128)(2,1)S(1)} %get-tuple-element.37.refs_0_), channel_id=1, source_target_pairs={{0,96},{1,25},{2,98},{3,27},{4,100},{5,29},{6,102},{7,31},{8,104},... | collective-permute-start | bytes 1179656 | tf_op jit(solution)/shard_map/ppermute | solution.py:51
  16.4 1.6 %collective-permute-done.5 = bf16[192,1024]{1,0:T(8,128)(2,1)S(1)} collective-permute-done((bf16[192,1024]{1,0:T(8,128)(2,1)S(1)}, bf16[192,1024]{1,0:T(8,128)(2,1)S(1)}, u32[]{:S(2)}, u32[]{:S(2)}) %collective-permute-start.5) | collective-permute-done | bytes 393248 | tf_op jit(solution)/shard_map/ppermute | solution.py:51
  18.0 1.1 %collective-permute-start.7 = (bf16[192,1024]{1,0:T(8,128)(2,1)S(1)}, bf16[192,1024]{1,0:T(8,128)(2,1)S(1)}, u32[]{:S(2)}, u32[]{:S(2)}) collective-permute-start(bf16[192,1024]{1,0:T(8,128)(2,1)S(1)} %broadcast_select_fusion.refs_4_), channel_id=1, source_target_pairs={{0,32},{1,9},{2,34},{3,11},{4,36},{5,13},{6,38},{7,15},{8,40},{9,1... | collective-permute-start | bytes 1179656 | tf_op jit(solution)/shard_map/ppermute | solution.py:51
  19.1 1.7 %collective-permute-start.6 = (bf16[192,1024]{1,0:T(8,128)(2,1)S(1)}, bf16[192,1024]{1,0:T(8,128)(2,1)S(1)}, u32[]{:S(2)}, u32[]{:S(2)}) collective-permute-start(bf16[192,1024]{1,0:T(8,128)(2,1)S(1)} %broadcast_select_fusion.refs_4_), channel_id=1, source_target_pairs={{0,96},{1,25},{2,98},{3,27},{4,100},{5,29},{6,102},{7,31},{8,104},... | collective-permute-start | bytes 1179656 | tf_op jit(solution)/shard_map/ppermute | solution.py:51
  21.0 2.7 %collective-permute-done.4.refs_6_.refs_2_ = bf16[192,1024]{1,0:T(8,128)(2,1)S(1)} collective-permute-done((bf16[192,1024]{1,0:T(8,128)(2,1)S(1)}, bf16[192,1024]{1,0:T(8,128)(2,1)S(1)}, u32[]{:S(2)}, u32[]{:S(2)}) %collective-permute-start.4) | collective-permute-done | bytes 393248 | tf_op jit(solution)/shard_map/ppermute | solution.py:51
  24.2 1.7 %collective-permute-done.7.refs_7_.refs_3_ = bf16[192,1024]{1,0:T(8,128)(2,1)S(1)} collective-permute-done((bf16[192,1024]{1,0:T(8,128)(2,1)S(1)}, bf16[192,1024]{1,0:T(8,128)(2,1)S(1)}, u32[]{:S(2)}, u32[]{:S(2)}) %collective-permute-start.7) | collective-permute-done | bytes 393248 | tf_op jit(solution)/shard_map/ppermute | solution.py:51
  27.6 2.3 %shard_map.59 = (f32[768,768]{1,0:T(8,128)S(1)}, bf16[2,768,1024]{2,1,0:T(8,128)(2,1)S(1)}, f32[8,768]{1,0:T(8,128)S(1)}) custom-call(s32[1]{0:T(128)} %bitcast.core, f32[1]{0:T(128)S(6)} %copy.6.scale, bf16[192,1024]{1,0:T(8,128)(2,1)S(1)} %get-tuple-element.37.refs_0_, bf16[192,1024]{1,0:T(8,128)(2,1)S(1)} %collective-permute-done.1.refs_1_, ...), custom_call_target="tpu_custom_call" | custom-call | flops 1207959552 | bytes 2359296 | tf_op jit(solution)/shard_map/pallas_call | solution.py:335
  30.0 2.3 %shard_map.60 = (f32[768,768]{1,0:T(8,128)S(1)}, bf16[2,768,1024]{2,1,0:T(8,128)(2,1)S(1)}, f32[8,768]{1,0:T(8,128)S(1)}) custom-call(s32[1]{0:T(128)} %bitcast.core, f32[1]{0:T(128)S(6)} %copy.6.scale, bf16[2,768,1024]{2,1,0:T(8,128)(2,1)S(1)} %get-tuple-element.45.x_ref.refs_2_, f32[8,768]{1,0:T(8,128)S(1)} %get-tuple-element.46.st1, ...), custom_call_target="tpu_custom_call" | custom-call | flops 1207959552 | bytes 2359296 | tf_op jit(solution)/shard_map/pallas_call | solution.py:342
  32.5 1.0 %collective-permute-done.15.peer_ref = f32[8,768]{1,0:T(8,128)S(1)} collective-permute-done((f32[8,768]{1,0:T(8,128)S(1)}, f32[8,768]{1,0:T(8,128)S(1)}, u32[]{:S(2)}, u32[]{:S(2)}) %collective-permute-start.15) | collective-permute-done | bytes 24608 | tf_op jit(solution)/shard_map/ppermute | solution.py:51
  33.6 2.9 %collective-permute-start.16 = (f32[8,768]{1,0:T(8,128)S(1)}, f32[8,768]{1,0:T(8,128)S(1)}, u32[]{:S(2)}, u32[]{:S(2)}) collective-permute-start(f32[8,768]{1,0:T(8,128)S(1)} %shard_map.61.a_ref), channel_id=1, source_target_pairs={{0,2},{1,7},{2,0},{3,5},{4,6},{5,3},{6,4},{7,1},{8,10},{9,15},{10,... | collective-permute-start | bytes 73736 | tf_op jit(solution)/shard_map/ppermute | solution.py:51
  36.5 1.2 %collective-permute-done.16.b_ref = f32[8,768]{1,0:T(8,128)S(1)} collective-permute-done((f32[8,768]{1,0:T(8,128)S(1)}, f32[8,768]{1,0:T(8,128)S(1)}, u32[]{:S(2)}, u32[]{:S(2)}) %collective-permute-start.16) | collective-permute-done | bytes 24608 | tf_op jit(solution)/shard_map/ppermute | solution.py:51
  38.1 3.3 %collective-permute-start.18 = (f32[8,768]{1,0:T(8,128)S(1)}, f32[8,768]{1,0:T(8,128)S(1)}, u32[]{:S(2)}, u32[]{:S(2)}) collective-permute-start(f32[8,768]{1,0:T(8,128)S(1)} %shard_map.62.a_ref), channel_id=1, source_target_pairs={{0,64},{1,17},{2,66},{3,19},{4,68},{5,21},{6,70},{7,23},{8,72},{9,... | collective-permute-start | bytes 73736 | tf_op jit(solution)/shard_map/ppermute | solution.py:51
  42.9 1.3 %collective-permute-done.17.b1_ref = f32[8,768]{1,0:T(8,128)S(1)} collective-permute-done((f32[8,768]{1,0:T(8,128)S(1)}, f32[8,768]{1,0:T(8,128)S(1)}, u32[]{:S(2)}, u32[]{:S(2)}) %collective-permute-start.17) | collective-permute-done | bytes 24608 | tf_op jit(solution)/shard_map/ppermute | solution.py:51
  44.3 1.8 %collective-permute-start.20 = (f32[8,768]{1,0:T(8,128)S(1)}, f32[8,768]{1,0:T(8,128)S(1)}, u32[]{:S(2)}, u32[]{:S(2)}) collective-permute-start(f32[8,768]{1,0:T(8,128)S(1)} %shard_map.63.mine_ref), channel_id=1, source_target_pairs={{0,1},{1,0},{2,3},{3,2},{4,5},{5,4},{6,7},{7,6},{8,9},{9,8},{10,11... | collective-permute-start | bytes 73736 | tf_op jit(solution)/shard_map/ppermute | solution.py:51
  49.3 1.5 %collective-permute-done.22.r2 = bf16[768,768]{1,0:T(8,128)(2,1)S(1)} collective-permute-done((bf16[768,768]{1,0:T(8,128)(2,1)S(1)}, bf16[768,768]{1,0:T(8,128)(2,1)S(1)}, u32[]{:S(2)}, u32[]{:S(2)}) %collective-permute-start.22) | collective-permute-done | bytes 1179680 | tf_op jit(solution)/shard_map/ppermute | solution.py:51
  50.8 1.6 %shard_map.69 = (bf16[208,1024]{1,0:T(8,128)(2,1)S(1)}, bf16[208,1024]{1,0:T(8,128)(2,1)S(1)}) custom-call(s32[1]{0:T(128)} %bitcast.core, bf16[768,768]{1,0:T(8,128)(2,1)S(1)} %shard_map.64.g1, bf16[768,768]{1,0:T(8,128)(2,1)S(1)} %shard_map.65.g2, bf16[768,768]{1,0:T(8,128)(2,1)S(1)} %collective-permute-done.22.r2, ...), custom_call_target="tpu_custom_call" | custom-call | flops 1207959552 | tf_op jit(solution)/shard_map/pallas_call | solution.py:369
  52.4 2.6 %collective-permute-start.27 = (bf16[208,1024]{1,0:T(8,128)(2,1)S(1)}, bf16[208,1024]{1,0:T(8,128)(2,1)S(1)}, u32[]{:S(2)}, u32[]{:S(2)}) collective-permute-start(bf16[208,1024]{1,0:T(8,128)(2,1)S(1)} %get-tuple-element.56), channel_id=1, source_target_pairs={{0,64},{1,17},{2,66},{3,19},{4,68},{5,21},{6,70},{7,23},{8,72},{9,... | collective-permute-start | bytes 1277960 | tf_op jit(solution)/shard_map/ppermute | solution.py:51
  55.4 1.6 %shard_map.68 = (f32[192,1024]{1,0:T(8,128)S(1)}, bf16[208,1024]{1,0:T(8,128)(2,1)S(1)}, f32[8,128]{1,0:T(8,128)S(1)}) custom-call(s32[1]{0:T(128)} %bitcast.core, bf16[768,768]{1,0:T(8,128)(2,1)S(1)} %shard_map.64.g1, bf16[768,768]{1,0:T(8,128)(2,1)S(1)} %shard_map.65.g2, bf16[768,768]{1,0:T(8,128)(2,1)S(1)} %collective-permute-done.22.r2, ...), custom_call_target="tpu_custom_call" | custom-call | flops 1207959552 | tf_op jit(solution)/shard_map/pallas_call | solution.py:369
  57.0 1.1 %collective-permute-start.26 = (bf16[208,1024]{1,0:T(8,128)(2,1)S(1)}, bf16[208,1024]{1,0:T(8,128)(2,1)S(1)}, u32[]{:S(2)}, u32[]{:S(2)}) collective-permute-start(bf16[208,1024]{1,0:T(8,128)(2,1)S(1)} %get-tuple-element.55), channel_id=1, source_target_pairs={{0,32},{1,9},{2,34},{3,11},{4,36},{5,13},{6,38},{7,15},{8,40},{9,1... | collective-permute-start | bytes 1277960 | tf_op jit(solution)/shard_map/ppermute | solution.py:51
  58.1 1.4 %shard_map.67 = (bf16[192,1024]{1,0:T(8,128)(2,1)S(1)}, bf16[192,1024]{1,0:T(8,128)(2,1)S(1)}) custom-call(s32[1]{0:T(128)} %bitcast.core, bf16[768,768]{1,0:T(8,128)(2,1)S(1)} %shard_map.64.g1, bf16[768,768]{1,0:T(8,128)(2,1)S(1)} %collective-permute-done.21.r1, bf16[768,768]{1,0:T(8,128)(2,1)S(1)} %collective-permute-done.22.r2, ...), custom_call_target="tpu_custom_call" | custom-call | flops 1207959552 | tf_op jit(solution)/shard_map/pallas_call | solution.py:369
  59.5 1.7 %collective-permute-start.25 = (bf16[192,1024]{1,0:T(8,128)(2,1)S(1)}, bf16[192,1024]{1,0:T(8,128)(2,1)S(1)}, u32[]{:S(2)}, u32[]{:S(2)}) collective-permute-start(bf16[192,1024]{1,0:T(8,128)(2,1)S(1)} %get-tuple-element.53), channel_id=1, source_target_pairs={{0,96},{1,25},{2,98},{3,27},{4,100},{5,29},{6,102},{7,31},{8,104},... | collective-permute-start | bytes 1179656 | tf_op jit(solution)/shard_map/ppermute | solution.py:51
  62.1 1.4 %shard_map.66 = (f32[192,1024]{1,0:T(8,128)S(1)}, bf16[192,1024]{1,0:T(8,128)(2,1)S(1)}) custom-call(s32[1]{0:T(128)} %bitcast.core, bf16[768,768]{1,0:T(8,128)(2,1)S(1)} %shard_map.64.g1, bf16[768,768]{1,0:T(8,128)(2,1)S(1)} %collective-permute-done.21.r1, bf16[768,768]{1,0:T(8,128)(2,1)S(1)} %collective-permute-done.22.r2, ...), custom_call_target="tpu_custom_call" | custom-call | flops 1207959552 | tf_op jit(solution)/shard_map/pallas_call | solution.py:369
  63.7 2.5 %collective-permute-done.28.r3 = bf16[208,1024]{1,0:T(8,128)(2,1)S(1)} collective-permute-done((bf16[208,1024]{1,0:T(8,128)(2,1)S(1)}, bf16[208,1024]{1,0:T(8,128)(2,1)S(1)}, u32[]{:S(2)}, u32[]{:S(2)}) %collective-permute-start.28) | collective-permute-done | bytes 426016 | tf_op jit(solution)/shard_map/ppermute | solution.py:51
  66.6 2.7 %collective-permute-start.32 = (bf16[96,1024]{1,0:T(8,128)(2,1)S(1)}, bf16[96,1024]{1,0:T(8,128)(2,1)S(1)}, u32[]{:S(2)}, u32[]{:S(2)}) collective-permute-start(bf16[96,1024]{1,0:T(8,128)(2,1)S(1)} %get-tuple-element.63), channel_id=1, source_target_pairs={{0,2},{1,7},{2,0},{3,5},{4,6},{5,3},{6,4},{7,1},{8,10},{9,15},{10,... | collective-permute-start | bytes 589832 | tf_op jit(solution)/shard_map/ppermute | solution.py:51
  70.4 2.6 %collective-permute-start.29 = (f32[8,128]{1,0:T(8,128)S(1)}, f32[8,128]{1,0:T(8,128)S(1)}, u32[]{:S(2)}, u32[]{:S(2)}) collective-permute-start(f32[8,128]{1,0:T(8,128)S(1)} %get-tuple-element.59.total), channel_id=1, source_target_pairs={{0,2},{1,7},{2,0},{3,5},{4,6},{5,3},{6,4},{7,1},{8,10},{9,15},{10,... | collective-permute-start | bytes 12296 | tf_op jit(solution)/shard_map/ppermute | solution.py:51
  73.0 1.2 %collective-permute-done.23.r1 = bf16[192,1024]{1,0:T(8,128)(2,1)S(1)} collective-permute-done((bf16[192,1024]{1,0:T(8,128)(2,1)S(1)}, bf16[192,1024]{1,0:T(8,128)(2,1)S(1)}, u32[]{:S(2)}, u32[]{:S(2)}) %collective-permute-start.23) | collective-permute-done | bytes 393248 | tf_op jit(solution)/shard_map/ppermute | solution.py:51
  76.0 1.2 %collective-permute-done.31.got_b = bf16[48,1024]{1,0:T(8,128)(2,1)S(1)} collective-permute-done((bf16[48,1024]{1,0:T(8,128)(2,1)S(1)}, bf16[48,1024]{1,0:T(8,128)(2,1)S(1)}, u32[]{:S(2)}, u32[]{:S(2)}) %collective-permute-start.31) | collective-permute-done | bytes 98336 | tf_op jit(solution)/shard_map/ppermute | solution.py:51
  77.2 0.9 %shard_map.72 = (bf16[96,1024]{1,0:T(8,128)(2,1)}, bf16[96,1024]{1,0:T(8,128)(2,1)}, f32[1]{0:T(128)}) custom-call(s32[1]{0:T(128)} %bitcast.core, f32[1]{0:T(128)S(6)} %copy.6.scale, f32[96,1024]{1,0:T(8,128)S(1)} %get-tuple-element.60.keep, bf16[64,1024]{1,0:T(8,128)(2,1)S(1)} %collective-permute-done.30.got_a, ...), custom_call_target="tpu_custom_call" | custom-call | tf_op jit(solution)/shard_map/pallas_call | solution.py:384
  (55 shorter events, 14.8 us)
Async XLA Ops:
  0.6 2.8 %collective-permute-start = (bf16[96,1024]{1,0:T(8,128)(2,1)}, bf16[96,1024]{1,0:T(8,128)(2,1)S(1)}, u32[]{:S(2)}, u32[]{:S(2)}) collective-permute-start(bf16[96,1024]{1,0:T(8,128)(2,1)} %text.1), channel_id=1, source_target_pairs={{0,1},{1,0},{2,3},{3,2},{4,5},{5,4},{6,7},{7,6},{8,9},{9,8},{10,11... | collective-permute-start | bytes 589832 | tf_op jit(solution)/shard_map/ppermute | solution.py:51
  4.4 11.1 %collective-permute-start.2 = (bf16[192,1024]{1,0:T(8,128)(2,1)S(1)}, bf16[192,1024]{1,0:T(8,128)(2,1)S(1)}, u32[]{:S(2)}, u32[]{:S(2)}) collective-permute-start(bf16[192,1024]{1,0:T(8,128)(2,1)S(1)} %get-tuple-element.37.refs_0_), channel_id=1, source_target_pairs={{0,64},{1,17},{2,66},{3,19},{4,68},{5,21},{6,70},{7,23},{8,72},{9,... | collective-permute-start | bytes 1179656 | tf_op jit(solution)/shard_map/ppermute | solution.py:51
  8.2 9.8 %collective-permute-start.5 = (bf16[192,1024]{1,0:T(8,128)(2,1)S(1)}, bf16[192,1024]{1,0:T(8,128)(2,1)S(1)}, u32[]{:S(2)}, u32[]{:S(2)}) collective-permute-start(bf16[192,1024]{1,0:T(8,128)(2,1)S(1)} %get-tuple-element.37.refs_0_), channel_id=1, source_target_pairs={{1,7},{3,5},{5,3},{7,1},{9,15},{11,13},{13,11},{15,9},{17,23},{19,... | collective-permute-start | bytes 1179656 | tf_op jit(solution)/shard_map/ppermute | solution.py:51
  12.8 8.2 %collective-permute-start.3 = (bf16[192,1024]{1,0:T(8,128)(2,1)S(1)}, bf16[192,1024]{1,0:T(8,128)(2,1)S(1)}, u32[]{:S(2)}, u32[]{:S(2)}) collective-permute-start(bf16[192,1024]{1,0:T(8,128)(2,1)S(1)} %get-tuple-element.37.refs_0_), channel_id=1, source_target_pairs={{0,32},{1,9},{2,34},{3,11},{4,36},{5,13},{6,38},{7,15},{8,40},{9,1... | collective-permute-start | bytes 1179656 | tf_op jit(solution)/shard_map/ppermute | solution.py:51
  13.6 7.4 %collective-permute-start.1 = (bf16[192,1024]{1,0:T(8,128)(2,1)S(1)}, bf16[192,1024]{1,0:T(8,128)(2,1)S(1)}, u32[]{:S(2)}, u32[]{:S(2)}) collective-permute-start(bf16[192,1024]{1,0:T(8,128)(2,1)S(1)} %get-tuple-element.37.refs_0_), channel_id=1, source_target_pairs={{0,96},{1,25},{2,98},{3,27},{4,100},{5,29},{6,102},{7,31},{8,104},... | collective-permute-start | bytes 1179656 | tf_op jit(solution)/shard_map/ppermute | solution.py:51
  15.5 8.1 %collective-permute-start.4 = (bf16[192,1024]{1,0:T(8,128)(2,1)S(1)}, bf16[192,1024]{1,0:T(8,128)(2,1)S(1)}, u32[]{:S(2)}, u32[]{:S(2)}) collective-permute-start(bf16[192,1024]{1,0:T(8,128)(2,1)S(1)} %collective-permute-done.2.refs_2_), channel_id=1, source_target_pairs={{0,2},{1,7},{2,0},{3,5},{4,6},{5,3},{6,4},{7,1},{8,10},{9,15},{10,... | collective-permute-start | bytes 1179656 | tf_op jit(solution)/shard_map/ppermute | solution.py:51
  18.0 7.9 %collective-permute-start.7 = (bf16[192,1024]{1,0:T(8,128)(2,1)S(1)}, bf16[192,1024]{1,0:T(8,128)(2,1)S(1)}, u32[]{:S(2)}, u32[]{:S(2)}) collective-permute-start(bf16[192,1024]{1,0:T(8,128)(2,1)S(1)} %broadcast_select_fusion.refs_4_), channel_id=1, source_target_pairs={{0,32},{1,9},{2,34},{3,11},{4,36},{5,13},{6,38},{7,15},{8,40},{9,1... | collective-permute-start | bytes 1179656 | tf_op jit(solution)/shard_map/ppermute | solution.py:51
  19.1 6.8 %collective-permute-start.6 = (bf16[192,1024]{1,0:T(8,128)(2,1)S(1)}, bf16[192,1024]{1,0:T(8,128)(2,1)S(1)}, u32[]{:S(2)}, u32[]{:S(2)}) collective-permute-start(bf16[192,1024]{1,0:T(8,128)(2,1)S(1)} %broadcast_select_fusion.refs_4_), channel_id=1, source_target_pairs={{0,96},{1,25},{2,98},{3,27},{4,100},{5,29},{6,102},{7,31},{8,104},... | collective-permute-start | bytes 1179656 | tf_op jit(solution)/shard_map/ppermute | solution.py:51
  23.7 2.8 %collective-permute-start.8 = (bf16[192,1024]{1,0:T(8,128)(2,1)S(1)}, bf16[192,1024]{1,0:T(8,128)(2,1)S(1)}, u32[]{:S(2)}, u32[]{:S(2)}) collective-permute-start(bf16[192,1024]{1,0:T(8,128)(2,1)S(1)} %collective-permute-done.1.refs_1_), channel_id=1, source_target_pairs={{0,1},{1,0},{2,3},{3,2},{4,5},{5,4},{6,7},{7,6},{8,9},{9,8},{10,11... | collective-permute-start | bytes 1179656 | tf_op jit(solution)/shard_map/ppermute | solution.py:51
  23.7 2.8 %collective-permute-start.9 = (bf16[192,1024]{1,0:T(8,128)(2,1)S(1)}, bf16[192,1024]{1,0:T(8,128)(2,1)S(1)}, u32[]{:S(2)}, u32[]{:S(2)}) collective-permute-start(bf16[192,1024]{1,0:T(8,128)(2,1)S(1)} %collective-permute-done.2.refs_2_), channel_id=1, source_target_pairs={{0,1},{1,0},{2,3},{3,2},{4,5},{5,4},{6,7},{7,6},{8,9},{9,8},{10,11... | collective-permute-start | bytes 1179656 | tf_op jit(solution)/shard_map/ppermute | solution.py:51
  24.2 3.4 %collective-permute-start.10 = (bf16[192,1024]{1,0:T(8,128)(2,1)S(1)}, bf16[192,1024]{1,0:T(8,128)(2,1)S(1)}, u32[]{:S(2)}, u32[]{:S(2)}) collective-permute-start(bf16[192,1024]{1,0:T(8,128)(2,1)S(1)} %collective-permute-done.3.refs_3_), channel_id=1, source_target_pairs={{0,1},{1,0},{2,3},{3,2},{4,5},{5,4},{6,7},{7,6},{8,9},{9,8},{10,11... | collective-permute-start | bytes 1179656 | tf_op jit(solution)/shard_map/ppermute | solution.py:51
  25.9 4.0 %collective-permute-start.11 = (bf16[192,1024]{1,0:T(8,128)(2,1)S(1)}, bf16[192,1024]{1,0:T(8,128)(2,1)S(1)}, u32[]{:S(2)}, u32[]{:S(2)}) collective-permute-start(bf16[192,1024]{1,0:T(8,128)(2,1)S(1)} %collective-permute-done.5), channel_id=1, source_target_pairs={{0,1},{1,0},{2,3},{3,2},{4,5},{5,4},{6,7},{7,6},{8,9},{9,8},{10,11... | collective-permute-start | bytes 1179656 | tf_op jit(solution)/shard_map/ppermute | solution.py:51
  25.9 4.0 %collective-permute-start.14 = (bf16[192,1024]{1,0:T(8,128)(2,1)S(1)}, bf16[192,1024]{1,0:T(8,128)(2,1)S(1)}, u32[]{:S(2)}, u32[]{:S(2)}) collective-permute-start(bf16[192,1024]{1,0:T(8,128)(2,1)S(1)} %collective-permute-done.7.refs_7_.refs_3_), channel_id=1, source_target_pairs={{0,1},{1,0},{2,3},{3,2},{4,5},{5,4},{6,7},{7,6},{8,9},{9,8},{10,11... | collective-permute-start | bytes 1179656 | tf_op jit(solution)/shard_map/ppermute | solution.py:51
  26.4 3.5 %collective-permute-start.12 = (bf16[192,1024]{1,0:T(8,128)(2,1)S(1)}, bf16[192,1024]{1,0:T(8,128)(2,1)S(1)}, u32[]{:S(2)}, u32[]{:S(2)}) collective-permute-start(bf16[192,1024]{1,0:T(8,128)(2,1)S(1)} %collective-permute-done.6.refs_5_.refs_1_), channel_id=1, source_target_pairs={{0,1},{1,0},{2,3},{3,2},{4,5},{5,4},{6,7},{7,6},{8,9},{9,8},{10,11... | collective-permute-start | bytes 1179656 | tf_op jit(solution)/shard_map/ppermute | solution.py:51
  26.5 3.5 %collective-permute-start.13 = (bf16[192,1024]{1,0:T(8,128)(2,1)S(1)}, bf16[192,1024]{1,0:T(8,128)(2,1)S(1)}, u32[]{:S(2)}, u32[]{:S(2)}) collective-permute-start(bf16[192,1024]{1,0:T(8,128)(2,1)S(1)} %collective-permute-done.4.refs_6_.refs_2_), channel_id=1, source_target_pairs={{0,1},{1,0},{2,3},{3,2},{4,5},{5,4},{6,7},{7,6},{8,9},{9,8},{10,11... | collective-permute-start | bytes 1179656 | tf_op jit(solution)/shard_map/ppermute | solution.py:51
  33.6 4.1 %collective-permute-start.16 = (f32[8,768]{1,0:T(8,128)S(1)}, f32[8,768]{1,0:T(8,128)S(1)}, u32[]{:S(2)}, u32[]{:S(2)}) collective-permute-start(f32[8,768]{1,0:T(8,128)S(1)} %shard_map.61.a_ref), channel_id=1, source_target_pairs={{0,2},{1,7},{2,0},{3,5},{4,6},{5,3},{6,4},{7,1},{8,10},{9,15},{10,... | collective-permute-start | bytes 73736 | tf_op jit(solution)/shard_map/ppermute | solution.py:51
  37.7 4.5 %collective-permute-start.19 = (f32[8,768]{1,0:T(8,128)S(1)}, f32[8,768]{1,0:T(8,128)S(1)}, u32[]{:S(2)}, u32[]{:S(2)}) collective-permute-start(f32[8,768]{1,0:T(8,128)S(1)} %shard_map.62.a_ref), channel_id=1, source_target_pairs={{0,32},{1,9},{2,34},{3,11},{4,36},{5,13},{6,38},{7,15},{8,40},{9,1... | collective-permute-start | bytes 73736 | tf_op jit(solution)/shard_map/ppermute | solution.py:51
  38.1 4.8 %collective-permute-start.18 = (f32[8,768]{1,0:T(8,128)S(1)}, f32[8,768]{1,0:T(8,128)S(1)}, u32[]{:S(2)}, u32[]{:S(2)}) collective-permute-start(f32[8,768]{1,0:T(8,128)S(1)} %shard_map.62.a_ref), channel_id=1, source_target_pairs={{0,64},{1,17},{2,66},{3,19},{4,68},{5,21},{6,70},{7,23},{8,72},{9,... | collective-permute-start | bytes 73736 | tf_op jit(solution)/shard_map/ppermute | solution.py:51
  41.4 2.7 %collective-permute-start.17 = (f32[8,768]{1,0:T(8,128)S(1)}, f32[8,768]{1,0:T(8,128)S(1)}, u32[]{:S(2)}, u32[]{:S(2)}) collective-permute-start(f32[8,768]{1,0:T(8,128)S(1)} %shard_map.62.a_ref), channel_id=1, source_target_pairs={{0,96},{1,25},{2,98},{3,27},{4,100},{5,29},{6,102},{7,31},{8,104},... | collective-permute-start | bytes 73736 | tf_op jit(solution)/shard_map/ppermute | solution.py:51
  44.3 2.6 %collective-permute-start.20 = (f32[8,768]{1,0:T(8,128)S(1)}, f32[8,768]{1,0:T(8,128)S(1)}, u32[]{:S(2)}, u32[]{:S(2)}) collective-permute-start(f32[8,768]{1,0:T(8,128)S(1)} %shard_map.63.mine_ref), channel_id=1, source_target_pairs={{0,1},{1,0},{2,3},{3,2},{4,5},{5,4},{6,7},{7,6},{8,9},{9,8},{10,11... | collective-permute-start | bytes 73736 | tf_op jit(solution)/shard_map/ppermute | solution.py:51
  47.7 3.1 %collective-permute-start.22 = (bf16[768,768]{1,0:T(8,128)(2,1)S(1)}, bf16[768,768]{1,0:T(8,128)(2,1)S(1)}, u32[]{:S(2)}, u32[]{:S(2)}) collective-permute-start(bf16[768,768]{1,0:T(8,128)(2,1)S(1)} %shard_map.65.g2), channel_id=1, source_target_pairs={{0,1},{1,0},{2,3},{3,2},{4,5},{5,4},{6,7},{7,6},{8,9},{9,8},{10,11... | collective-permute-start | bytes 3538952 | tf_op jit(solution)/shard_map/ppermute | solution.py:51
  49.0 9.1 %collective-permute-start.21 = (bf16[768,768]{1,0:T(8,128)(2,1)S(1)}, bf16[768,768]{1,0:T(8,128)(2,1)S(1)}, u32[]{:S(2)}, u32[]{:S(2)}) collective-permute-start(bf16[768,768]{1,0:T(8,128)(2,1)S(1)} %shard_map.64.g1), channel_id=1, source_target_pairs={{0,1},{1,0},{2,3},{3,2},{4,5},{5,4},{6,7},{7,6},{8,9},{9,8},{10,11... | collective-permute-start | bytes 3538952 | tf_op jit(solution)/shard_map/ppermute | solution.py:51
  52.4 11.2 %collective-permute-start.27 = (bf16[208,1024]{1,0:T(8,128)(2,1)S(1)}, bf16[208,1024]{1,0:T(8,128)(2,1)S(1)}, u32[]{:S(2)}, u32[]{:S(2)}) collective-permute-start(bf16[208,1024]{1,0:T(8,128)(2,1)S(1)} %get-tuple-element.56), channel_id=1, source_target_pairs={{0,64},{1,17},{2,66},{3,19},{4,68},{5,21},{6,70},{7,23},{8,72},{9,... | collective-permute-start | bytes 1277960 | tf_op jit(solution)/shard_map/ppermute | solution.py:51
  55.0 11.2 %collective-permute-start.28 = (bf16[208,1024]{1,0:T(8,128)(2,1)S(1)}, bf16[208,1024]{1,0:T(8,128)(2,1)S(1)}, u32[]{:S(2)}, u32[]{:S(2)}) collective-permute-start(bf16[208,1024]{1,0:T(8,128)(2,1)S(1)} %get-tuple-element.57), channel_id=1, source_target_pairs={{0,96},{1,25},{2,98},{3,27},{4,100},{5,29},{6,102},{7,31},{8,104},... | collective-permute-start | bytes 1277960 | tf_op jit(solution)/shard_map/ppermute | solution.py:51
  57.0 9.2 %collective-permute-start.26 = (bf16[208,1024]{1,0:T(8,128)(2,1)S(1)}, bf16[208,1024]{1,0:T(8,128)(2,1)S(1)}, u32[]{:S(2)}, u32[]{:S(2)}) collective-permute-start(bf16[208,1024]{1,0:T(8,128)(2,1)S(1)} %get-tuple-element.55), channel_id=1, source_target_pairs={{0,32},{1,9},{2,34},{3,11},{4,36},{5,13},{6,38},{7,15},{8,40},{9,1... | collective-permute-start | bytes 1277960 | tf_op jit(solution)/shard_map/ppermute | solution.py:51
  59.5 10.9 %collective-permute-start.25 = (bf16[192,1024]{1,0:T(8,128)(2,1)S(1)}, bf16[192,1024]{1,0:T(8,128)(2,1)S(1)}, u32[]{:S(2)}, u32[]{:S(2)}) collective-permute-start(bf16[192,1024]{1,0:T(8,128)(2,1)S(1)} %get-tuple-element.53), channel_id=1, source_target_pairs={{0,96},{1,25},{2,98},{3,27},{4,100},{5,29},{6,102},{7,31},{8,104},... | collective-permute-start | bytes 1179656 | tf_op jit(solution)/shard_map/ppermute | solution.py:51
  61.2 11.7 %collective-permute-start.24 = (bf16[192,1024]{1,0:T(8,128)(2,1)S(1)}, bf16[192,1024]{1,0:T(8,128)(2,1)S(1)}, u32[]{:S(2)}, u32[]{:S(2)}) collective-permute-start(bf16[192,1024]{1,0:T(8,128)(2,1)S(1)} %get-tuple-element.52.refs_0_), channel_id=1, source_target_pairs={{0,64},{1,17},{2,66},{3,19},{4,68},{5,21},{6,70},{7,23},{8,72},{9,... | collective-permute-start | bytes 1179656 | tf_op jit(solution)/shard_map/ppermute | solution.py:51
  63.6 10.6 %collective-permute-start.23 = (bf16[192,1024]{1,0:T(8,128)(2,1)S(1)}, bf16[192,1024]{1,0:T(8,128)(2,1)S(1)}, u32[]{:S(2)}, u32[]{:S(2)}) collective-permute-start(bf16[192,1024]{1,0:T(8,128)(2,1)S(1)} %get-tuple-element.51), channel_id=1, source_target_pairs={{0,32},{1,9},{2,34},{3,11},{4,36},{5,13},{6,38},{7,15},{8,40},{9,1... | collective-permute-start | bytes 1179656 | tf_op jit(solution)/shard_map/ppermute | solution.py:51
  66.6 10.6 %collective-permute-start.32 = (bf16[96,1024]{1,0:T(8,128)(2,1)S(1)}, bf16[96,1024]{1,0:T(8,128)(2,1)S(1)}, u32[]{:S(2)}, u32[]{:S(2)}) collective-permute-start(bf16[96,1024]{1,0:T(8,128)(2,1)S(1)} %get-tuple-element.63), channel_id=1, source_target_pairs={{0,2},{1,7},{2,0},{3,5},{4,6},{5,3},{6,4},{7,1},{8,10},{9,15},{10,... | collective-permute-start | bytes 589832 | tf_op jit(solution)/shard_map/ppermute | solution.py:51
  69.2 8.0 %collective-permute-start.33 = (bf16[96,1024]{1,0:T(8,128)(2,1)S(1)}, bf16[96,1024]{1,0:T(8,128)(2,1)S(1)}, u32[]{:S(2)}, u32[]{:S(2)}) collective-permute-start(bf16[96,1024]{1,0:T(8,128)(2,1)S(1)} %get-tuple-element.64), channel_id=1, source_target_pairs={{0,3},{1,6},{2,1},{3,4},{4,7},{5,2},{6,5},{7,0},{8,11},{9,14},{10,... | collective-permute-start | bytes 589832 | tf_op jit(solution)/shard_map/ppermute | solution.py:51
  70.4 4.4 %collective-permute-start.29 = (f32[8,128]{1,0:T(8,128)S(1)}, f32[8,128]{1,0:T(8,128)S(1)}, u32[]{:S(2)}, u32[]{:S(2)}) collective-permute-start(f32[8,128]{1,0:T(8,128)S(1)} %get-tuple-element.59.total), channel_id=1, source_target_pairs={{0,2},{1,7},{2,0},{3,5},{4,6},{5,3},{6,4},{7,1},{8,10},{9,15},{10,... | collective-permute-start | bytes 12296 | tf_op jit(solution)/shard_map/ppermute | solution.py:51
  75.2 2.0 %collective-permute-start.30 = (bf16[64,1024]{1,0:T(8,128)(2,1)S(1)}, bf16[64,1024]{1,0:T(8,128)(2,1)S(1)}, u32[]{:S(2)}, u32[]{:S(2)}) collective-permute-start(bf16[64,1024]{1,0:T(8,128)(2,1)S(1)} %get-tuple-element.61), channel_id=1, source_target_pairs={{0,1},{1,0},{2,3},{3,2},{4,5},{5,4},{6,7},{7,6},{8,9},{9,8},{10,11... | collective-permute-start | bytes 393224 | tf_op jit(solution)/shard_map/ppermute | solution.py:51
  (3 other events, 3.5 us)

commit v3 on v2

--- a/solution.py
+++ b/solution.py
@@ -38,8 +38,8 @@
 
 
 AHEAD = [pairs_of(on_ring(lambda r, d=d: (r + d) % 4)) for d in range(4)]
-PAIR_A = pairs_of(on_ring(lambda r: r ^ 1))
-PAIR_B = pairs_of(on_ring(lambda r: r ^ 3))
+ahead_one = on_ring(lambda r: (r + 1) % 4)
+AHEAD_CROSS = pairs_of(lambda x, z, yh, yl, c: (*ahead_one(x, z, yh, yl, c)[:4], 1 - c))
 flip_y = lambda x, z, yh, yl, c: (x, z, yh, 1 - yl, c) if c == 0 else (x, z, 1 - yh, 1 - yl, c)
 FLIP_Y = pairs_of(flip_y)
 CROSS_Y = pairs_of(lambda x, z, yh, yl, c: (*flip_y(x, z, yh, yl, c)[:4], 1 - c))
@@ -80,8 +80,8 @@
 
 
 def score_tiles(factor, rows, cols, s_ref, row_ref, col_max, col_sum):
-    for r in range(2):
-        part = slice(r * TILE, (r + 1) * TILE)
+    for r in range(3):
+        part = slice(r * 256, (r + 1) * 256)
         s = factor * lax.dot_general(rows(part), cols(slice(None)), (((1,), (1,)), ((), ())), preferred_element_type=F32)
         s_ref[part, :] = s
         top = lanes_of(s, jnp.maximum)
@@ -236,25 +236,28 @@
 def product(core, half, left, left_t, first, second, outs):
     at = slice(half * TILE, (half + 1) * TILE)
 
-    def write(out):
-        for k in range(2):
-            value = out[k * CHIP : (k + 1) * CHIP, :]
-            outs[k][0:CHIP, :] = value if (half, k) == (0, 0) else value.astype(BF16)
+    def write(out, me):
+        outs[0][0:CHIP, :] = out[:CHIP] if half == 0 else out[:CHIP].astype(BF16)
+        if len(outs) == 3:
+            outs[1 + me][...] = out[CHIP : CHIP + PIECE].astype(BF16)
+            outs[2 - me][...] = out[CHIP + PIECE :].astype(BF16)
+        else:
+            outs[1][0:CHIP, :] = out[CHIP:].astype(BF16)
 
     @pl.when(core[0] == 0)
     def _():
         out = jnp.dot(left[0][at, :], first[0], preferred_element_type=F32)
-        write(out + jnp.dot(left[1][at, :], second[0], preferred_element_type=F32))
+        write(out + jnp.dot(left[1][at, :], second[0], preferred_element_type=F32), 0)
 
     @pl.when(core[0] == 1)
     def _():
         over = (((0,), (0,)), ((), ()))
         out = lax.dot_general(left_t[0][:, at], first[0], over, preferred_element_type=F32)
-        write(out + lax.dot_general(left_t[1][:, at], second[0], over, preferred_element_type=F32))
+        write(out + lax.dot_general(left_t[1][:, at], second[0], over, preferred_element_type=F32), 1)
 
 
 def grads_other(half, core, g1, g2, r2, x_ref, y_ref, mine_ref, peer_ref, *outs):
-    product(core, half, (g2, r2), (g1, g2), x_ref, y_ref, outs)
+    product(core, half, (g2, r2), (g1, g2), x_ref, y_ref, outs[0:2])
     peer = peer_ref[...]
     term = jnp.sum(jnp.sum(peer[0:2], axis=0, keepdims=True), axis=1, keepdims=True)
     term = term - jnp.where(core[0] == 0, 0.0, 2.0 * peer[4:5, 0:1])
@@ -277,34 +280,35 @@
         total = total + gathered(r[CHIP:, :])
     low, high = out[:PIECE].astype(BF16), out[PIECE:].astype(BF16)
     image = core[0] == 0
-    same_ref[...] = jnp.where(image, low, high)
-    cross_ref[...] = jnp.where(image, high, low)
+    same_ref[0:PIECE, :] = jnp.where(image, low, high)
+    cross_ref[0:PIECE, :] = jnp.where(image, high, low)
+    rows = spread(total)
+    same_ref[PIECE:, :] = rows
+    cross_ref[PIECE:, :] = rows
     total_ref[...] = jnp.broadcast_to(total, (8, 128))
 
 
-def sum_own(core, acc, r1, r2, r3, total, pair_total, keep_ref, give_a_ref, give_b_ref, total_ref):
+def sum_own(core, acc, r2, r3, total, keep_ref, give_a_ref, give_b_ref):
     out = acc[...]
-    for r in (r1, r2, r3):
+    for r in (r2, r3):
         out = out + r[...].astype(F32)
     low, high = out[:PIECE], out[PIECE:]
     image = core[0] == 0
     keep_ref[...] = jnp.where(image, low, high)
     give = jnp.where(image, high, low).astype(BF16)
-    whole = total[...] + pair_total[...]
     give_a_ref[0 : PIECE // 2, :] = give[: PIECE // 2]
-    give_a_ref[PIECE // 2 :, :] = spread(whole[0:1, 0:1])
+    give_a_ref[PIECE // 2 :, :] = spread(total[0:1, 0:1])
     give_b_ref[...] = give[PIECE // 2 :]
-    total_ref[...] = whole
-
-
-def finish(core, scale, keep, got_a, got_b, same, cross, total, image_ref, text_ref, loss_ref):
-    mine = (scale[0] * (keep[...] + same[...].astype(F32))).astype(BF16)
+
+
+def finish(core, scale, keep, got_a, got_b, same, cross, near_same, near_cross, total, image_ref, text_ref, loss_ref):
+    mine = (scale[0] * (keep[...] + same[0:PIECE, :].astype(F32) + near_same[...].astype(F32))).astype(BF16)
     got = jnp.concatenate([got_a[: PIECE // 2, :], got_b[...]], axis=0)
-    other = (scale[0] * (got.astype(F32) + cross[...].astype(F32))).astype(BF16)
+    other = (scale[0] * (got.astype(F32) + cross[0:PIECE, :].astype(F32) + near_cross[...].astype(F32))).astype(BF16)
     image = core[0] == 0
     image_ref[...] = jnp.where(image, mine, other)
     text_ref[...] = jnp.where(image, other, mine)
-    loss = total[0:1, 0:1] + gathered(got_a[PIECE // 2 :, :])
+    loss = total[0:1, 0:1] + gathered(got_a[PIECE // 2 :, :]) + gathered(same[PIECE:, :]) + gathered(cross[PIECE:, :])
     loss_ref[0] = loss[0, 0] / (16.0 * 2 * KIND)
 
 
@@ -372,18 +376,19 @@
     acc2, send_1, term = grads(functools.partial(grads_other, 0), (own, long, small), g1, g2, r2, x, y, side, peer)
     got2 = [move(v, AHEAD[k + 1]) for k, v in enumerate((send_1, send_2, send_3))]
     send_2, send_3 = grads(functools.partial(grads_own, 1), (chip, chip), g1, r1, r2, x, y)
-    acc1, send_1 = grads(functools.partial(grads_own, 0), (own, chip), g1, r1, r2, x, y)
-    got1 = [move(v, AHEAD[k + 1]) for k, v in enumerate((send_1, send_2, send_3))]
-    piece, part = mat(PIECE, WIDTH), mat(PIECE // 2, WIDTH)
-    same, cross, total = call(sum_other, (piece, piece, small), [SMEM] + [VMEM] * 7)(core, acc2, *got2, term, send_2, acc1)
-    pair_total = move(total, FLIP_Y)
+    half_chip = mat(PIECE, WIDTH)
+    acc1, near_same, near_cross = grads(functools.partial(grads_own, 0), (own, half_chip, half_chip), g1, r1, r2, x, y)
+    near_same, near_cross = move(near_same, AHEAD[1]), move(near_cross, AHEAD_CROSS)
+    got1 = [move(send_2, AHEAD[2]), move(send_3, AHEAD[3])]
+    piece, part, tail = mat(PIECE, WIDTH), mat(PIECE // 2, WIDTH), mat(PIECE + EXTRA, WIDTH)
+    same, cross, total = grads(sum_other, (tail, tail, small), acc2, *got2, term, send_2, acc1)
     same, cross = move(same, FLIP_Y), move(cross, CROSS_Y)
-    keep, give_a, give_b, total = call(
-        sum_own, (shape(PIECE, WIDTH), mat(PIECE // 2 + EXTRA, WIDTH), part, small), [SMEM] + [VMEM] * 6
-    )(core, acc1, *got1, total, pair_total)
+    keep, give_a, give_b = grads(
+        sum_own, (shape(PIECE, WIDTH), mat(PIECE // 2 + EXTRA, WIDTH), part), acc1, *got1, total
+    )
     grad_image, grad_text, loss = call(
-        finish, (piece, piece, shape(1)), [SMEM] * 2 + [VMEM] * 6, out_specs=(VMEM, VMEM, SMEM)
-    )(core, logit_scale, keep, move(give_a, FLIP_C), move(give_b, FLIP_C), same, cross, total)
+        finish, (piece, piece, shape(1)), [SMEM] * 2 + [VMEM] * 8, out_specs=(VMEM, VMEM, SMEM)
+    )(core, logit_scale, keep, move(give_a, FLIP_C), move(give_b, FLIP_C), same, cross, near_same, near_cross, total)
     return loss, grad_image, grad_text
 
 

time: 78.5 us -> 77.8 us (level)
    pallas_call x4 -> x6, Pallas kernels: 5.94 us -> 6.67 us  [grads(): call(body, out_shape, [SMEM] + [VMEM] * len(operands), flops=half)]
    pallas_call x3 -> x1, Pallas kernels: 1.71 us -> 1.01 us  [on_device(): call(finish, (piece, piece, shape(1)), [SMEM] * 2 + [VMEM] * 8, out_specs...]
where the time goes in v3:
time: 77.8 us; the launch traced here: 77.6 us
  starting transfers between devices  41.5 us (53%)
  waiting for transfers between devices  18.5 us (24%)
  Pallas kernels  13.9 us (18%)
  local copies, waits for them, and re-layouts  2.09 us (3%)
  between operations  1.63 us (2%)
    ppermute x34, starting transfers between devices, move(): return lax.ppermute(value, AXES, pairs)  41.5 us
    ppermute x34, waiting for transfers between devices, move(): return lax.ppermute(value, AXES, pairs)  18.5 us
    pallas_call x6, Pallas kernels, grads(): call(body, out_shape, [SMEM] + [VMEM] * len(operands), flops=half)  6.67 us
    pallas_call x1, Pallas kernels, on_device(): call(scores_second, (shape(KIND, KIND), mat(2, KIND, WIDTH), shape(8, KIN...  2.26 us
    pallas_call x1, Pallas kernels, on_device(): call(scores_first, (shape(KIND, KIND), mat(2, KIND, WIDTH), shape(8, KIND...  2.25 us
  transfers between devices with their start and end apart: 34, of which 16 were waited for; matrix products, arithmetic and copies ran while one was open for 2% of the time, Pallas kernels for 12%

profile of v3, /device:TPU:1, one launch (start us, length us, event | category | flops | bytes accessed | tf_op | source)
XLA Modules:
  0.0 77.6 jit_solution(8679440077627325624)
XLA Ops:
  0.6 1.5 %collective-permute-start = (bf16[96,1024]{1,0:T(8,128)(2,1)}, bf16[96,1024]{1,0:T(8,128)(2,1)S(1)}, u32[]{:S(2)}, u32[]{:S(2)}) collective-permute-start(bf16[96,1024]{1,0:T(8,128)(2,1)} %text.1), channel_id=1, source_target_pairs={{0,1},{1,0},{2,3},{3,2},{4,5},{5,4},{6,7},{7,6},{8,9},{9,8},{10,11... | collective-permute-start | bytes 589832 | tf_op jit(solution)/shard_map/ppermute | solution.py:51
  2.1 1.2 %constant_dynamic-slice_fusion = (bf16[192,1024]{1,0:T(8,128)(2,1)S(1)}, bf16[192,1024]{1,0:T(8,128)(2,1)S(1)}) fusion(bf16[384,1024]{1,0:T(8,128)(2,1)} %param.3, s32[]{:T(128)S(6)} %select_n.20, s32[]{:T(128)S(6)} %select_n.19), kind=kLoop, calls=%fused_computation.1 | loop fusion | bytes 1572872 | tf_op jit(solution)/shard_map/dynamic_slice | solution.py:326
  3.4 0.9 %copy-done = bf16[96,1024]{1,0:T(8,128)(2,1)S(1)} copy-done((bf16[96,1024]{1,0:T(8,128)(2,1)S(1)}, bf16[96,1024]{1,0:T(8,128)(2,1)}, u32[]{:S(2)}) %copy-start) | copy-done | bytes 196632
  4.4 3.8 %collective-permute-start.2 = (bf16[192,1024]{1,0:T(8,128)(2,1)S(1)}, bf16[192,1024]{1,0:T(8,128)(2,1)S(1)}, u32[]{:S(2)}, u32[]{:S(2)}) collective-permute-start(bf16[192,1024]{1,0:T(8,128)(2,1)S(1)} %get-tuple-element.37.refs_0_), channel_id=1, source_target_pairs={{0,64},{1,17},{2,66},{3,19},{4,68},{5,21},{6,70},{7,23},{8,72},{9,... | collective-permute-start | bytes 1179656 | tf_op jit(solution)/shard_map/ppermute | solution.py:51
  8.2 4.6 %collective-permute-start.5 = (bf16[192,1024]{1,0:T(8,128)(2,1)S(1)}, bf16[192,1024]{1,0:T(8,128)(2,1)S(1)}, u32[]{:S(2)}, u32[]{:S(2)}) collective-permute-start(bf16[192,1024]{1,0:T(8,128)(2,1)S(1)} %get-tuple-element.37.refs_0_), channel_id=1, source_target_pairs={{1,7},{3,5},{5,3},{7,1},{9,15},{11,13},{13,11},{15,9},{17,23},{19,... | collective-permute-start | bytes 1179656 | tf_op jit(solution)/shard_map/ppermute | solution.py:51
  13.6 1.9 %collective-permute-start.1 = (bf16[192,1024]{1,0:T(8,128)(2,1)S(1)}, bf16[192,1024]{1,0:T(8,128)(2,1)S(1)}, u32[]{:S(2)}, u32[]{:S(2)}) collective-permute-start(bf16[192,1024]{1,0:T(8,128)(2,1)S(1)} %get-tuple-element.37.refs_0_), channel_id=1, source_target_pairs={{0,96},{1,25},{2,98},{3,27},{4,100},{5,29},{6,102},{7,31},{8,104},... | collective-permute-start | bytes 1179656 | tf_op jit(solution)/shard_map/ppermute | solution.py:51
  16.4 1.6 %collective-permute-done.5 = bf16[192,1024]{1,0:T(8,128)(2,1)S(1)} collective-permute-done((bf16[192,1024]{1,0:T(8,128)(2,1)S(1)}, bf16[192,1024]{1,0:T(8,128)(2,1)S(1)}, u32[]{:S(2)}, u32[]{:S(2)}) %collective-permute-start.5) | collective-permute-done | bytes 393248 | tf_op jit(solution)/shard_map/ppermute | solution.py:51
  18.0 1.1 %collective-permute-start.7 = (bf16[192,1024]{1,0:T(8,128)(2,1)S(1)}, bf16[192,1024]{1,0:T(8,128)(2,1)S(1)}, u32[]{:S(2)}, u32[]{:S(2)}) collective-permute-start(bf16[192,1024]{1,0:T(8,128)(2,1)S(1)} %broadcast_select_fusion.refs_4_), channel_id=1, source_target_pairs={{0,32},{1,9},{2,34},{3,11},{4,36},{5,13},{6,38},{7,15},{8,40},{9,1... | collective-permute-start | bytes 1179656 | tf_op jit(solution)/shard_map/ppermute | solution.py:51
  19.1 1.7 %collective-permute-start.6 = (bf16[192,1024]{1,0:T(8,128)(2,1)S(1)}, bf16[192,1024]{1,0:T(8,128)(2,1)S(1)}, u32[]{:S(2)}, u32[]{:S(2)}) collective-permute-start(bf16[192,1024]{1,0:T(8,128)(2,1)S(1)} %broadcast_select_fusion.refs_4_), channel_id=1, source_target_pairs={{0,96},{1,25},{2,98},{3,27},{4,100},{5,29},{6,102},{7,31},{8,104},... | collective-permute-start | bytes 1179656 | tf_op jit(solution)/shard_map/ppermute | solution.py:51
  21.0 2.7 %collective-permute-done.4.refs_6_.refs_2_ = bf16[192,1024]{1,0:T(8,128)(2,1)S(1)} collective-permute-done((bf16[192,1024]{1,0:T(8,128)(2,1)S(1)}, bf16[192,1024]{1,0:T(8,128)(2,1)S(1)}, u32[]{:S(2)}, u32[]{:S(2)}) %collective-permute-start.4) | collective-permute-done | bytes 393248 | tf_op jit(solution)/shard_map/ppermute | solution.py:51
  24.2 1.7 %collective-permute-done.7.refs_7_.refs_3_ = bf16[192,1024]{1,0:T(8,128)(2,1)S(1)} collective-permute-done((bf16[192,1024]{1,0:T(8,128)(2,1)S(1)}, bf16[192,1024]{1,0:T(8,128)(2,1)S(1)}, u32[]{:S(2)}, u32[]{:S(2)}) %collective-permute-start.7) | collective-permute-done | bytes 393248 | tf_op jit(solution)/shard_map/ppermute | solution.py:51
  27.6 2.2 %shard_map.59 = (f32[768,768]{1,0:T(8,128)S(1)}, bf16[2,768,1024]{2,1,0:T(8,128)(2,1)S(1)}, f32[8,768]{1,0:T(8,128)S(1)}) custom-call(s32[1]{0:T(128)} %bitcast.core, f32[1]{0:T(128)S(6)} %copy.6.scale, bf16[192,1024]{1,0:T(8,128)(2,1)S(1)} %get-tuple-element.37.refs_0_, bf16[192,1024]{1,0:T(8,128)(2,1)S(1)} %collective-permute-done.1.refs_1_, ...), custom_call_target="tpu_custom_call" | custom-call | flops 1207959552 | bytes 2359296 | tf_op jit(solution)/shard_map/pallas_call | solution.py:339
  29.9 2.3 %shard_map.60 = (f32[768,768]{1,0:T(8,128)S(1)}, bf16[2,768,1024]{2,1,0:T(8,128)(2,1)S(1)}, f32[8,768]{1,0:T(8,128)S(1)}) custom-call(s32[1]{0:T(128)} %bitcast.core, f32[1]{0:T(128)S(6)} %copy.6.scale, bf16[2,768,1024]{2,1,0:T(8,128)(2,1)S(1)} %get-tuple-element.45.x_ref.refs_2_, f32[8,768]{1,0:T(8,128)S(1)} %get-tuple-element.46.st1, ...), custom_call_target="tpu_custom_call" | custom-call | flops 1207959552 | bytes 2359296 | tf_op jit(solution)/shard_map/pallas_call | solution.py:346
  32.4 1.0 %collective-permute-done.15.peer_ref = f32[8,768]{1,0:T(8,128)S(1)} collective-permute-done((f32[8,768]{1,0:T(8,128)S(1)}, f32[8,768]{1,0:T(8,128)S(1)}, u32[]{:S(2)}, u32[]{:S(2)}) %collective-permute-start.15) | collective-permute-done | bytes 24608 | tf_op jit(solution)/shard_map/ppermute | solution.py:51
  33.5 2.9 %collective-permute-start.16 = (f32[8,768]{1,0:T(8,128)S(1)}, f32[8,768]{1,0:T(8,128)S(1)}, u32[]{:S(2)}, u32[]{:S(2)}) collective-permute-start(f32[8,768]{1,0:T(8,128)S(1)} %shard_map.61.a_ref), channel_id=1, source_target_pairs={{0,2},{1,7},{2,0},{3,5},{4,6},{5,3},{6,4},{7,1},{8,10},{9,15},{10,... | collective-permute-start | bytes 73736 | tf_op jit(solution)/shard_map/ppermute | solution.py:51
  36.4 1.2 %collective-permute-done.16.b_ref = f32[8,768]{1,0:T(8,128)S(1)} collective-permute-done((f32[8,768]{1,0:T(8,128)S(1)}, f32[8,768]{1,0:T(8,128)S(1)}, u32[]{:S(2)}, u32[]{:S(2)}) %collective-permute-start.16) | collective-permute-done | bytes 24608 | tf_op jit(solution)/shard_map/ppermute | solution.py:51
  38.0 3.3 %collective-permute-start.18 = (f32[8,768]{1,0:T(8,128)S(1)}, f32[8,768]{1,0:T(8,128)S(1)}, u32[]{:S(2)}, u32[]{:S(2)}) collective-permute-start(f32[8,768]{1,0:T(8,128)S(1)} %shard_map.62.a_ref), channel_id=1, source_target_pairs={{0,64},{1,17},{2,66},{3,19},{4,68},{5,21},{6,70},{7,23},{8,72},{9,... | collective-permute-start | bytes 73736 | tf_op jit(solution)/shard_map/ppermute | solution.py:51
  42.8 1.3 %collective-permute-done.17.b1_ref = f32[8,768]{1,0:T(8,128)S(1)} collective-permute-done((f32[8,768]{1,0:T(8,128)S(1)}, f32[8,768]{1,0:T(8,128)S(1)}, u32[]{:S(2)}, u32[]{:S(2)}) %collective-permute-start.17) | collective-permute-done | bytes 24608 | tf_op jit(solution)/shard_map/ppermute | solution.py:51
  44.2 1.8 %collective-permute-start.20 = (f32[8,768]{1,0:T(8,128)S(1)}, f32[8,768]{1,0:T(8,128)S(1)}, u32[]{:S(2)}, u32[]{:S(2)}) collective-permute-start(f32[8,768]{1,0:T(8,128)S(1)} %shard_map.63.mine_ref), channel_id=1, source_target_pairs={{0,1},{1,0},{2,3},{3,2},{4,5},{5,4},{6,7},{7,6},{8,9},{9,8},{10,11... | collective-permute-start | bytes 73736 | tf_op jit(solution)/shard_map/ppermute | solution.py:51
  49.2 1.5 %collective-permute-done.22.r2 = bf16[768,768]{1,0:T(8,128)(2,1)S(1)} collective-permute-done((bf16[768,768]{1,0:T(8,128)(2,1)S(1)}, bf16[768,768]{1,0:T(8,128)(2,1)S(1)}, u32[]{:S(2)}, u32[]{:S(2)}) %collective-permute-start.22) | collective-permute-done | bytes 1179680 | tf_op jit(solution)/shard_map/ppermute | solution.py:51
  50.7 1.6 %shard_map.69 = (bf16[208,1024]{1,0:T(8,128)(2,1)S(1)}, bf16[208,1024]{1,0:T(8,128)(2,1)S(1)}) custom-call(s32[1]{0:T(128)} %bitcast.core, bf16[768,768]{1,0:T(8,128)(2,1)S(1)} %shard_map.64.g1, bf16[768,768]{1,0:T(8,128)(2,1)S(1)} %shard_map.65.g2, bf16[768,768]{1,0:T(8,128)(2,1)S(1)} %collective-permute-done.22.r2, ...), custom_call_target="tpu_custom_call" | custom-call | flops 1207959552 | tf_op jit(solution)/shard_map/pallas_call | solution.py:373
  52.3 2.6 %collective-permute-start.26 = (bf16[208,1024]{1,0:T(8,128)(2,1)S(1)}, bf16[208,1024]{1,0:T(8,128)(2,1)S(1)}, u32[]{:S(2)}, u32[]{:S(2)}) collective-permute-start(bf16[208,1024]{1,0:T(8,128)(2,1)S(1)} %get-tuple-element.55), channel_id=1, source_target_pairs={{0,64},{1,17},{2,66},{3,19},{4,68},{5,21},{6,70},{7,23},{8,72},{9,... | collective-permute-start | bytes 1277960 | tf_op jit(solution)/shard_map/ppermute | solution.py:51
  55.3 1.6 %shard_map.68 = (f32[192,1024]{1,0:T(8,128)S(1)}, bf16[208,1024]{1,0:T(8,128)(2,1)S(1)}, f32[8,128]{1,0:T(8,128)S(1)}) custom-call(s32[1]{0:T(128)} %bitcast.core, bf16[768,768]{1,0:T(8,128)(2,1)S(1)} %shard_map.64.g1, bf16[768,768]{1,0:T(8,128)(2,1)S(1)} %shard_map.65.g2, bf16[768,768]{1,0:T(8,128)(2,1)S(1)} %collective-permute-done.22.r2, ...), custom_call_target="tpu_custom_call" | custom-call | flops 1207959552 | tf_op jit(solution)/shard_map/pallas_call | solution.py:373
  56.9 1.1 %collective-permute-start.25 = (bf16[208,1024]{1,0:T(8,128)(2,1)S(1)}, bf16[208,1024]{1,0:T(8,128)(2,1)S(1)}, u32[]{:S(2)}, u32[]{:S(2)}) collective-permute-start(bf16[208,1024]{1,0:T(8,128)(2,1)S(1)} %get-tuple-element.54), channel_id=1, source_target_pairs={{0,32},{1,9},{2,34},{3,11},{4,36},{5,13},{6,38},{7,15},{8,40},{9,1... | collective-permute-start | bytes 1277960 | tf_op jit(solution)/shard_map/ppermute | solution.py:51
  58.0 1.4 %shard_map.67 = (bf16[192,1024]{1,0:T(8,128)(2,1)S(1)}, bf16[192,1024]{1,0:T(8,128)(2,1)S(1)}) custom-call(s32[1]{0:T(128)} %bitcast.core, bf16[768,768]{1,0:T(8,128)(2,1)S(1)} %shard_map.64.g1, bf16[768,768]{1,0:T(8,128)(2,1)S(1)} %collective-permute-done.21.r1, bf16[768,768]{1,0:T(8,128)(2,1)S(1)} %collective-permute-done.22.r2, ...), custom_call_target="tpu_custom_call" | custom-call | flops 1207959552 | tf_op jit(solution)/shard_map/pallas_call | solution.py:373
  59.4 1.7 %collective-permute-start.24 = (bf16[192,1024]{1,0:T(8,128)(2,1)S(1)}, bf16[192,1024]{1,0:T(8,128)(2,1)S(1)}, u32[]{:S(2)}, u32[]{:S(2)}) collective-permute-start(bf16[192,1024]{1,0:T(8,128)(2,1)S(1)} %get-tuple-element.52), channel_id=1, source_target_pairs={{0,96},{1,25},{2,98},{3,27},{4,100},{5,29},{6,102},{7,31},{8,104},... | collective-permute-start | bytes 1179656 | tf_op jit(solution)/shard_map/ppermute | solution.py:51
  62.0 1.4 %shard_map.66 = (f32[192,1024]{1,0:T(8,128)S(1)}, bf16[96,1024]{1,0:T(8,128)(2,1)S(1)}, bf16[96,1024]{1,0:T(8,128)(2,1)S(1)}) custom-call(s32[1]{0:T(128)} %bitcast.core, bf16[768,768]{1,0:T(8,128)(2,1)S(1)} %shard_map.64.g1, bf16[768,768]{1,0:T(8,128)(2,1)S(1)} %collective-permute-done.21.r1, bf16[768,768]{1,0:T(8,128)(2,1)S(1)} %collective-permute-done.22.r2, ...), custom_call_target="tpu_custom_call" | custom-call | flops 1207959552 | tf_op jit(solution)/shard_map/pallas_call | solution.py:373
  63.6 2.5 %collective-permute-done.27.r3 = bf16[208,1024]{1,0:T(8,128)(2,1)S(1)} collective-permute-done((bf16[208,1024]{1,0:T(8,128)(2,1)S(1)}, bf16[208,1024]{1,0:T(8,128)(2,1)S(1)}, u32[]{:S(2)}, u32[]{:S(2)}) %collective-permute-start.27) | collective-permute-done | bytes 426016 | tf_op jit(solution)/shard_map/ppermute | solution.py:51
  67.2 2.1 %collective-permute-start.30 = (bf16[112,1024]{1,0:T(8,128)(2,1)S(1)}, bf16[112,1024]{1,0:T(8,128)(2,1)S(1)}, u32[]{:S(2)}, u32[]{:S(2)}) collective-permute-start(bf16[112,1024]{1,0:T(8,128)(2,1)S(1)} %get-tuple-element.62), channel_id=1, source_target_pairs={{0,2},{1,7},{2,0},{3,5},{4,6},{5,3},{6,4},{7,1},{8,10},{9,15},{10,... | collective-permute-start | bytes 688136 | tf_op jit(solution)/shard_map/ppermute | solution.py:51
  70.3 3.2 %collective-permute-start.31 = (bf16[112,1024]{1,0:T(8,128)(2,1)S(1)}, bf16[112,1024]{1,0:T(8,128)(2,1)S(1)}, u32[]{:S(2)}, u32[]{:S(2)}) collective-permute-start(bf16[112,1024]{1,0:T(8,128)(2,1)S(1)} %get-tuple-element.63), channel_id=1, source_target_pairs={{0,3},{1,6},{2,1},{3,4},{4,7},{5,2},{6,5},{7,0},{8,11},{9,14},{10,... | collective-permute-start | bytes 688136 | tf_op jit(solution)/shard_map/ppermute | solution.py:51
  75.4 1.1 %collective-permute-done.31.cross = bf16[112,1024]{1,0:T(8,128)(2,1)S(1)} collective-permute-done((bf16[112,1024]{1,0:T(8,128)(2,1)S(1)}, bf16[112,1024]{1,0:T(8,128)(2,1)S(1)}, u32[]{:S(2)}, u32[]{:S(2)}) %collective-permute-start.31) | collective-permute-done | bytes 229408 | tf_op jit(solution)/shard_map/ppermute | solution.py:51
  76.5 1.0 %shard_map.72 = (bf16[96,1024]{1,0:T(8,128)(2,1)}, bf16[96,1024]{1,0:T(8,128)(2,1)}, f32[1]{0:T(128)}) custom-call(s32[1]{0:T(128)} %bitcast.core, f32[1]{0:T(128)S(6)} %copy.6.scale, f32[96,1024]{1,0:T(8,128)S(1)} %get-tuple-element.59.keep, bf16[64,1024]{1,0:T(8,128)(2,1)S(1)} %collective-permute-done.28.got_a, ...), custom_call_target="tpu_custom_call" | custom-call | tf_op jit(solution)/shard_map/pallas_call | solution.py:389
  (55 shorter events, 14.5 us)
Async XLA Ops:
  0.6 2.8 %collective-permute-start = (bf16[96,1024]{1,0:T(8,128)(2,1)}, bf16[96,1024]{1,0:T(8,128)(2,1)S(1)}, u32[]{:S(2)}, u32[]{:S(2)}) collective-permute-start(bf16[96,1024]{1,0:T(8,128)(2,1)} %text.1), channel_id=1, source_target_pairs={{0,1},{1,0},{2,3},{3,2},{4,5},{5,4},{6,7},{7,6},{8,9},{9,8},{10,11... | collective-permute-start | bytes 589832 | tf_op jit(solution)/shard_map/ppermute | solution.py:51
  4.4 11.1 %collective-permute-start.2 = (bf16[192,1024]{1,0:T(8,128)(2,1)S(1)}, bf16[192,1024]{1,0:T(8,128)(2,1)S(1)}, u32[]{:S(2)}, u32[]{:S(2)}) collective-permute-start(bf16[192,1024]{1,0:T(8,128)(2,1)S(1)} %get-tuple-element.37.refs_0_), channel_id=1, source_target_pairs={{0,64},{1,17},{2,66},{3,19},{4,68},{5,21},{6,70},{7,23},{8,72},{9,... | collective-permute-start | bytes 1179656 | tf_op jit(solution)/shard_map/ppermute | solution.py:51
  8.2 9.8 %collective-permute-start.5 = (bf16[192,1024]{1,0:T(8,128)(2,1)S(1)}, bf16[192,1024]{1,0:T(8,128)(2,1)S(1)}, u32[]{:S(2)}, u32[]{:S(2)}) collective-permute-start(bf16[192,1024]{1,0:T(8,128)(2,1)S(1)} %get-tuple-element.37.refs_0_), channel_id=1, source_target_pairs={{1,7},{3,5},{5,3},{7,1},{9,15},{11,13},{13,11},{15,9},{17,23},{19,... | collective-permute-start | bytes 1179656 | tf_op jit(solution)/shard_map/ppermute | solution.py:51
  12.8 8.2 %collective-permute-start.3 = (bf16[192,1024]{1,0:T(8,128)(2,1)S(1)}, bf16[192,1024]{1,0:T(8,128)(2,1)S(1)}, u32[]{:S(2)}, u32[]{:S(2)}) collective-permute-start(bf16[192,1024]{1,0:T(8,128)(2,1)S(1)} %get-tuple-element.37.refs_0_), channel_id=1, source_target_pairs={{0,32},{1,9},{2,34},{3,11},{4,36},{5,13},{6,38},{7,15},{8,40},{9,1... | collective-permute-start | bytes 1179656 | tf_op jit(solution)/shard_map/ppermute | solution.py:51
  13.6 7.4 %collective-permute-start.1 = (bf16[192,1024]{1,0:T(8,128)(2,1)S(1)}, bf16[192,1024]{1,0:T(8,128)(2,1)S(1)}, u32[]{:S(2)}, u32[]{:S(2)}) collective-permute-start(bf16[192,1024]{1,0:T(8,128)(2,1)S(1)} %get-tuple-element.37.refs_0_), channel_id=1, source_target_pairs={{0,96},{1,25},{2,98},{3,27},{4,100},{5,29},{6,102},{7,31},{8,104},... | collective-permute-start | bytes 1179656 | tf_op jit(solution)/shard_map/ppermute | solution.py:51
  15.5 8.1 %collective-permute-start.4 = (bf16[192,1024]{1,0:T(8,128)(2,1)S(1)}, bf16[192,1024]{1,0:T(8,128)(2,1)S(1)}, u32[]{:S(2)}, u32[]{:S(2)}) collective-permute-start(bf16[192,1024]{1,0:T(8,128)(2,1)S(1)} %collective-permute-done.2.refs_2_), channel_id=1, source_target_pairs={{0,2},{1,7},{2,0},{3,5},{4,6},{5,3},{6,4},{7,1},{8,10},{9,15},{10,... | collective-permute-start | bytes 1179656 | tf_op jit(solution)/shard_map/ppermute | solution.py:51
  18.0 7.9 %collective-permute-start.7 = (bf16[192,1024]{1,0:T(8,128)(2,1)S(1)}, bf16[192,1024]{1,0:T(8,128)(2,1)S(1)}, u32[]{:S(2)}, u32[]{:S(2)}) collective-permute-start(bf16[192,1024]{1,0:T(8,128)(2,1)S(1)} %broadcast_select_fusion.refs_4_), channel_id=1, source_target_pairs={{0,32},{1,9},{2,34},{3,11},{4,36},{5,13},{6,38},{7,15},{8,40},{9,1... | collective-permute-start | bytes 1179656 | tf_op jit(solution)/shard_map/ppermute | solution.py:51
  19.1 6.8 %collective-permute-start.6 = (bf16[192,1024]{1,0:T(8,128)(2,1)S(1)}, bf16[192,1024]{1,0:T(8,128)(2,1)S(1)}, u32[]{:S(2)}, u32[]{:S(2)}) collective-permute-start(bf16[192,1024]{1,0:T(8,128)(2,1)S(1)} %broadcast_select_fusion.refs_4_), channel_id=1, source_target_pairs={{0,96},{1,25},{2,98},{3,27},{4,100},{5,29},{6,102},{7,31},{8,104},... | collective-permute-start | bytes 1179656 | tf_op jit(solution)/shard_map/ppermute | solution.py:51
  23.7 2.8 %collective-permute-start.8 = (bf16[192,1024]{1,0:T(8,128)(2,1)S(1)}, bf16[192,1024]{1,0:T(8,128)(2,1)S(1)}, u32[]{:S(2)}, u32[]{:S(2)}) collective-permute-start(bf16[192,1024]{1,0:T(8,128)(2,1)S(1)} %collective-permute-done.1.refs_1_), channel_id=1, source_target_pairs={{0,1},{1,0},{2,3},{3,2},{4,5},{5,4},{6,7},{7,6},{8,9},{9,8},{10,11... | collective-permute-start | bytes 1179656 | tf_op jit(solution)/shard_map/ppermute | solution.py:51
  23.7 2.8 %collective-permute-start.9 = (bf16[192,1024]{1,0:T(8,128)(2,1)S(1)}, bf16[192,1024]{1,0:T(8,128)(2,1)S(1)}, u32[]{:S(2)}, u32[]{:S(2)}) collective-permute-start(bf16[192,1024]{1,0:T(8,128)(2,1)S(1)} %collective-permute-done.2.refs_2_), channel_id=1, source_target_pairs={{0,1},{1,0},{2,3},{3,2},{4,5},{5,4},{6,7},{7,6},{8,9},{9,8},{10,11... | collective-permute-start | bytes 1179656 | tf_op jit(solution)/shard_map/ppermute | solution.py:51
  24.2 3.4 %collective-permute-start.10 = (bf16[192,1024]{1,0:T(8,128)(2,1)S(1)}, bf16[192,1024]{1,0:T(8,128)(2,1)S(1)}, u32[]{:S(2)}, u32[]{:S(2)}) collective-permute-start(bf16[192,1024]{1,0:T(8,128)(2,1)S(1)} %collective-permute-done.3.refs_3_), channel_id=1, source_target_pairs={{0,1},{1,0},{2,3},{3,2},{4,5},{5,4},{6,7},{7,6},{8,9},{9,8},{10,11... | collective-permute-start | bytes 1179656 | tf_op jit(solution)/shard_map/ppermute | solution.py:51
  25.9 3.9 %collective-permute-start.11 = (bf16[192,1024]{1,0:T(8,128)(2,1)S(1)}, bf16[192,1024]{1,0:T(8,128)(2,1)S(1)}, u32[]{:S(2)}, u32[]{:S(2)}) collective-permute-start(bf16[192,1024]{1,0:T(8,128)(2,1)S(1)} %collective-permute-done.5), channel_id=1, source_target_pairs={{0,1},{1,0},{2,3},{3,2},{4,5},{5,4},{6,7},{7,6},{8,9},{9,8},{10,11... | collective-permute-start | bytes 1179656 | tf_op jit(solution)/shard_map/ppermute | solution.py:51
  25.9 3.9 %collective-permute-start.14 = (bf16[192,1024]{1,0:T(8,128)(2,1)S(1)}, bf16[192,1024]{1,0:T(8,128)(2,1)S(1)}, u32[]{:S(2)}, u32[]{:S(2)}) collective-permute-start(bf16[192,1024]{1,0:T(8,128)(2,1)S(1)} %collective-permute-done.7.refs_7_.refs_3_), channel_id=1, source_target_pairs={{0,1},{1,0},{2,3},{3,2},{4,5},{5,4},{6,7},{7,6},{8,9},{9,8},{10,11... | collective-permute-start | bytes 1179656 | tf_op jit(solution)/shard_map/ppermute | solution.py:51
  26.4 3.4 %collective-permute-start.12 = (bf16[192,1024]{1,0:T(8,128)(2,1)S(1)}, bf16[192,1024]{1,0:T(8,128)(2,1)S(1)}, u32[]{:S(2)}, u32[]{:S(2)}) collective-permute-start(bf16[192,1024]{1,0:T(8,128)(2,1)S(1)} %collective-permute-done.6.refs_5_.refs_1_), channel_id=1, source_target_pairs={{0,1},{1,0},{2,3},{3,2},{4,5},{5,4},{6,7},{7,6},{8,9},{9,8},{10,11... | collective-permute-start | bytes 1179656 | tf_op jit(solution)/shard_map/ppermute | solution.py:51
  26.5 3.4 %collective-permute-start.13 = (bf16[192,1024]{1,0:T(8,128)(2,1)S(1)}, bf16[192,1024]{1,0:T(8,128)(2,1)S(1)}, u32[]{:S(2)}, u32[]{:S(2)}) collective-permute-start(bf16[192,1024]{1,0:T(8,128)(2,1)S(1)} %collective-permute-done.4.refs_6_.refs_2_), channel_id=1, source_target_pairs={{0,1},{1,0},{2,3},{3,2},{4,5},{5,4},{6,7},{7,6},{8,9},{9,8},{10,11... | collective-permute-start | bytes 1179656 | tf_op jit(solution)/shard_map/ppermute | solution.py:51
  33.5 4.1 %collective-permute-start.16 = (f32[8,768]{1,0:T(8,128)S(1)}, f32[8,768]{1,0:T(8,128)S(1)}, u32[]{:S(2)}, u32[]{:S(2)}) collective-permute-start(f32[8,768]{1,0:T(8,128)S(1)} %shard_map.61.a_ref), channel_id=1, source_target_pairs={{0,2},{1,7},{2,0},{3,5},{4,6},{5,3},{6,4},{7,1},{8,10},{9,15},{10,... | collective-permute-start | bytes 73736 | tf_op jit(solution)/shard_map/ppermute | solution.py:51
  37.6 4.5 %collective-permute-start.19 = (f32[8,768]{1,0:T(8,128)S(1)}, f32[8,768]{1,0:T(8,128)S(1)}, u32[]{:S(2)}, u32[]{:S(2)}) collective-permute-start(f32[8,768]{1,0:T(8,128)S(1)} %shard_map.62.a_ref), channel_id=1, source_target_pairs={{0,32},{1,9},{2,34},{3,11},{4,36},{5,13},{6,38},{7,15},{8,40},{9,1... | collective-permute-start | bytes 73736 | tf_op jit(solution)/shard_map/ppermute | solution.py:51
  38.0 4.8 %collective-permute-start.18 = (f32[8,768]{1,0:T(8,128)S(1)}, f32[8,768]{1,0:T(8,128)S(1)}, u32[]{:S(2)}, u32[]{:S(2)}) collective-permute-start(f32[8,768]{1,0:T(8,128)S(1)} %shard_map.62.a_ref), channel_id=1, source_target_pairs={{0,64},{1,17},{2,66},{3,19},{4,68},{5,21},{6,70},{7,23},{8,72},{9,... | collective-permute-start | bytes 73736 | tf_op jit(solution)/shard_map/ppermute | solution.py:51
  41.3 2.7 %collective-permute-start.17 = (f32[8,768]{1,0:T(8,128)S(1)}, f32[8,768]{1,0:T(8,128)S(1)}, u32[]{:S(2)}, u32[]{:S(2)}) collective-permute-start(f32[8,768]{1,0:T(8,128)S(1)} %shard_map.62.a_ref), channel_id=1, source_target_pairs={{0,96},{1,25},{2,98},{3,27},{4,100},{5,29},{6,102},{7,31},{8,104},... | collective-permute-start | bytes 73736 | tf_op jit(solution)/shard_map/ppermute | solution.py:51
  44.2 2.6 %collective-permute-start.20 = (f32[8,768]{1,0:T(8,128)S(1)}, f32[8,768]{1,0:T(8,128)S(1)}, u32[]{:S(2)}, u32[]{:S(2)}) collective-permute-start(f32[8,768]{1,0:T(8,128)S(1)} %shard_map.63.mine_ref), channel_id=1, source_target_pairs={{0,1},{1,0},{2,3},{3,2},{4,5},{5,4},{6,7},{7,6},{8,9},{9,8},{10,11... | collective-permute-start | bytes 73736 | tf_op jit(solution)/shard_map/ppermute | solution.py:51
  47.6 3.1 %collective-permute-start.22 = (bf16[768,768]{1,0:T(8,128)(2,1)S(1)}, bf16[768,768]{1,0:T(8,128)(2,1)S(1)}, u32[]{:S(2)}, u32[]{:S(2)}) collective-permute-start(bf16[768,768]{1,0:T(8,128)(2,1)S(1)} %shard_map.65.g2), channel_id=1, source_target_pairs={{0,1},{1,0},{2,3},{3,2},{4,5},{5,4},{6,7},{7,6},{8,9},{9,8},{10,11... | collective-permute-start | bytes 3538952 | tf_op jit(solution)/shard_map/ppermute | solution.py:51
  48.9 9.1 %collective-permute-start.21 = (bf16[768,768]{1,0:T(8,128)(2,1)S(1)}, bf16[768,768]{1,0:T(8,128)(2,1)S(1)}, u32[]{:S(2)}, u32[]{:S(2)}) collective-permute-start(bf16[768,768]{1,0:T(8,128)(2,1)S(1)} %shard_map.64.g1), channel_id=1, source_target_pairs={{0,1},{1,0},{2,3},{3,2},{4,5},{5,4},{6,7},{7,6},{8,9},{9,8},{10,11... | collective-permute-start | bytes 3538952 | tf_op jit(solution)/shard_map/ppermute | solution.py:51
  52.3 11.2 %collective-permute-start.26 = (bf16[208,1024]{1,0:T(8,128)(2,1)S(1)}, bf16[208,1024]{1,0:T(8,128)(2,1)S(1)}, u32[]{:S(2)}, u32[]{:S(2)}) collective-permute-start(bf16[208,1024]{1,0:T(8,128)(2,1)S(1)} %get-tuple-element.55), channel_id=1, source_target_pairs={{0,64},{1,17},{2,66},{3,19},{4,68},{5,21},{6,70},{7,23},{8,72},{9,... | collective-permute-start | bytes 1277960 | tf_op jit(solution)/shard_map/ppermute | solution.py:51
  54.9 11.2 %collective-permute-start.27 = (bf16[208,1024]{1,0:T(8,128)(2,1)S(1)}, bf16[208,1024]{1,0:T(8,128)(2,1)S(1)}, u32[]{:S(2)}, u32[]{:S(2)}) collective-permute-start(bf16[208,1024]{1,0:T(8,128)(2,1)S(1)} %get-tuple-element.56), channel_id=1, source_target_pairs={{0,96},{1,25},{2,98},{3,27},{4,100},{5,29},{6,102},{7,31},{8,104},... | collective-permute-start | bytes 1277960 | tf_op jit(solution)/shard_map/ppermute | solution.py:51
  56.9 9.9 %collective-permute-start.25 = (bf16[208,1024]{1,0:T(8,128)(2,1)S(1)}, bf16[208,1024]{1,0:T(8,128)(2,1)S(1)}, u32[]{:S(2)}, u32[]{:S(2)}) collective-permute-start(bf16[208,1024]{1,0:T(8,128)(2,1)S(1)} %get-tuple-element.54), channel_id=1, source_target_pairs={{0,32},{1,9},{2,34},{3,11},{4,36},{5,13},{6,38},{7,15},{8,40},{9,1... | collective-permute-start | bytes 1277960 | tf_op jit(solution)/shard_map/ppermute | solution.py:51
  59.4 10.9 %collective-permute-start.24 = (bf16[192,1024]{1,0:T(8,128)(2,1)S(1)}, bf16[192,1024]{1,0:T(8,128)(2,1)S(1)}, u32[]{:S(2)}, u32[]{:S(2)}) collective-permute-start(bf16[192,1024]{1,0:T(8,128)(2,1)S(1)} %get-tuple-element.52), channel_id=1, source_target_pairs={{0,96},{1,25},{2,98},{3,27},{4,100},{5,29},{6,102},{7,31},{8,104},... | collective-permute-start | bytes 1179656 | tf_op jit(solution)/shard_map/ppermute | solution.py:51
  61.1 12.4 %collective-permute-start.23 = (bf16[192,1024]{1,0:T(8,128)(2,1)S(1)}, bf16[192,1024]{1,0:T(8,128)(2,1)S(1)}, u32[]{:S(2)}, u32[]{:S(2)}) collective-permute-start(bf16[192,1024]{1,0:T(8,128)(2,1)S(1)} %get-tuple-element.51.refs_0_), channel_id=1, source_target_pairs={{0,64},{1,17},{2,66},{3,19},{4,68},{5,21},{6,70},{7,23},{8,72},{9,... | collective-permute-start | bytes 1179656 | tf_op jit(solution)/shard_map/ppermute | solution.py:51
  63.5 10.5 %collective-permute-start.32 = (bf16[96,1024]{1,0:T(8,128)(2,1)S(1)}, bf16[96,1024]{1,0:T(8,128)(2,1)S(1)}, u32[]{:S(2)}, u32[]{:S(2)}) collective-permute-start(bf16[96,1024]{1,0:T(8,128)(2,1)S(1)} %get-tuple-element.64), channel_id=1, source_target_pairs={{0,32},{1,9},{2,34},{3,11},{4,36},{5,13},{6,38},{7,15},{8,40},{9,1... | collective-permute-start | bytes 589832 | tf_op jit(solution)/shard_map/ppermute | solution.py:51
  66.1 8.8 %collective-permute-start.33 = (bf16[96,1024]{1,0:T(8,128)(2,1)S(1)}, bf16[96,1024]{1,0:T(8,128)(2,1)S(1)}, u32[]{:S(2)}, u32[]{:S(2)}) collective-permute-start(bf16[96,1024]{1,0:T(8,128)(2,1)S(1)} %get-tuple-element.65), channel_id=1, source_target_pairs={{0,33},{1,8},{2,35},{3,10},{4,37},{5,12},{6,39},{7,14},{8,41},{9,1... | collective-permute-start | bytes 589832 | tf_op jit(solution)/shard_map/ppermute | solution.py:51
  67.2 8.2 %collective-permute-start.30 = (bf16[112,1024]{1,0:T(8,128)(2,1)S(1)}, bf16[112,1024]{1,0:T(8,128)(2,1)S(1)}, u32[]{:S(2)}, u32[]{:S(2)}) collective-permute-start(bf16[112,1024]{1,0:T(8,128)(2,1)S(1)} %get-tuple-element.62), channel_id=1, source_target_pairs={{0,2},{1,7},{2,0},{3,5},{4,6},{5,3},{6,4},{7,1},{8,10},{9,15},{10,... | collective-permute-start | bytes 688136 | tf_op jit(solution)/shard_map/ppermute | solution.py:51
  70.3 6.2 %collective-permute-start.31 = (bf16[112,1024]{1,0:T(8,128)(2,1)S(1)}, bf16[112,1024]{1,0:T(8,128)(2,1)S(1)}, u32[]{:S(2)}, u32[]{:S(2)}) collective-permute-start(bf16[112,1024]{1,0:T(8,128)(2,1)S(1)} %get-tuple-element.63), channel_id=1, source_target_pairs={{0,3},{1,6},{2,1},{3,4},{4,7},{5,2},{6,5},{7,0},{8,11},{9,14},{10,... | collective-permute-start | bytes 688136 | tf_op jit(solution)/shard_map/ppermute | solution.py:51
  73.8 1.6 %collective-permute-start.28 = (bf16[64,1024]{1,0:T(8,128)(2,1)S(1)}, bf16[64,1024]{1,0:T(8,128)(2,1)S(1)}, u32[]{:S(2)}, u32[]{:S(2)}) collective-permute-start(bf16[64,1024]{1,0:T(8,128)(2,1)S(1)} %get-tuple-element.60), channel_id=1, source_target_pairs={{0,1},{1,0},{2,3},{3,2},{4,5},{5,4},{6,7},{7,6},{8,9},{9,8},{10,11... | collective-permute-start | bytes 393224 | tf_op jit(solution)/shard_map/ppermute | solution.py:51
  (3 other events, 3.7 us)

commit v4 on v3

--- a/solution.py
+++ b/solution.py
@@ -1,4 +1,5 @@
 import functools
+import math
 
 import jax
 import jax.numpy as jnp
@@ -14,6 +15,7 @@
 KIND = 4 * CHIP
 TILE = KIND // 2
 WIDTH = 1024
+LOG2_E = 1.0 / math.log(2.0)
 EXTRA = 16
 VMEM_LIMIT = 16 * 1024 * 1024
 
@@ -86,10 +88,10 @@
         s_ref[part, :] = s
         top = lanes_of(s, jnp.maximum)
         row_ref[0:1, part] = jnp.max(top.T, axis=0, keepdims=True)
-        e = jnp.exp(s - jnp.max(top, axis=1, keepdims=True))
+        e = jnp.exp2(s - jnp.max(top, axis=1, keepdims=True))
         row_ref[1:2, part] = jnp.sum(lanes_of(e, jnp.add).T, axis=0, keepdims=True)
         new_max = jnp.maximum(col_max, jnp.max(s, axis=0, keepdims=True))
-        col_sum = col_sum * jnp.exp(col_max - new_max) + jnp.sum(jnp.exp(s - new_max), axis=0, keepdims=True)
+        col_sum = col_sum * jnp.exp2(col_max - new_max) + jnp.sum(jnp.exp2(s - new_max), axis=0, keepdims=True)
         col_max = new_max
     return col_max, col_sum
 
@@ -126,7 +128,7 @@
 
     st_ref[...] = jnp.ones((8, KIND), F32)
     col_max, col_sum = score_tiles(
-        scale[0],
+        scale[0] * LOG2_E,
         lambda part: x_ref[1 - me, part, :],
         lambda part: x_ref[me, part, :],
         s_ref,
@@ -162,7 +164,7 @@
         y_ref[0, slot * CHIP : (slot + 1) * CHIP, :] = b2[slot - 1][...]
 
     col_max, col_sum = score_tiles(
-        scale[0],
+        scale[0] * LOG2_E,
         lambda part: y_ref[1 - me, part, :],
         lambda part: x_ref[me, part, :],
         s_ref,
@@ -177,7 +179,7 @@
 
 def join(a, b):
     top = jnp.maximum(a[0:2], b[0:2])
-    total = a[2:4] * jnp.exp(a[0:2] - top) + b[2:4] * jnp.exp(b[0:2] - top)
+    total = a[2:4] * jnp.exp2(a[0:2] - top) + b[2:4] * jnp.exp2(b[0:2] - top)
     return jnp.concatenate([top, total, a[4:5] + b[4:5], jnp.ones((3, KIND), F32)], axis=0)
 
 
@@ -201,7 +203,7 @@
     for k, b_ref in enumerate((b1_ref, b2_ref, b3_ref)):
         b, cut = b_ref[...], KIND - (k + 1) * CHIP
         out = join(out, jnp.concatenate([b[:, cut:], b[:, :cut]], axis=1))
-    refs[-1][...] = jnp.concatenate([out[0:2] + jnp.log(out[2:4]), out[2:8]], axis=0)
+    refs[-1][...] = jnp.concatenate([out[0:2] + jnp.log2(out[2:4]), out[2:8]], axis=0)
 
 
 def grad_weights(kind, core, s_ref, mine_ref, peer_ref, g_ref):
@@ -213,7 +215,7 @@
         for j in range(KIND // 128):
             at = slice(j * 128, (j + 1) * 128)
             s = s_ref[r * TILE : (r + 1) * TILE, at]
-            g = 0.5 * (jnp.exp(s - lse) + jnp.exp(s - cols[:, at]))
+            g = 0.5 * (jnp.exp2(s - lse) + jnp.exp2(s - cols[:, at]))
             if kind == 0 and r == 0 and j < 2:
                 g = g - jnp.where(on_diagonal(j) & image, 1.0, 0.0)
             g_ref[r * TILE : (r + 1) * TILE, at] = g.astype(BF16)
@@ -309,7 +311,7 @@
     image_ref[...] = jnp.where(image, mine, other)
     text_ref[...] = jnp.where(image, other, mine)
     loss = total[0:1, 0:1] + gathered(got_a[PIECE // 2 :, :]) + gathered(same[PIECE:, :]) + gathered(cross[PIECE:, :])
-    loss_ref[0] = loss[0, 0] / (16.0 * 2 * KIND)
+    loss_ref[0] = loss[0, 0] * (math.log(2.0) / (16.0 * 2 * KIND))
 
 
 def on_device(image, text, logit_scale):

time: 77.8 us -> 77.6 us (level)
  no operation moved by 1% of the time
where the time goes in v4:
time: 77.6 us; the launch traced here: 77.4 us
  starting transfers between devices  41.5 us (53%)
  waiting for transfers between devices  18.6 us (24%)
  Pallas kernels  13.5 us (17%)
  local copies, waits for them, and re-layouts  2.09 us (3%)
  between operations  1.63 us (2%)
    ppermute x34, starting transfers between devices, move(): return lax.ppermute(value, AXES, pairs)  41.5 us
    ppermute x34, waiting for transfers between devices, move(): return lax.ppermute(value, AXES, pairs)  18.6 us
    pallas_call x6, Pallas kernels, grads(): call(body, out_shape, [SMEM] + [VMEM] * len(operands), flops=half)  6.68 us
    pallas_call x1, Pallas kernels, on_device(): call(scores_first, (shape(KIND, KIND), mat(2, KIND, WIDTH), shape(8, KIND...  2.24 us
    pallas_call x1, Pallas kernels, on_device(): call(scores_second, (shape(KIND, KIND), mat(2, KIND, WIDTH), shape(8, KIN...  2.09 us
  transfers between devices with their start and end apart: 34, of which 16 were waited for; matrix products, arithmetic and copies ran while one was open for 2% of the time, Pallas kernels for 12%

profile of v4, /device:TPU:1, one launch (start us, length us, event | category | flops | bytes accessed | tf_op | source)
XLA Modules:
  0.0 77.4 jit_solution(6530996711692352005)
XLA Ops:
  0.6 1.5 %collective-permute-start = (bf16[96,1024]{1,0:T(8,128)(2,1)}, bf16[96,1024]{1,0:T(8,128)(2,1)S(1)}, u32[]{:S(2)}, u32[]{:S(2)}) collective-permute-start(bf16[96,1024]{1,0:T(8,128)(2,1)} %text.1), channel_id=1, source_target_pairs={{0,1},{1,0},{2,3},{3,2},{4,5},{5,4},{6,7},{7,6},{8,9},{9,8},{10,11... | collective-permute-start | bytes 589832 | tf_op jit(solution)/shard_map/ppermute | solution.py:53
  2.1 1.2 %constant_dynamic-slice_fusion = (bf16[192,1024]{1,0:T(8,128)(2,1)S(1)}, bf16[192,1024]{1,0:T(8,128)(2,1)S(1)}) fusion(bf16[384,1024]{1,0:T(8,128)(2,1)} %param.3, s32[]{:T(128)S(6)} %select_n.20, s32[]{:T(128)S(6)} %select_n.19), kind=kLoop, calls=%fused_computation.1 | loop fusion | bytes 1572872 | tf_op jit(solution)/shard_map/dynamic_slice | solution.py:328
  4.4 3.8 %collective-permute-start.2 = (bf16[192,1024]{1,0:T(8,128)(2,1)S(1)}, bf16[192,1024]{1,0:T(8,128)(2,1)S(1)}, u32[]{:S(2)}, u32[]{:S(2)}) collective-permute-start(bf16[192,1024]{1,0:T(8,128)(2,1)S(1)} %get-tuple-element.37.refs_0_), channel_id=1, source_target_pairs={{0,64},{1,17},{2,66},{3,19},{4,68},{5,21},{6,70},{7,23},{8,72},{9,... | collective-permute-start | bytes 1179656 | tf_op jit(solution)/shard_map/ppermute | solution.py:53
  8.2 4.6 %collective-permute-start.5 = (bf16[192,1024]{1,0:T(8,128)(2,1)S(1)}, bf16[192,1024]{1,0:T(8,128)(2,1)S(1)}, u32[]{:S(2)}, u32[]{:S(2)}) collective-permute-start(bf16[192,1024]{1,0:T(8,128)(2,1)S(1)} %get-tuple-element.37.refs_0_), channel_id=1, source_target_pairs={{1,7},{3,5},{5,3},{7,1},{9,15},{11,13},{13,11},{15,9},{17,23},{19,... | collective-permute-start | bytes 1179656 | tf_op jit(solution)/shard_map/ppermute | solution.py:53
  13.6 1.9 %collective-permute-start.1 = (bf16[192,1024]{1,0:T(8,128)(2,1)S(1)}, bf16[192,1024]{1,0:T(8,128)(2,1)S(1)}, u32[]{:S(2)}, u32[]{:S(2)}) collective-permute-start(bf16[192,1024]{1,0:T(8,128)(2,1)S(1)} %get-tuple-element.37.refs_0_), channel_id=1, source_target_pairs={{0,96},{1,25},{2,98},{3,27},{4,100},{5,29},{6,102},{7,31},{8,104},... | collective-permute-start | bytes 1179656 | tf_op jit(solution)/shard_map/ppermute | solution.py:53
  16.4 1.6 %collective-permute-done.5 = bf16[192,1024]{1,0:T(8,128)(2,1)S(1)} collective-permute-done((bf16[192,1024]{1,0:T(8,128)(2,1)S(1)}, bf16[192,1024]{1,0:T(8,128)(2,1)S(1)}, u32[]{:S(2)}, u32[]{:S(2)}) %collective-permute-start.5) | collective-permute-done | bytes 393248 | tf_op jit(solution)/shard_map/ppermute | solution.py:53
  18.0 1.1 %collective-permute-start.7 = (bf16[192,1024]{1,0:T(8,128)(2,1)S(1)}, bf16[192,1024]{1,0:T(8,128)(2,1)S(1)}, u32[]{:S(2)}, u32[]{:S(2)}) collective-permute-start(bf16[192,1024]{1,0:T(8,128)(2,1)S(1)} %broadcast_select_fusion.refs_4_), channel_id=1, source_target_pairs={{0,32},{1,9},{2,34},{3,11},{4,36},{5,13},{6,38},{7,15},{8,40},{9,1... | collective-permute-start | bytes 1179656 | tf_op jit(solution)/shard_map/ppermute | solution.py:53
  19.1 1.7 %collective-permute-start.6 = (bf16[192,1024]{1,0:T(8,128)(2,1)S(1)}, bf16[192,1024]{1,0:T(8,128)(2,1)S(1)}, u32[]{:S(2)}, u32[]{:S(2)}) collective-permute-start(bf16[192,1024]{1,0:T(8,128)(2,1)S(1)} %broadcast_select_fusion.refs_4_), channel_id=1, source_target_pairs={{0,96},{1,25},{2,98},{3,27},{4,100},{5,29},{6,102},{7,31},{8,104},... | collective-permute-start | bytes 1179656 | tf_op jit(solution)/shard_map/ppermute | solution.py:53
  21.0 2.7 %collective-permute-done.4.refs_6_.refs_2_ = bf16[192,1024]{1,0:T(8,128)(2,1)S(1)} collective-permute-done((bf16[192,1024]{1,0:T(8,128)(2,1)S(1)}, bf16[192,1024]{1,0:T(8,128)(2,1)S(1)}, u32[]{:S(2)}, u32[]{:S(2)}) %collective-permute-start.4) | collective-permute-done | bytes 393248 | tf_op jit(solution)/shard_map/ppermute | solution.py:53
  24.2 1.7 %collective-permute-done.7.refs_7_.refs_3_ = bf16[192,1024]{1,0:T(8,128)(2,1)S(1)} collective-permute-done((bf16[192,1024]{1,0:T(8,128)(2,1)S(1)}, bf16[192,1024]{1,0:T(8,128)(2,1)S(1)}, u32[]{:S(2)}, u32[]{:S(2)}) %collective-permute-start.7) | collective-permute-done | bytes 393248 | tf_op jit(solution)/shard_map/ppermute | solution.py:53
  27.6 2.2 %shard_map.59 = (f32[768,768]{1,0:T(8,128)S(1)}, bf16[2,768,1024]{2,1,0:T(8,128)(2,1)S(1)}, f32[8,768]{1,0:T(8,128)S(1)}) custom-call(s32[1]{0:T(128)} %bitcast.core, f32[1]{0:T(128)S(6)} %copy.6.scale, bf16[192,1024]{1,0:T(8,128)(2,1)S(1)} %get-tuple-element.37.refs_0_, bf16[192,1024]{1,0:T(8,128)(2,1)S(1)} %collective-permute-done.1.refs_1_, ...), custom_call_target="tpu_custom_call" | custom-call | flops 1207959552 | bytes 2359296 | tf_op jit(solution)/shard_map/pallas_call | solution.py:341
  29.9 2.1 %shard_map.60 = (f32[768,768]{1,0:T(8,128)S(1)}, bf16[2,768,1024]{2,1,0:T(8,128)(2,1)S(1)}, f32[8,768]{1,0:T(8,128)S(1)}) custom-call(s32[1]{0:T(128)} %bitcast.core, f32[1]{0:T(128)S(6)} %copy.6.scale, bf16[2,768,1024]{2,1,0:T(8,128)(2,1)S(1)} %get-tuple-element.45.x_ref.refs_2_, f32[8,768]{1,0:T(8,128)S(1)} %get-tuple-element.46.st1, ...), custom_call_target="tpu_custom_call" | custom-call | flops 1207959552 | bytes 2359296 | tf_op jit(solution)/shard_map/pallas_call | solution.py:348
  32.2 1.0 %collective-permute-done.15.peer_ref = f32[8,768]{1,0:T(8,128)S(1)} collective-permute-done((f32[8,768]{1,0:T(8,128)S(1)}, f32[8,768]{1,0:T(8,128)S(1)}, u32[]{:S(2)}, u32[]{:S(2)}) %collective-permute-start.15) | collective-permute-done | bytes 24608 | tf_op jit(solution)/shard_map/ppermute | solution.py:53
  33.3 2.9 %collective-permute-start.16 = (f32[8,768]{1,0:T(8,128)S(1)}, f32[8,768]{1,0:T(8,128)S(1)}, u32[]{:S(2)}, u32[]{:S(2)}) collective-permute-start(f32[8,768]{1,0:T(8,128)S(1)} %shard_map.61.a_ref), channel_id=1, source_target_pairs={{0,2},{1,7},{2,0},{3,5},{4,6},{5,3},{6,4},{7,1},{8,10},{9,15},{10,... | collective-permute-start | bytes 73736 | tf_op jit(solution)/shard_map/ppermute | solution.py:53
  36.2 1.2 %collective-permute-done.16.b_ref = f32[8,768]{1,0:T(8,128)S(1)} collective-permute-done((f32[8,768]{1,0:T(8,128)S(1)}, f32[8,768]{1,0:T(8,128)S(1)}, u32[]{:S(2)}, u32[]{:S(2)}) %collective-permute-start.16) | collective-permute-done | bytes 24608 | tf_op jit(solution)/shard_map/ppermute | solution.py:53
  37.8 3.3 %collective-permute-start.18 = (f32[8,768]{1,0:T(8,128)S(1)}, f32[8,768]{1,0:T(8,128)S(1)}, u32[]{:S(2)}, u32[]{:S(2)}) collective-permute-start(f32[8,768]{1,0:T(8,128)S(1)} %shard_map.62.a_ref), channel_id=1, source_target_pairs={{0,64},{1,17},{2,66},{3,19},{4,68},{5,21},{6,70},{7,23},{8,72},{9,... | collective-permute-start | bytes 73736 | tf_op jit(solution)/shard_map/ppermute | solution.py:53
  42.6 1.3 %collective-permute-done.17.b1_ref = f32[8,768]{1,0:T(8,128)S(1)} collective-permute-done((f32[8,768]{1,0:T(8,128)S(1)}, f32[8,768]{1,0:T(8,128)S(1)}, u32[]{:S(2)}, u32[]{:S(2)}) %collective-permute-start.17) | collective-permute-done | bytes 24608 | tf_op jit(solution)/shard_map/ppermute | solution.py:53
  44.0 1.8 %collective-permute-start.20 = (f32[8,768]{1,0:T(8,128)S(1)}, f32[8,768]{1,0:T(8,128)S(1)}, u32[]{:S(2)}, u32[]{:S(2)}) collective-permute-start(f32[8,768]{1,0:T(8,128)S(1)} %shard_map.63.mine_ref), channel_id=1, source_target_pairs={{0,1},{1,0},{2,3},{3,2},{4,5},{5,4},{6,7},{7,6},{8,9},{9,8},{10,11... | collective-permute-start | bytes 73736 | tf_op jit(solution)/shard_map/ppermute | solution.py:53
  48.8 1.6 %collective-permute-done.22.r2 = bf16[768,768]{1,0:T(8,128)(2,1)S(1)} collective-permute-done((bf16[768,768]{1,0:T(8,128)(2,1)S(1)}, bf16[768,768]{1,0:T(8,128)(2,1)S(1)}, u32[]{:S(2)}, u32[]{:S(2)}) %collective-permute-start.22) | collective-permute-done | bytes 1179680 | tf_op jit(solution)/shard_map/ppermute | solution.py:53
  50.4 1.6 %shard_map.69 = (bf16[208,1024]{1,0:T(8,128)(2,1)S(1)}, bf16[208,1024]{1,0:T(8,128)(2,1)S(1)}) custom-call(s32[1]{0:T(128)} %bitcast.core, bf16[768,768]{1,0:T(8,128)(2,1)S(1)} %shard_map.64.g1, bf16[768,768]{1,0:T(8,128)(2,1)S(1)} %shard_map.65.g2, bf16[768,768]{1,0:T(8,128)(2,1)S(1)} %collective-permute-done.22.r2, ...), custom_call_target="tpu_custom_call" | custom-call | flops 1207959552 | tf_op jit(solution)/shard_map/pallas_call | solution.py:375
  52.0 2.6 %collective-permute-start.26 = (bf16[208,1024]{1,0:T(8,128)(2,1)S(1)}, bf16[208,1024]{1,0:T(8,128)(2,1)S(1)}, u32[]{:S(2)}, u32[]{:S(2)}) collective-permute-start(bf16[208,1024]{1,0:T(8,128)(2,1)S(1)} %get-tuple-element.55), channel_id=1, source_target_pairs={{0,64},{1,17},{2,66},{3,19},{4,68},{5,21},{6,70},{7,23},{8,72},{9,... | collective-permute-start | bytes 1277960 | tf_op jit(solution)/shard_map/ppermute | solution.py:53
  55.0 1.6 %shard_map.68 = (f32[192,1024]{1,0:T(8,128)S(1)}, bf16[208,1024]{1,0:T(8,128)(2,1)S(1)}, f32[8,128]{1,0:T(8,128)S(1)}) custom-call(s32[1]{0:T(128)} %bitcast.core, bf16[768,768]{1,0:T(8,128)(2,1)S(1)} %shard_map.64.g1, bf16[768,768]{1,0:T(8,128)(2,1)S(1)} %shard_map.65.g2, bf16[768,768]{1,0:T(8,128)(2,1)S(1)} %collective-permute-done.22.r2, ...), custom_call_target="tpu_custom_call" | custom-call | flops 1207959552 | tf_op jit(solution)/shard_map/pallas_call | solution.py:375
  56.6 1.1 %collective-permute-start.25 = (bf16[208,1024]{1,0:T(8,128)(2,1)S(1)}, bf16[208,1024]{1,0:T(8,128)(2,1)S(1)}, u32[]{:S(2)}, u32[]{:S(2)}) collective-permute-start(bf16[208,1024]{1,0:T(8,128)(2,1)S(1)} %get-tuple-element.54), channel_id=1, source_target_pairs={{0,32},{1,9},{2,34},{3,11},{4,36},{5,13},{6,38},{7,15},{8,40},{9,1... | collective-permute-start | bytes 1277960 | tf_op jit(solution)/shard_map/ppermute | solution.py:53
  57.7 1.4 %shard_map.67 = (bf16[192,1024]{1,0:T(8,128)(2,1)S(1)}, bf16[192,1024]{1,0:T(8,128)(2,1)S(1)}) custom-call(s32[1]{0:T(128)} %bitcast.core, bf16[768,768]{1,0:T(8,128)(2,1)S(1)} %shard_map.64.g1, bf16[768,768]{1,0:T(8,128)(2,1)S(1)} %collective-permute-done.21.r1, bf16[768,768]{1,0:T(8,128)(2,1)S(1)} %collective-permute-done.22.r2, ...), custom_call_target="tpu_custom_call" | custom-call | flops 1207959552 | tf_op jit(solution)/shard_map/pallas_call | solution.py:375
  59.2 1.7 %collective-permute-start.24 = (bf16[192,1024]{1,0:T(8,128)(2,1)S(1)}, bf16[192,1024]{1,0:T(8,128)(2,1)S(1)}, u32[]{:S(2)}, u32[]{:S(2)}) collective-permute-start(bf16[192,1024]{1,0:T(8,128)(2,1)S(1)} %get-tuple-element.52), channel_id=1, source_target_pairs={{0,96},{1,25},{2,98},{3,27},{4,100},{5,29},{6,102},{7,31},{8,104},... | collective-permute-start | bytes 1179656 | tf_op jit(solution)/shard_map/ppermute | solution.py:53
  61.8 1.4 %shard_map.66 = (f32[192,1024]{1,0:T(8,128)S(1)}, bf16[96,1024]{1,0:T(8,128)(2,1)S(1)}, bf16[96,1024]{1,0:T(8,128)(2,1)S(1)}) custom-call(s32[1]{0:T(128)} %bitcast.core, bf16[768,768]{1,0:T(8,128)(2,1)S(1)} %shard_map.64.g1, bf16[768,768]{1,0:T(8,128)(2,1)S(1)} %collective-permute-done.21.r1, bf16[768,768]{1,0:T(8,128)(2,1)S(1)} %collective-permute-done.22.r2, ...), custom_call_target="tpu_custom_call" | custom-call | flops 1207959552 | tf_op jit(solution)/shard_map/pallas_call | solution.py:375
  63.3 2.5 %collective-permute-done.27.r3 = bf16[208,1024]{1,0:T(8,128)(2,1)S(1)} collective-permute-done((bf16[208,1024]{1,0:T(8,128)(2,1)S(1)}, bf16[208,1024]{1,0:T(8,128)(2,1)S(1)}, u32[]{:S(2)}, u32[]{:S(2)}) %collective-permute-start.27) | collective-permute-done | bytes 426016 | tf_op jit(solution)/shard_map/ppermute | solution.py:53
  67.0 2.1 %collective-permute-start.30 = (bf16[112,1024]{1,0:T(8,128)(2,1)S(1)}, bf16[112,1024]{1,0:T(8,128)(2,1)S(1)}, u32[]{:S(2)}, u32[]{:S(2)}) collective-permute-start(bf16[112,1024]{1,0:T(8,128)(2,1)S(1)} %get-tuple-element.62), channel_id=1, source_target_pairs={{0,2},{1,7},{2,0},{3,5},{4,6},{5,3},{6,4},{7,1},{8,10},{9,15},{10,... | collective-permute-start | bytes 688136 | tf_op jit(solution)/shard_map/ppermute | solution.py:53
  69.1 0.9 %collective-permute-done.24.r3 = bf16[192,1024]{1,0:T(8,128)(2,1)S(1)} collective-permute-done((bf16[192,1024]{1,0:T(8,128)(2,1)S(1)}, bf16[192,1024]{1,0:T(8,128)(2,1)S(1)}, u32[]{:S(2)}, u32[]{:S(2)}) %collective-permute-start.24) | collective-permute-done | bytes 393248 | tf_op jit(solution)/shard_map/ppermute | solution.py:53
  70.0 3.2 %collective-permute-start.31 = (bf16[112,1024]{1,0:T(8,128)(2,1)S(1)}, bf16[112,1024]{1,0:T(8,128)(2,1)S(1)}, u32[]{:S(2)}, u32[]{:S(2)}) collective-permute-start(bf16[112,1024]{1,0:T(8,128)(2,1)S(1)} %get-tuple-element.63), channel_id=1, source_target_pairs={{0,3},{1,6},{2,1},{3,4},{4,7},{5,2},{6,5},{7,0},{8,11},{9,14},{10,... | collective-permute-start | bytes 688136 | tf_op jit(solution)/shard_map/ppermute | solution.py:53
  75.1 1.1 %collective-permute-done.31.cross = bf16[112,1024]{1,0:T(8,128)(2,1)S(1)} collective-permute-done((bf16[112,1024]{1,0:T(8,128)(2,1)S(1)}, bf16[112,1024]{1,0:T(8,128)(2,1)S(1)}, u32[]{:S(2)}, u32[]{:S(2)}) %collective-permute-start.31) | collective-permute-done | bytes 229408 | tf_op jit(solution)/shard_map/ppermute | solution.py:53
  76.2 1.0 %shard_map.72 = (bf16[96,1024]{1,0:T(8,128)(2,1)}, bf16[96,1024]{1,0:T(8,128)(2,1)}, f32[1]{0:T(128)}) custom-call(s32[1]{0:T(128)} %bitcast.core, f32[1]{0:T(128)S(6)} %copy.6.scale, f32[96,1024]{1,0:T(8,128)S(1)} %get-tuple-element.59.keep, bf16[64,1024]{1,0:T(8,128)(2,1)S(1)} %collective-permute-done.28.got_a, ...), custom_call_target="tpu_custom_call" | custom-call | tf_op jit(solution)/shard_map/pallas_call | solution.py:391
  (55 shorter events, 14.3 us)
Async XLA Ops:
  0.6 2.8 %collective-permute-start = (bf16[96,1024]{1,0:T(8,128)(2,1)}, bf16[96,1024]{1,0:T(8,128)(2,1)S(1)}, u32[]{:S(2)}, u32[]{:S(2)}) collective-permute-start(bf16[96,1024]{1,0:T(8,128)(2,1)} %text.1), channel_id=1, source_target_pairs={{0,1},{1,0},{2,3},{3,2},{4,5},{5,4},{6,7},{7,6},{8,9},{9,8},{10,11... | collective-permute-start | bytes 589832 | tf_op jit(solution)/shard_map/ppermute | solution.py:53
  4.4 11.1 %collective-permute-start.2 = (bf16[192,1024]{1,0:T(8,128)(2,1)S(1)}, bf16[192,1024]{1,0:T(8,128)(2,1)S(1)}, u32[]{:S(2)}, u32[]{:S(2)}) collective-permute-start(bf16[192,1024]{1,0:T(8,128)(2,1)S(1)} %get-tuple-element.37.refs_0_), channel_id=1, source_target_pairs={{0,64},{1,17},{2,66},{3,19},{4,68},{5,21},{6,70},{7,23},{8,72},{9,... | collective-permute-start | bytes 1179656 | tf_op jit(solution)/shard_map/ppermute | solution.py:53
  8.2 9.8 %collective-permute-start.5 = (bf16[192,1024]{1,0:T(8,128)(2,1)S(1)}, bf16[192,1024]{1,0:T(8,128)(2,1)S(1)}, u32[]{:S(2)}, u32[]{:S(2)}) collective-permute-start(bf16[192,1024]{1,0:T(8,128)(2,1)S(1)} %get-tuple-element.37.refs_0_), channel_id=1, source_target_pairs={{1,7},{3,5},{5,3},{7,1},{9,15},{11,13},{13,11},{15,9},{17,23},{19,... | collective-permute-start | bytes 1179656 | tf_op jit(solution)/shard_map/ppermute | solution.py:53
  12.8 8.2 %collective-permute-start.3 = (bf16[192,1024]{1,0:T(8,128)(2,1)S(1)}, bf16[192,1024]{1,0:T(8,128)(2,1)S(1)}, u32[]{:S(2)}, u32[]{:S(2)}) collective-permute-start(bf16[192,1024]{1,0:T(8,128)(2,1)S(1)} %get-tuple-element.37.refs_0_), channel_id=1, source_target_pairs={{0,32},{1,9},{2,34},{3,11},{4,36},{5,13},{6,38},{7,15},{8,40},{9,1... | collective-permute-start | bytes 1179656 | tf_op jit(solution)/shard_map/ppermute | solution.py:53
  13.6 7.4 %collective-permute-start.1 = (bf16[192,1024]{1,0:T(8,128)(2,1)S(1)}, bf16[192,1024]{1,0:T(8,128)(2,1)S(1)}, u32[]{:S(2)}, u32[]{:S(2)}) collective-permute-start(bf16[192,1024]{1,0:T(8,128)(2,1)S(1)} %get-tuple-element.37.refs_0_), channel_id=1, source_target_pairs={{0,96},{1,25},{2,98},{3,27},{4,100},{5,29},{6,102},{7,31},{8,104},... | collective-permute-start | bytes 1179656 | tf_op jit(solution)/shard_map/ppermute | solution.py:53
  15.5 8.1 %collective-permute-start.4 = (bf16[192,1024]{1,0:T(8,128)(2,1)S(1)}, bf16[192,1024]{1,0:T(8,128)(2,1)S(1)}, u32[]{:S(2)}, u32[]{:S(2)}) collective-permute-start(bf16[192,1024]{1,0:T(8,128)(2,1)S(1)} %collective-permute-done.2.refs_2_), channel_id=1, source_target_pairs={{0,2},{1,7},{2,0},{3,5},{4,6},{5,3},{6,4},{7,1},{8,10},{9,15},{10,... | collective-permute-start | bytes 1179656 | tf_op jit(solution)/shard_map/ppermute | solution.py:53
  18.0 7.9 %collective-permute-start.7 = (bf16[192,1024]{1,0:T(8,128)(2,1)S(1)}, bf16[192,1024]{1,0:T(8,128)(2,1)S(1)}, u32[]{:S(2)}, u32[]{:S(2)}) collective-permute-start(bf16[192,1024]{1,0:T(8,128)(2,1)S(1)} %broadcast_select_fusion.refs_4_), channel_id=1, source_target_pairs={{0,32},{1,9},{2,34},{3,11},{4,36},{5,13},{6,38},{7,15},{8,40},{9,1... | collective-permute-start | bytes 1179656 | tf_op jit(solution)/shard_map/ppermute | solution.py:53
  19.1 6.8 %collective-permute-start.6 = (bf16[192,1024]{1,0:T(8,128)(2,1)S(1)}, bf16[192,1024]{1,0:T(8,128)(2,1)S(1)}, u32[]{:S(2)}, u32[]{:S(2)}) collective-permute-start(bf16[192,1024]{1,0:T(8,128)(2,1)S(1)} %broadcast_select_fusion.refs_4_), channel_id=1, source_target_pairs={{0,96},{1,25},{2,98},{3,27},{4,100},{5,29},{6,102},{7,31},{8,104},... | collective-permute-start | bytes 1179656 | tf_op jit(solution)/shard_map/ppermute | solution.py:53
  23.7 2.8 %collective-permute-start.8 = (bf16[192,1024]{1,0:T(8,128)(2,1)S(1)}, bf16[192,1024]{1,0:T(8,128)(2,1)S(1)}, u32[]{:S(2)}, u32[]{:S(2)}) collective-permute-start(bf16[192,1024]{1,0:T(8,128)(2,1)S(1)} %collective-permute-done.1.refs_1_), channel_id=1, source_target_pairs={{0,1},{1,0},{2,3},{3,2},{4,5},{5,4},{6,7},{7,6},{8,9},{9,8},{10,11... | collective-permute-start | bytes 1179656 | tf_op jit(solution)/shard_map/ppermute | solution.py:53
  23.7 2.8 %collective-permute-start.9 = (bf16[192,1024]{1,0:T(8,128)(2,1)S(1)}, bf16[192,1024]{1,0:T(8,128)(2,1)S(1)}, u32[]{:S(2)}, u32[]{:S(2)}) collective-permute-start(bf16[192,1024]{1,0:T(8,128)(2,1)S(1)} %collective-permute-done.2.refs_2_), channel_id=1, source_target_pairs={{0,1},{1,0},{2,3},{3,2},{4,5},{5,4},{6,7},{7,6},{8,9},{9,8},{10,11... | collective-permute-start | bytes 1179656 | tf_op jit(solution)/shard_map/ppermute | solution.py:53
  24.2 3.4 %collective-permute-start.10 = (bf16[192,1024]{1,0:T(8,128)(2,1)S(1)}, bf16[192,1024]{1,0:T(8,128)(2,1)S(1)}, u32[]{:S(2)}, u32[]{:S(2)}) collective-permute-start(bf16[192,1024]{1,0:T(8,128)(2,1)S(1)} %collective-permute-done.3.refs_3_), channel_id=1, source_target_pairs={{0,1},{1,0},{2,3},{3,2},{4,5},{5,4},{6,7},{7,6},{8,9},{9,8},{10,11... | collective-permute-start | bytes 1179656 | tf_op jit(solution)/shard_map/ppermute | solution.py:53
  25.9 3.9 %collective-permute-start.11 = (bf16[192,1024]{1,0:T(8,128)(2,1)S(1)}, bf16[192,1024]{1,0:T(8,128)(2,1)S(1)}, u32[]{:S(2)}, u32[]{:S(2)}) collective-permute-start(bf16[192,1024]{1,0:T(8,128)(2,1)S(1)} %collective-permute-done.5), channel_id=1, source_target_pairs={{0,1},{1,0},{2,3},{3,2},{4,5},{5,4},{6,7},{7,6},{8,9},{9,8},{10,11... | collective-permute-start | bytes 1179656 | tf_op jit(solution)/shard_map/ppermute | solution.py:53
  25.9 3.9 %collective-permute-start.14 = (bf16[192,1024]{1,0:T(8,128)(2,1)S(1)}, bf16[192,1024]{1,0:T(8,128)(2,1)S(1)}, u32[]{:S(2)}, u32[]{:S(2)}) collective-permute-start(bf16[192,1024]{1,0:T(8,128)(2,1)S(1)} %collective-permute-done.7.refs_7_.refs_3_), channel_id=1, source_target_pairs={{0,1},{1,0},{2,3},{3,2},{4,5},{5,4},{6,7},{7,6},{8,9},{9,8},{10,11... | collective-permute-start | bytes 1179656 | tf_op jit(solution)/shard_map/ppermute | solution.py:53
  26.4 3.4 %collective-permute-start.12 = (bf16[192,1024]{1,0:T(8,128)(2,1)S(1)}, bf16[192,1024]{1,0:T(8,128)(2,1)S(1)}, u32[]{:S(2)}, u32[]{:S(2)}) collective-permute-start(bf16[192,1024]{1,0:T(8,128)(2,1)S(1)} %collective-permute-done.6.refs_5_.refs_1_), channel_id=1, source_target_pairs={{0,1},{1,0},{2,3},{3,2},{4,5},{5,4},{6,7},{7,6},{8,9},{9,8},{10,11... | collective-permute-start | bytes 1179656 | tf_op jit(solution)/shard_map/ppermute | solution.py:53
  26.5 3.3 %collective-permute-start.13 = (bf16[192,1024]{1,0:T(8,128)(2,1)S(1)}, bf16[192,1024]{1,0:T(8,128)(2,1)S(1)}, u32[]{:S(2)}, u32[]{:S(2)}) collective-permute-start(bf16[192,1024]{1,0:T(8,128)(2,1)S(1)} %collective-permute-done.4.refs_6_.refs_2_), channel_id=1, source_target_pairs={{0,1},{1,0},{2,3},{3,2},{4,5},{5,4},{6,7},{7,6},{8,9},{9,8},{10,11... | collective-permute-start | bytes 1179656 | tf_op jit(solution)/shard_map/ppermute | solution.py:53
  33.3 4.1 %collective-permute-start.16 = (f32[8,768]{1,0:T(8,128)S(1)}, f32[8,768]{1,0:T(8,128)S(1)}, u32[]{:S(2)}, u32[]{:S(2)}) collective-permute-start(f32[8,768]{1,0:T(8,128)S(1)} %shard_map.61.a_ref), channel_id=1, source_target_pairs={{0,2},{1,7},{2,0},{3,5},{4,6},{5,3},{6,4},{7,1},{8,10},{9,15},{10,... | collective-permute-start | bytes 73736 | tf_op jit(solution)/shard_map/ppermute | solution.py:53
  37.4 4.5 %collective-permute-start.19 = (f32[8,768]{1,0:T(8,128)S(1)}, f32[8,768]{1,0:T(8,128)S(1)}, u32[]{:S(2)}, u32[]{:S(2)}) collective-permute-start(f32[8,768]{1,0:T(8,128)S(1)} %shard_map.62.a_ref), channel_id=1, source_target_pairs={{0,32},{1,9},{2,34},{3,11},{4,36},{5,13},{6,38},{7,15},{8,40},{9,1... | collective-permute-start | bytes 73736 | tf_op jit(solution)/shard_map/ppermute | solution.py:53
  37.8 4.8 %collective-permute-start.18 = (f32[8,768]{1,0:T(8,128)S(1)}, f32[8,768]{1,0:T(8,128)S(1)}, u32[]{:S(2)}, u32[]{:S(2)}) collective-permute-start(f32[8,768]{1,0:T(8,128)S(1)} %shard_map.62.a_ref), channel_id=1, source_target_pairs={{0,64},{1,17},{2,66},{3,19},{4,68},{5,21},{6,70},{7,23},{8,72},{9,... | collective-permute-start | bytes 73736 | tf_op jit(solution)/shard_map/ppermute | solution.py:53
  41.1 2.8 %collective-permute-start.17 = (f32[8,768]{1,0:T(8,128)S(1)}, f32[8,768]{1,0:T(8,128)S(1)}, u32[]{:S(2)}, u32[]{:S(2)}) collective-permute-start(f32[8,768]{1,0:T(8,128)S(1)} %shard_map.62.a_ref), channel_id=1, source_target_pairs={{0,96},{1,25},{2,98},{3,27},{4,100},{5,29},{6,102},{7,31},{8,104},... | collective-permute-start | bytes 73736 | tf_op jit(solution)/shard_map/ppermute | solution.py:53
  44.0 2.6 %collective-permute-start.20 = (f32[8,768]{1,0:T(8,128)S(1)}, f32[8,768]{1,0:T(8,128)S(1)}, u32[]{:S(2)}, u32[]{:S(2)}) collective-permute-start(f32[8,768]{1,0:T(8,128)S(1)} %shard_map.63.mine_ref), channel_id=1, source_target_pairs={{0,1},{1,0},{2,3},{3,2},{4,5},{5,4},{6,7},{7,6},{8,9},{9,8},{10,11... | collective-permute-start | bytes 73736 | tf_op jit(solution)/shard_map/ppermute | solution.py:53
  47.3 3.1 %collective-permute-start.22 = (bf16[768,768]{1,0:T(8,128)(2,1)S(1)}, bf16[768,768]{1,0:T(8,128)(2,1)S(1)}, u32[]{:S(2)}, u32[]{:S(2)}) collective-permute-start(bf16[768,768]{1,0:T(8,128)(2,1)S(1)} %shard_map.65.g2), channel_id=1, source_target_pairs={{0,1},{1,0},{2,3},{3,2},{4,5},{5,4},{6,7},{7,6},{8,9},{9,8},{10,11... | collective-permute-start | bytes 3538952 | tf_op jit(solution)/shard_map/ppermute | solution.py:53
  48.6 9.2 %collective-permute-start.21 = (bf16[768,768]{1,0:T(8,128)(2,1)S(1)}, bf16[768,768]{1,0:T(8,128)(2,1)S(1)}, u32[]{:S(2)}, u32[]{:S(2)}) collective-permute-start(bf16[768,768]{1,0:T(8,128)(2,1)S(1)} %shard_map.64.g1), channel_id=1, source_target_pairs={{0,1},{1,0},{2,3},{3,2},{4,5},{5,4},{6,7},{7,6},{8,9},{9,8},{10,11... | collective-permute-start | bytes 3538952 | tf_op jit(solution)/shard_map/ppermute | solution.py:53
  52.0 11.2 %collective-permute-start.26 = (bf16[208,1024]{1,0:T(8,128)(2,1)S(1)}, bf16[208,1024]{1,0:T(8,128)(2,1)S(1)}, u32[]{:S(2)}, u32[]{:S(2)}) collective-permute-start(bf16[208,1024]{1,0:T(8,128)(2,1)S(1)} %get-tuple-element.55), channel_id=1, source_target_pairs={{0,64},{1,17},{2,66},{3,19},{4,68},{5,21},{6,70},{7,23},{8,72},{9,... | collective-permute-start | bytes 1277960 | tf_op jit(solution)/shard_map/ppermute | solution.py:53
  54.6 11.2 %collective-permute-start.27 = (bf16[208,1024]{1,0:T(8,128)(2,1)S(1)}, bf16[208,1024]{1,0:T(8,128)(2,1)S(1)}, u32[]{:S(2)}, u32[]{:S(2)}) collective-permute-start(bf16[208,1024]{1,0:T(8,128)(2,1)S(1)} %get-tuple-element.56), channel_id=1, source_target_pairs={{0,96},{1,25},{2,98},{3,27},{4,100},{5,29},{6,102},{7,31},{8,104},... | collective-permute-start | bytes 1277960 | tf_op jit(solution)/shard_map/ppermute | solution.py:53
  56.6 9.9 %collective-permute-start.25 = (bf16[208,1024]{1,0:T(8,128)(2,1)S(1)}, bf16[208,1024]{1,0:T(8,128)(2,1)S(1)}, u32[]{:S(2)}, u32[]{:S(2)}) collective-permute-start(bf16[208,1024]{1,0:T(8,128)(2,1)S(1)} %get-tuple-element.54), channel_id=1, source_target_pairs={{0,32},{1,9},{2,34},{3,11},{4,36},{5,13},{6,38},{7,15},{8,40},{9,1... | collective-permute-start | bytes 1277960 | tf_op jit(solution)/shard_map/ppermute | solution.py:53
  59.2 10.9 %collective-permute-start.24 = (bf16[192,1024]{1,0:T(8,128)(2,1)S(1)}, bf16[192,1024]{1,0:T(8,128)(2,1)S(1)}, u32[]{:S(2)}, u32[]{:S(2)}) collective-permute-start(bf16[192,1024]{1,0:T(8,128)(2,1)S(1)} %get-tuple-element.52), channel_id=1, source_target_pairs={{0,96},{1,25},{2,98},{3,27},{4,100},{5,29},{6,102},{7,31},{8,104},... | collective-permute-start | bytes 1179656 | tf_op jit(solution)/shard_map/ppermute | solution.py:53
  60.9 12.4 %collective-permute-start.23 = (bf16[192,1024]{1,0:T(8,128)(2,1)S(1)}, bf16[192,1024]{1,0:T(8,128)(2,1)S(1)}, u32[]{:S(2)}, u32[]{:S(2)}) collective-permute-start(bf16[192,1024]{1,0:T(8,128)(2,1)S(1)} %get-tuple-element.51.refs_0_), channel_id=1, source_target_pairs={{0,64},{1,17},{2,66},{3,19},{4,68},{5,21},{6,70},{7,23},{8,72},{9,... | collective-permute-start | bytes 1179656 | tf_op jit(solution)/shard_map/ppermute | solution.py:53
  63.2 10.5 %collective-permute-start.32 = (bf16[96,1024]{1,0:T(8,128)(2,1)S(1)}, bf16[96,1024]{1,0:T(8,128)(2,1)S(1)}, u32[]{:S(2)}, u32[]{:S(2)}) collective-permute-start(bf16[96,1024]{1,0:T(8,128)(2,1)S(1)} %get-tuple-element.64), channel_id=1, source_target_pairs={{0,32},{1,9},{2,34},{3,11},{4,36},{5,13},{6,38},{7,15},{8,40},{9,1... | collective-permute-start | bytes 589832 | tf_op jit(solution)/shard_map/ppermute | solution.py:53
  65.8 8.8 %collective-permute-start.33 = (bf16[96,1024]{1,0:T(8,128)(2,1)S(1)}, bf16[96,1024]{1,0:T(8,128)(2,1)S(1)}, u32[]{:S(2)}, u32[]{:S(2)}) collective-permute-start(bf16[96,1024]{1,0:T(8,128)(2,1)S(1)} %get-tuple-element.65), channel_id=1, source_target_pairs={{0,33},{1,8},{2,35},{3,10},{4,37},{5,12},{6,39},{7,14},{8,41},{9,1... | collective-permute-start | bytes 589832 | tf_op jit(solution)/shard_map/ppermute | solution.py:53
  67.0 8.2 %collective-permute-start.30 = (bf16[112,1024]{1,0:T(8,128)(2,1)S(1)}, bf16[112,1024]{1,0:T(8,128)(2,1)S(1)}, u32[]{:S(2)}, u32[]{:S(2)}) collective-permute-start(bf16[112,1024]{1,0:T(8,128)(2,1)S(1)} %get-tuple-element.62), channel_id=1, source_target_pairs={{0,2},{1,7},{2,0},{3,5},{4,6},{5,3},{6,4},{7,1},{8,10},{9,15},{10,... | collective-permute-start | bytes 688136 | tf_op jit(solution)/shard_map/ppermute | solution.py:53
  70.0 6.2 %collective-permute-start.31 = (bf16[112,1024]{1,0:T(8,128)(2,1)S(1)}, bf16[112,1024]{1,0:T(8,128)(2,1)S(1)}, u32[]{:S(2)}, u32[]{:S(2)}) collective-permute-start(bf16[112,1024]{1,0:T(8,128)(2,1)S(1)} %get-tuple-element.63), channel_id=1, source_target_pairs={{0,3},{1,6},{2,1},{3,4},{4,7},{5,2},{6,5},{7,0},{8,11},{9,14},{10,... | collective-permute-start | bytes 688136 | tf_op jit(solution)/shard_map/ppermute | solution.py:53
  73.6 1.6 %collective-permute-start.28 = (bf16[64,1024]{1,0:T(8,128)(2,1)S(1)}, bf16[64,1024]{1,0:T(8,128)(2,1)S(1)}, u32[]{:S(2)}, u32[]{:S(2)}) collective-permute-start(bf16[64,1024]{1,0:T(8,128)(2,1)S(1)} %get-tuple-element.60), channel_id=1, source_target_pairs={{0,1},{1,0},{2,3},{3,2},{4,5},{5,4},{6,7},{7,6},{8,9},{9,8},{10,11... | collective-permute-start | bytes 393224 | tf_op jit(solution)/shard_map/ppermute | solution.py:53
  (3 other events, 3.7 us)

commit v5 on v4

--- a/solution.py
+++ b/solution.py
@@ -332,7 +332,7 @@
     ring1 = [move(first, AHEAD[4 - slot]) for slot in (1, 2, 3)]
     second = jnp.where(is_image, image_other, text_y)
     ring2 = [move(second, AHEAD[3]), move(ring1[1], FLIP_Y), move(second, AHEAD[1])]
-    ring1[0], ring1[1], ring1[2], ring2[1] = lax.optimization_barrier((*ring1, ring2[1]))
+    ring1[0], ring1[1], ring1[2], ring2[1], text_y = lax.optimization_barrier((*ring1, ring2[1], text_y))
     peer1 = [move(v, FLIP_C) for v in ring1]
     text_yc = move(text_y, FLIP_C)
     peer2 = [move(v, FLIP_C) for v in ring2]

time: 77.6 us -> 77.6 us (level)
  no operation moved by 1% of the time
where the time goes in v5:
time: 77.6 us; the launch traced here: 77.4 us
  starting transfers between devices  41.5 us (53%)
  waiting for transfers between devices  18.6 us (24%)
  Pallas kernels  13.5 us (17%)
  local copies, waits for them, and re-layouts  2.09 us (3%)
  between operations  1.63 us (2%)
    ppermute x34, starting transfers between devices, move(): return lax.ppermute(value, AXES, pairs)  41.5 us
    ppermute x34, waiting for transfers between devices, move(): return lax.ppermute(value, AXES, pairs)  18.6 us
    pallas_call x6, Pallas kernels, grads(): call(body, out_shape, [SMEM] + [VMEM] * len(operands), flops=half)  6.68 us
    pallas_call x1, Pallas kernels, on_device(): call(scores_first, (shape(KIND, KIND), mat(2, KIND, WIDTH), shape(8, KIND...  2.24 us
    pallas_call x1, Pallas kernels, on_device(): call(scores_second, (shape(KIND, KIND), mat(2, KIND, WIDTH), shape(8, KIN...  2.09 us
  transfers between devices with their start and end apart: 34, of which 16 were waited for; matrix products, arithmetic and copies ran while one was open for 2% of the time, Pallas kernels for 12%

profile of v5, /device:TPU:1, one launch (start us, length us, event | category | flops | bytes accessed | tf_op | source)
XLA Modules:
  0.0 77.4 jit_solution(1706168057369483861)
XLA Ops:
  0.6 1.5 %collective-permute-start = (bf16[96,1024]{1,0:T(8,128)(2,1)}, bf16[96,1024]{1,0:T(8,128)(2,1)S(1)}, u32[]{:S(2)}, u32[]{:S(2)}) collective-permute-start(bf16[96,1024]{1,0:T(8,128)(2,1)} %text.1), channel_id=1, source_target_pairs={{0,1},{1,0},{2,3},{3,2},{4,5},{5,4},{6,7},{7,6},{8,9},{9,8},{10,11... | collective-permute-start | bytes 589832 | tf_op jit(solution)/shard_map/ppermute | solution.py:53
  2.1 1.2 %constant_dynamic-slice_fusion = (bf16[192,1024]{1,0:T(8,128)(2,1)S(1)}, bf16[192,1024]{1,0:T(8,128)(2,1)S(1)}) fusion(bf16[384,1024]{1,0:T(8,128)(2,1)} %param.3, s32[]{:T(128)S(6)} %select_n.20, s32[]{:T(128)S(6)} %select_n.19), kind=kLoop, calls=%fused_computation.1 | loop fusion | bytes 1572872 | tf_op jit(solution)/shard_map/dynamic_slice | solution.py:328
  4.4 3.8 %collective-permute-start.2 = (bf16[192,1024]{1,0:T(8,128)(2,1)S(1)}, bf16[192,1024]{1,0:T(8,128)(2,1)S(1)}, u32[]{:S(2)}, u32[]{:S(2)}) collective-permute-start(bf16[192,1024]{1,0:T(8,128)(2,1)S(1)} %get-tuple-element.38.refs_0_), channel_id=1, source_target_pairs={{0,64},{1,17},{2,66},{3,19},{4,68},{5,21},{6,70},{7,23},{8,72},{9,... | collective-permute-start | bytes 1179656 | tf_op jit(solution)/shard_map/ppermute | solution.py:53
  8.2 4.6 %collective-permute-start.5 = (bf16[192,1024]{1,0:T(8,128)(2,1)S(1)}, bf16[192,1024]{1,0:T(8,128)(2,1)S(1)}, u32[]{:S(2)}, u32[]{:S(2)}) collective-permute-start(bf16[192,1024]{1,0:T(8,128)(2,1)S(1)} %get-tuple-element.38.refs_0_), channel_id=1, source_target_pairs={{1,7},{3,5},{5,3},{7,1},{9,15},{11,13},{13,11},{15,9},{17,23},{19,... | collective-permute-start | bytes 1179656 | tf_op jit(solution)/shard_map/ppermute | solution.py:53
  13.6 1.9 %collective-permute-start.1 = (bf16[192,1024]{1,0:T(8,128)(2,1)S(1)}, bf16[192,1024]{1,0:T(8,128)(2,1)S(1)}, u32[]{:S(2)}, u32[]{:S(2)}) collective-permute-start(bf16[192,1024]{1,0:T(8,128)(2,1)S(1)} %get-tuple-element.38.refs_0_), channel_id=1, source_target_pairs={{0,96},{1,25},{2,98},{3,27},{4,100},{5,29},{6,102},{7,31},{8,104},... | collective-permute-start | bytes 1179656 | tf_op jit(solution)/shard_map/ppermute | solution.py:53
  16.4 1.6 %collective-permute-done.5 = bf16[192,1024]{1,0:T(8,128)(2,1)S(1)} collective-permute-done((bf16[192,1024]{1,0:T(8,128)(2,1)S(1)}, bf16[192,1024]{1,0:T(8,128)(2,1)S(1)}, u32[]{:S(2)}, u32[]{:S(2)}) %collective-permute-start.5) | collective-permute-done | bytes 393248 | tf_op jit(solution)/shard_map/ppermute | solution.py:53
  18.0 1.1 %collective-permute-start.7 = (bf16[192,1024]{1,0:T(8,128)(2,1)S(1)}, bf16[192,1024]{1,0:T(8,128)(2,1)S(1)}, u32[]{:S(2)}, u32[]{:S(2)}) collective-permute-start(bf16[192,1024]{1,0:T(8,128)(2,1)S(1)} %broadcast_select_fusion.refs_4_), channel_id=1, source_target_pairs={{0,32},{1,9},{2,34},{3,11},{4,36},{5,13},{6,38},{7,15},{8,40},{9,1... | collective-permute-start | bytes 1179656 | tf_op jit(solution)/shard_map/ppermute | solution.py:53
  19.1 1.7 %collective-permute-start.6 = (bf16[192,1024]{1,0:T(8,128)(2,1)S(1)}, bf16[192,1024]{1,0:T(8,128)(2,1)S(1)}, u32[]{:S(2)}, u32[]{:S(2)}) collective-permute-start(bf16[192,1024]{1,0:T(8,128)(2,1)S(1)} %broadcast_select_fusion.refs_4_), channel_id=1, source_target_pairs={{0,96},{1,25},{2,98},{3,27},{4,100},{5,29},{6,102},{7,31},{8,104},... | collective-permute-start | bytes 1179656 | tf_op jit(solution)/shard_map/ppermute | solution.py:53
  21.0 2.7 %collective-permute-done.4.refs_6_.refs_2_ = bf16[192,1024]{1,0:T(8,128)(2,1)S(1)} collective-permute-done((bf16[192,1024]{1,0:T(8,128)(2,1)S(1)}, bf16[192,1024]{1,0:T(8,128)(2,1)S(1)}, u32[]{:S(2)}, u32[]{:S(2)}) %collective-permute-start.4) | collective-permute-done | bytes 393248 | tf_op jit(solution)/shard_map/ppermute | solution.py:53
  24.2 1.7 %collective-permute-done.7.refs_7_.refs_3_ = bf16[192,1024]{1,0:T(8,128)(2,1)S(1)} collective-permute-done((bf16[192,1024]{1,0:T(8,128)(2,1)S(1)}, bf16[192,1024]{1,0:T(8,128)(2,1)S(1)}, u32[]{:S(2)}, u32[]{:S(2)}) %collective-permute-start.7) | collective-permute-done | bytes 393248 | tf_op jit(solution)/shard_map/ppermute | solution.py:53
  27.6 2.2 %shard_map.59 = (f32[768,768]{1,0:T(8,128)S(1)}, bf16[2,768,1024]{2,1,0:T(8,128)(2,1)S(1)}, f32[8,768]{1,0:T(8,128)S(1)}) custom-call(s32[1]{0:T(128)} %bitcast.core, f32[1]{0:T(128)S(6)} %copy.6.scale, bf16[192,1024]{1,0:T(8,128)(2,1)S(1)} %get-tuple-element.38.refs_0_, bf16[192,1024]{1,0:T(8,128)(2,1)S(1)} %collective-permute-done.1.refs_1_, ...), custom_call_target="tpu_custom_call" | custom-call | flops 1207959552 | bytes 2359296 | tf_op jit(solution)/shard_map/pallas_call | solution.py:341
  29.9 2.1 %shard_map.60 = (f32[768,768]{1,0:T(8,128)S(1)}, bf16[2,768,1024]{2,1,0:T(8,128)(2,1)S(1)}, f32[8,768]{1,0:T(8,128)S(1)}) custom-call(s32[1]{0:T(128)} %bitcast.core, f32[1]{0:T(128)S(6)} %copy.6.scale, bf16[2,768,1024]{2,1,0:T(8,128)(2,1)S(1)} %get-tuple-element.46.x_ref.refs_2_, f32[8,768]{1,0:T(8,128)S(1)} %get-tuple-element.47.st1, ...), custom_call_target="tpu_custom_call" | custom-call | flops 1207959552 | bytes 2359296 | tf_op jit(solution)/shard_map/pallas_call | solution.py:348
  32.2 1.0 %collective-permute-done.15.peer_ref = f32[8,768]{1,0:T(8,128)S(1)} collective-permute-done((f32[8,768]{1,0:T(8,128)S(1)}, f32[8,768]{1,0:T(8,128)S(1)}, u32[]{:S(2)}, u32[]{:S(2)}) %collective-permute-start.15) | collective-permute-done | bytes 24608 | tf_op jit(solution)/shard_map/ppermute | solution.py:53
  33.3 2.9 %collective-permute-start.16 = (f32[8,768]{1,0:T(8,128)S(1)}, f32[8,768]{1,0:T(8,128)S(1)}, u32[]{:S(2)}, u32[]{:S(2)}) collective-permute-start(f32[8,768]{1,0:T(8,128)S(1)} %shard_map.61.a_ref), channel_id=1, source_target_pairs={{0,2},{1,7},{2,0},{3,5},{4,6},{5,3},{6,4},{7,1},{8,10},{9,15},{10,... | collective-permute-start | bytes 73736 | tf_op jit(solution)/shard_map/ppermute | solution.py:53
  36.2 1.2 %collective-permute-done.16.b_ref = f32[8,768]{1,0:T(8,128)S(1)} collective-permute-done((f32[8,768]{1,0:T(8,128)S(1)}, f32[8,768]{1,0:T(8,128)S(1)}, u32[]{:S(2)}, u32[]{:S(2)}) %collective-permute-start.16) | collective-permute-done | bytes 24608 | tf_op jit(solution)/shard_map/ppermute | solution.py:53
  37.8 3.3 %collective-permute-start.18 = (f32[8,768]{1,0:T(8,128)S(1)}, f32[8,768]{1,0:T(8,128)S(1)}, u32[]{:S(2)}, u32[]{:S(2)}) collective-permute-start(f32[8,768]{1,0:T(8,128)S(1)} %shard_map.62.a_ref), channel_id=1, source_target_pairs={{0,64},{1,17},{2,66},{3,19},{4,68},{5,21},{6,70},{7,23},{8,72},{9,... | collective-permute-start | bytes 73736 | tf_op jit(solution)/shard_map/ppermute | solution.py:53
  42.6 1.3 %collective-permute-done.17.b1_ref = f32[8,768]{1,0:T(8,128)S(1)} collective-permute-done((f32[8,768]{1,0:T(8,128)S(1)}, f32[8,768]{1,0:T(8,128)S(1)}, u32[]{:S(2)}, u32[]{:S(2)}) %collective-permute-start.17) | collective-permute-done | bytes 24608 | tf_op jit(solution)/shard_map/ppermute | solution.py:53
  44.0 1.8 %collective-permute-start.20 = (f32[8,768]{1,0:T(8,128)S(1)}, f32[8,768]{1,0:T(8,128)S(1)}, u32[]{:S(2)}, u32[]{:S(2)}) collective-permute-start(f32[8,768]{1,0:T(8,128)S(1)} %shard_map.63.mine_ref), channel_id=1, source_target_pairs={{0,1},{1,0},{2,3},{3,2},{4,5},{5,4},{6,7},{7,6},{8,9},{9,8},{10,11... | collective-permute-start | bytes 73736 | tf_op jit(solution)/shard_map/ppermute | solution.py:53
  48.8 1.6 %collective-permute-done.22.r2 = bf16[768,768]{1,0:T(8,128)(2,1)S(1)} collective-permute-done((bf16[768,768]{1,0:T(8,128)(2,1)S(1)}, bf16[768,768]{1,0:T(8,128)(2,1)S(1)}, u32[]{:S(2)}, u32[]{:S(2)}) %collective-permute-start.22) | collective-permute-done | bytes 1179680 | tf_op jit(solution)/shard_map/ppermute | solution.py:53
  50.4 1.6 %shard_map.69 = (bf16[208,1024]{1,0:T(8,128)(2,1)S(1)}, bf16[208,1024]{1,0:T(8,128)(2,1)S(1)}) custom-call(s32[1]{0:T(128)} %bitcast.core, bf16[768,768]{1,0:T(8,128)(2,1)S(1)} %shard_map.64.g1, bf16[768,768]{1,0:T(8,128)(2,1)S(1)} %shard_map.65.g2, bf16[768,768]{1,0:T(8,128)(2,1)S(1)} %collective-permute-done.22.r2, ...), custom_call_target="tpu_custom_call" | custom-call | flops 1207959552 | tf_op jit(solution)/shard_map/pallas_call | solution.py:375
  52.0 2.6 %collective-permute-start.26 = (bf16[208,1024]{1,0:T(8,128)(2,1)S(1)}, bf16[208,1024]{1,0:T(8,128)(2,1)S(1)}, u32[]{:S(2)}, u32[]{:S(2)}) collective-permute-start(bf16[208,1024]{1,0:T(8,128)(2,1)S(1)} %get-tuple-element.57), channel_id=1, source_target_pairs={{0,64},{1,17},{2,66},{3,19},{4,68},{5,21},{6,70},{7,23},{8,72},{9,... | collective-permute-start | bytes 1277960 | tf_op jit(solution)/shard_map/ppermute | solution.py:53
  55.0 1.6 %shard_map.68 = (f32[192,1024]{1,0:T(8,128)S(1)}, bf16[208,1024]{1,0:T(8,128)(2,1)S(1)}, f32[8,128]{1,0:T(8,128)S(1)}) custom-call(s32[1]{0:T(128)} %bitcast.core, bf16[768,768]{1,0:T(8,128)(2,1)S(1)} %shard_map.64.g1, bf16[768,768]{1,0:T(8,128)(2,1)S(1)} %shard_map.65.g2, bf16[768,768]{1,0:T(8,128)(2,1)S(1)} %collective-permute-done.22.r2, ...), custom_call_target="tpu_custom_call" | custom-call | flops 1207959552 | tf_op jit(solution)/shard_map/pallas_call | solution.py:375
  56.6 1.1 %collective-permute-start.25 = (bf16[208,1024]{1,0:T(8,128)(2,1)S(1)}, bf16[208,1024]{1,0:T(8,128)(2,1)S(1)}, u32[]{:S(2)}, u32[]{:S(2)}) collective-permute-start(bf16[208,1024]{1,0:T(8,128)(2,1)S(1)} %get-tuple-element.56), channel_id=1, source_target_pairs={{0,32},{1,9},{2,34},{3,11},{4,36},{5,13},{6,38},{7,15},{8,40},{9,1... | collective-permute-start | bytes 1277960 | tf_op jit(solution)/shard_map/ppermute | solution.py:53
  57.7 1.4 %shard_map.67 = (bf16[192,1024]{1,0:T(8,128)(2,1)S(1)}, bf16[192,1024]{1,0:T(8,128)(2,1)S(1)}) custom-call(s32[1]{0:T(128)} %bitcast.core, bf16[768,768]{1,0:T(8,128)(2,1)S(1)} %shard_map.64.g1, bf16[768,768]{1,0:T(8,128)(2,1)S(1)} %collective-permute-done.21.r1, bf16[768,768]{1,0:T(8,128)(2,1)S(1)} %collective-permute-done.22.r2, ...), custom_call_target="tpu_custom_call" | custom-call | flops 1207959552 | tf_op jit(solution)/shard_map/pallas_call | solution.py:375
  59.2 1.7 %collective-permute-start.24 = (bf16[192,1024]{1,0:T(8,128)(2,1)S(1)}, bf16[192,1024]{1,0:T(8,128)(2,1)S(1)}, u32[]{:S(2)}, u32[]{:S(2)}) collective-permute-start(bf16[192,1024]{1,0:T(8,128)(2,1)S(1)} %get-tuple-element.54), channel_id=1, source_target_pairs={{0,96},{1,25},{2,98},{3,27},{4,100},{5,29},{6,102},{7,31},{8,104},... | collective-permute-start | bytes 1179656 | tf_op jit(solution)/shard_map/ppermute | solution.py:53
  61.8 1.4 %shard_map.66 = (f32[192,1024]{1,0:T(8,128)S(1)}, bf16[96,1024]{1,0:T(8,128)(2,1)S(1)}, bf16[96,1024]{1,0:T(8,128)(2,1)S(1)}) custom-call(s32[1]{0:T(128)} %bitcast.core, bf16[768,768]{1,0:T(8,128)(2,1)S(1)} %shard_map.64.g1, bf16[768,768]{1,0:T(8,128)(2,1)S(1)} %collective-permute-done.21.r1, bf16[768,768]{1,0:T(8,128)(2,1)S(1)} %collective-permute-done.22.r2, ...), custom_call_target="tpu_custom_call" | custom-call | flops 1207959552 | tf_op jit(solution)/shard_map/pallas_call | solution.py:375
  63.3 2.5 %collective-permute-done.27.r3 = bf16[208,1024]{1,0:T(8,128)(2,1)S(1)} collective-permute-done((bf16[208,1024]{1,0:T(8,128)(2,1)S(1)}, bf16[208,1024]{1,0:T(8,128)(2,1)S(1)}, u32[]{:S(2)}, u32[]{:S(2)}) %collective-permute-start.27) | collective-permute-done | bytes 426016 | tf_op jit(solution)/shard_map/ppermute | solution.py:53
  67.0 2.1 %collective-permute-start.30 = (bf16[112,1024]{1,0:T(8,128)(2,1)S(1)}, bf16[112,1024]{1,0:T(8,128)(2,1)S(1)}, u32[]{:S(2)}, u32[]{:S(2)}) collective-permute-start(bf16[112,1024]{1,0:T(8,128)(2,1)S(1)} %get-tuple-element.64), channel_id=1, source_target_pairs={{0,2},{1,7},{2,0},{3,5},{4,6},{5,3},{6,4},{7,1},{8,10},{9,15},{10,... | collective-permute-start | bytes 688136 | tf_op jit(solution)/shard_map/ppermute | solution.py:53
  69.1 0.9 %collective-permute-done.24.r3 = bf16[192,1024]{1,0:T(8,128)(2,1)S(1)} collective-permute-done((bf16[192,1024]{1,0:T(8,128)(2,1)S(1)}, bf16[192,1024]{1,0:T(8,128)(2,1)S(1)}, u32[]{:S(2)}, u32[]{:S(2)}) %collective-permute-start.24) | collective-permute-done | bytes 393248 | tf_op jit(solution)/shard_map/ppermute | solution.py:53
  70.0 3.2 %collective-permute-start.31 = (bf16[112,1024]{1,0:T(8,128)(2,1)S(1)}, bf16[112,1024]{1,0:T(8,128)(2,1)S(1)}, u32[]{:S(2)}, u32[]{:S(2)}) collective-permute-start(bf16[112,1024]{1,0:T(8,128)(2,1)S(1)} %get-tuple-element.65), channel_id=1, source_target_pairs={{0,3},{1,6},{2,1},{3,4},{4,7},{5,2},{6,5},{7,0},{8,11},{9,14},{10,... | collective-permute-start | bytes 688136 | tf_op jit(solution)/shard_map/ppermute | solution.py:53
  75.1 1.1 %collective-permute-done.31.cross = bf16[112,1024]{1,0:T(8,128)(2,1)S(1)} collective-permute-done((bf16[112,1024]{1,0:T(8,128)(2,1)S(1)}, bf16[112,1024]{1,0:T(8,128)(2,1)S(1)}, u32[]{:S(2)}, u32[]{:S(2)}) %collective-permute-start.31) | collective-permute-done | bytes 229408 | tf_op jit(solution)/shard_map/ppermute | solution.py:53
  76.2 1.0 %shard_map.72 = (bf16[96,1024]{1,0:T(8,128)(2,1)}, bf16[96,1024]{1,0:T(8,128)(2,1)}, f32[1]{0:T(128)}) custom-call(s32[1]{0:T(128)} %bitcast.core, f32[1]{0:T(128)S(6)} %copy.6.scale, f32[96,1024]{1,0:T(8,128)S(1)} %get-tuple-element.61.keep, bf16[64,1024]{1,0:T(8,128)(2,1)S(1)} %collective-permute-done.28.got_a, ...), custom_call_target="tpu_custom_call" | custom-call | tf_op jit(solution)/shard_map/pallas_call | solution.py:391
  (55 shorter events, 14.3 us)
Async XLA Ops:
  0.6 2.8 %collective-permute-start = (bf16[96,1024]{1,0:T(8,128)(2,1)}, bf16[96,1024]{1,0:T(8,128)(2,1)S(1)}, u32[]{:S(2)}, u32[]{:S(2)}) collective-permute-start(bf16[96,1024]{1,0:T(8,128)(2,1)} %text.1), channel_id=1, source_target_pairs={{0,1},{1,0},{2,3},{3,2},{4,5},{5,4},{6,7},{7,6},{8,9},{9,8},{10,11... | collective-permute-start | bytes 589832 | tf_op jit(solution)/shard_map/ppermute | solution.py:53
  4.4 11.1 %collective-permute-start.2 = (bf16[192,1024]{1,0:T(8,128)(2,1)S(1)}, bf16[192,1024]{1,0:T(8,128)(2,1)S(1)}, u32[]{:S(2)}, u32[]{:S(2)}) collective-permute-start(bf16[192,1024]{1,0:T(8,128)(2,1)S(1)} %get-tuple-element.38.refs_0_), channel_id=1, source_target_pairs={{0,64},{1,17},{2,66},{3,19},{4,68},{5,21},{6,70},{7,23},{8,72},{9,... | collective-permute-start | bytes 1179656 | tf_op jit(solution)/shard_map/ppermute | solution.py:53
  8.2 9.8 %collective-permute-start.5 = (bf16[192,1024]{1,0:T(8,128)(2,1)S(1)}, bf16[192,1024]{1,0:T(8,128)(2,1)S(1)}, u32[]{:S(2)}, u32[]{:S(2)}) collective-permute-start(bf16[192,1024]{1,0:T(8,128)(2,1)S(1)} %get-tuple-element.38.refs_0_), channel_id=1, source_target_pairs={{1,7},{3,5},{5,3},{7,1},{9,15},{11,13},{13,11},{15,9},{17,23},{19,... | collective-permute-start | bytes 1179656 | tf_op jit(solution)/shard_map/ppermute | solution.py:53
  12.8 8.2 %collective-permute-start.3 = (bf16[192,1024]{1,0:T(8,128)(2,1)S(1)}, bf16[192,1024]{1,0:T(8,128)(2,1)S(1)}, u32[]{:S(2)}, u32[]{:S(2)}) collective-permute-start(bf16[192,1024]{1,0:T(8,128)(2,1)S(1)} %get-tuple-element.38.refs_0_), channel_id=1, source_target_pairs={{0,32},{1,9},{2,34},{3,11},{4,36},{5,13},{6,38},{7,15},{8,40},{9,1... | collective-permute-start | bytes 1179656 | tf_op jit(solution)/shard_map/ppermute | solution.py:53
  13.6 7.4 %collective-permute-start.1 = (bf16[192,1024]{1,0:T(8,128)(2,1)S(1)}, bf16[192,1024]{1,0:T(8,128)(2,1)S(1)}, u32[]{:S(2)}, u32[]{:S(2)}) collective-permute-start(bf16[192,1024]{1,0:T(8,128)(2,1)S(1)} %get-tuple-element.38.refs_0_), channel_id=1, source_target_pairs={{0,96},{1,25},{2,98},{3,27},{4,100},{5,29},{6,102},{7,31},{8,104},... | collective-permute-start | bytes 1179656 | tf_op jit(solution)/shard_map/ppermute | solution.py:53
  15.5 8.1 %collective-permute-start.4 = (bf16[192,1024]{1,0:T(8,128)(2,1)S(1)}, bf16[192,1024]{1,0:T(8,128)(2,1)S(1)}, u32[]{:S(2)}, u32[]{:S(2)}) collective-permute-start(bf16[192,1024]{1,0:T(8,128)(2,1)S(1)} %collective-permute-done.2.refs_2_), channel_id=1, source_target_pairs={{0,2},{1,7},{2,0},{3,5},{4,6},{5,3},{6,4},{7,1},{8,10},{9,15},{10,... | collective-permute-start | bytes 1179656 | tf_op jit(solution)/shard_map/ppermute | solution.py:53
  18.0 7.9 %collective-permute-start.7 = (bf16[192,1024]{1,0:T(8,128)(2,1)S(1)}, bf16[192,1024]{1,0:T(8,128)(2,1)S(1)}, u32[]{:S(2)}, u32[]{:S(2)}) collective-permute-start(bf16[192,1024]{1,0:T(8,128)(2,1)S(1)} %broadcast_select_fusion.refs_4_), channel_id=1, source_target_pairs={{0,32},{1,9},{2,34},{3,11},{4,36},{5,13},{6,38},{7,15},{8,40},{9,1... | collective-permute-start | bytes 1179656 | tf_op jit(solution)/shard_map/ppermute | solution.py:53
  19.1 6.8 %collective-permute-start.6 = (bf16[192,1024]{1,0:T(8,128)(2,1)S(1)}, bf16[192,1024]{1,0:T(8,128)(2,1)S(1)}, u32[]{:S(2)}, u32[]{:S(2)}) collective-permute-start(bf16[192,1024]{1,0:T(8,128)(2,1)S(1)} %broadcast_select_fusion.refs_4_), channel_id=1, source_target_pairs={{0,96},{1,25},{2,98},{3,27},{4,100},{5,29},{6,102},{7,31},{8,104},... | collective-permute-start | bytes 1179656 | tf_op jit(solution)/shard_map/ppermute | solution.py:53
  23.7 2.8 %collective-permute-start.8 = (bf16[192,1024]{1,0:T(8,128)(2,1)S(1)}, bf16[192,1024]{1,0:T(8,128)(2,1)S(1)}, u32[]{:S(2)}, u32[]{:S(2)}) collective-permute-start(bf16[192,1024]{1,0:T(8,128)(2,1)S(1)} %collective-permute-done.1.refs_1_), channel_id=1, source_target_pairs={{0,1},{1,0},{2,3},{3,2},{4,5},{5,4},{6,7},{7,6},{8,9},{9,8},{10,11... | collective-permute-start | bytes 1179656 | tf_op jit(solution)/shard_map/ppermute | solution.py:53
  23.7 2.8 %collective-permute-start.9 = (bf16[192,1024]{1,0:T(8,128)(2,1)S(1)}, bf16[192,1024]{1,0:T(8,128)(2,1)S(1)}, u32[]{:S(2)}, u32[]{:S(2)}) collective-permute-start(bf16[192,1024]{1,0:T(8,128)(2,1)S(1)} %collective-permute-done.2.refs_2_), channel_id=1, source_target_pairs={{0,1},{1,0},{2,3},{3,2},{4,5},{5,4},{6,7},{7,6},{8,9},{9,8},{10,11... | collective-permute-start | bytes 1179656 | tf_op jit(solution)/shard_map/ppermute | solution.py:53
  24.2 3.4 %collective-permute-start.10 = (bf16[192,1024]{1,0:T(8,128)(2,1)S(1)}, bf16[192,1024]{1,0:T(8,128)(2,1)S(1)}, u32[]{:S(2)}, u32[]{:S(2)}) collective-permute-start(bf16[192,1024]{1,0:T(8,128)(2,1)S(1)} %collective-permute-done.3.refs_3_), channel_id=1, source_target_pairs={{0,1},{1,0},{2,3},{3,2},{4,5},{5,4},{6,7},{7,6},{8,9},{9,8},{10,11... | collective-permute-start | bytes 1179656 | tf_op jit(solution)/shard_map/ppermute | solution.py:53
  25.9 3.9 %collective-permute-start.11 = (bf16[192,1024]{1,0:T(8,128)(2,1)S(1)}, bf16[192,1024]{1,0:T(8,128)(2,1)S(1)}, u32[]{:S(2)}, u32[]{:S(2)}) collective-permute-start(bf16[192,1024]{1,0:T(8,128)(2,1)S(1)} %collective-permute-done.5), channel_id=1, source_target_pairs={{0,1},{1,0},{2,3},{3,2},{4,5},{5,4},{6,7},{7,6},{8,9},{9,8},{10,11... | collective-permute-start | bytes 1179656 | tf_op jit(solution)/shard_map/ppermute | solution.py:53
  25.9 3.9 %collective-permute-start.14 = (bf16[192,1024]{1,0:T(8,128)(2,1)S(1)}, bf16[192,1024]{1,0:T(8,128)(2,1)S(1)}, u32[]{:S(2)}, u32[]{:S(2)}) collective-permute-start(bf16[192,1024]{1,0:T(8,128)(2,1)S(1)} %collective-permute-done.7.refs_7_.refs_3_), channel_id=1, source_target_pairs={{0,1},{1,0},{2,3},{3,2},{4,5},{5,4},{6,7},{7,6},{8,9},{9,8},{10,11... | collective-permute-start | bytes 1179656 | tf_op jit(solution)/shard_map/ppermute | solution.py:53
  26.4 3.4 %collective-permute-start.12 = (bf16[192,1024]{1,0:T(8,128)(2,1)S(1)}, bf16[192,1024]{1,0:T(8,128)(2,1)S(1)}, u32[]{:S(2)}, u32[]{:S(2)}) collective-permute-start(bf16[192,1024]{1,0:T(8,128)(2,1)S(1)} %collective-permute-done.6.refs_5_.refs_1_), channel_id=1, source_target_pairs={{0,1},{1,0},{2,3},{3,2},{4,5},{5,4},{6,7},{7,6},{8,9},{9,8},{10,11... | collective-permute-start | bytes 1179656 | tf_op jit(solution)/shard_map/ppermute | solution.py:53
  26.5 3.3 %collective-permute-start.13 = (bf16[192,1024]{1,0:T(8,128)(2,1)S(1)}, bf16[192,1024]{1,0:T(8,128)(2,1)S(1)}, u32[]{:S(2)}, u32[]{:S(2)}) collective-permute-start(bf16[192,1024]{1,0:T(8,128)(2,1)S(1)} %collective-permute-done.4.refs_6_.refs_2_), channel_id=1, source_target_pairs={{0,1},{1,0},{2,3},{3,2},{4,5},{5,4},{6,7},{7,6},{8,9},{9,8},{10,11... | collective-permute-start | bytes 1179656 | tf_op jit(solution)/shard_map/ppermute | solution.py:53
  33.3 4.1 %collective-permute-start.16 = (f32[8,768]{1,0:T(8,128)S(1)}, f32[8,768]{1,0:T(8,128)S(1)}, u32[]{:S(2)}, u32[]{:S(2)}) collective-permute-start(f32[8,768]{1,0:T(8,128)S(1)} %shard_map.61.a_ref), channel_id=1, source_target_pairs={{0,2},{1,7},{2,0},{3,5},{4,6},{5,3},{6,4},{7,1},{8,10},{9,15},{10,... | collective-permute-start | bytes 73736 | tf_op jit(solution)/shard_map/ppermute | solution.py:53
  37.4 4.5 %collective-permute-start.19 = (f32[8,768]{1,0:T(8,128)S(1)}, f32[8,768]{1,0:T(8,128)S(1)}, u32[]{:S(2)}, u32[]{:S(2)}) collective-permute-start(f32[8,768]{1,0:T(8,128)S(1)} %shard_map.62.a_ref), channel_id=1, source_target_pairs={{0,32},{1,9},{2,34},{3,11},{4,36},{5,13},{6,38},{7,15},{8,40},{9,1... | collective-permute-start | bytes 73736 | tf_op jit(solution)/shard_map/ppermute | solution.py:53
  37.8 4.8 %collective-permute-start.18 = (f32[8,768]{1,0:T(8,128)S(1)}, f32[8,768]{1,0:T(8,128)S(1)}, u32[]{:S(2)}, u32[]{:S(2)}) collective-permute-start(f32[8,768]{1,0:T(8,128)S(1)} %shard_map.62.a_ref), channel_id=1, source_target_pairs={{0,64},{1,17},{2,66},{3,19},{4,68},{5,21},{6,70},{7,23},{8,72},{9,... | collective-permute-start | bytes 73736 | tf_op jit(solution)/shard_map/ppermute | solution.py:53
  41.1 2.8 %collective-permute-start.17 = (f32[8,768]{1,0:T(8,128)S(1)}, f32[8,768]{1,0:T(8,128)S(1)}, u32[]{:S(2)}, u32[]{:S(2)}) collective-permute-start(f32[8,768]{1,0:T(8,128)S(1)} %shard_map.62.a_ref), channel_id=1, source_target_pairs={{0,96},{1,25},{2,98},{3,27},{4,100},{5,29},{6,102},{7,31},{8,104},... | collective-permute-start | bytes 73736 | tf_op jit(solution)/shard_map/ppermute | solution.py:53
  44.0 2.6 %collective-permute-start.20 = (f32[8,768]{1,0:T(8,128)S(1)}, f32[8,768]{1,0:T(8,128)S(1)}, u32[]{:S(2)}, u32[]{:S(2)}) collective-permute-start(f32[8,768]{1,0:T(8,128)S(1)} %shard_map.63.mine_ref), channel_id=1, source_target_pairs={{0,1},{1,0},{2,3},{3,2},{4,5},{5,4},{6,7},{7,6},{8,9},{9,8},{10,11... | collective-permute-start | bytes 73736 | tf_op jit(solution)/shard_map/ppermute | solution.py:53
  47.3 3.1 %collective-permute-start.22 = (bf16[768,768]{1,0:T(8,128)(2,1)S(1)}, bf16[768,768]{1,0:T(8,128)(2,1)S(1)}, u32[]{:S(2)}, u32[]{:S(2)}) collective-permute-start(bf16[768,768]{1,0:T(8,128)(2,1)S(1)} %shard_map.65.g2), channel_id=1, source_target_pairs={{0,1},{1,0},{2,3},{3,2},{4,5},{5,4},{6,7},{7,6},{8,9},{9,8},{10,11... | collective-permute-start | bytes 3538952 | tf_op jit(solution)/shard_map/ppermute | solution.py:53
  48.6 9.2 %collective-permute-start.21 = (bf16[768,768]{1,0:T(8,128)(2,1)S(1)}, bf16[768,768]{1,0:T(8,128)(2,1)S(1)}, u32[]{:S(2)}, u32[]{:S(2)}) collective-permute-start(bf16[768,768]{1,0:T(8,128)(2,1)S(1)} %shard_map.64.g1), channel_id=1, source_target_pairs={{0,1},{1,0},{2,3},{3,2},{4,5},{5,4},{6,7},{7,6},{8,9},{9,8},{10,11... | collective-permute-start | bytes 3538952 | tf_op jit(solution)/shard_map/ppermute | solution.py:53
  52.0 11.2 %collective-permute-start.26 = (bf16[208,1024]{1,0:T(8,128)(2,1)S(1)}, bf16[208,1024]{1,0:T(8,128)(2,1)S(1)}, u32[]{:S(2)}, u32[]{:S(2)}) collective-permute-start(bf16[208,1024]{1,0:T(8,128)(2,1)S(1)} %get-tuple-element.57), channel_id=1, source_target_pairs={{0,64},{1,17},{2,66},{3,19},{4,68},{5,21},{6,70},{7,23},{8,72},{9,... | collective-permute-start | bytes 1277960 | tf_op jit(solution)/shard_map/ppermute | solution.py:53
  54.6 11.2 %collective-permute-start.27 = (bf16[208,1024]{1,0:T(8,128)(2,1)S(1)}, bf16[208,1024]{1,0:T(8,128)(2,1)S(1)}, u32[]{:S(2)}, u32[]{:S(2)}) collective-permute-start(bf16[208,1024]{1,0:T(8,128)(2,1)S(1)} %get-tuple-element.58), channel_id=1, source_target_pairs={{0,96},{1,25},{2,98},{3,27},{4,100},{5,29},{6,102},{7,31},{8,104},... | collective-permute-start | bytes 1277960 | tf_op jit(solution)/shard_map/ppermute | solution.py:53
  56.6 9.9 %collective-permute-start.25 = (bf16[208,1024]{1,0:T(8,128)(2,1)S(1)}, bf16[208,1024]{1,0:T(8,128)(2,1)S(1)}, u32[]{:S(2)}, u32[]{:S(2)}) collective-permute-start(bf16[208,1024]{1,0:T(8,128)(2,1)S(1)} %get-tuple-element.56), channel_id=1, source_target_pairs={{0,32},{1,9},{2,34},{3,11},{4,36},{5,13},{6,38},{7,15},{8,40},{9,1... | collective-permute-start | bytes 1277960 | tf_op jit(solution)/shard_map/ppermute | solution.py:53
  59.2 10.9 %collective-permute-start.24 = (bf16[192,1024]{1,0:T(8,128)(2,1)S(1)}, bf16[192,1024]{1,0:T(8,128)(2,1)S(1)}, u32[]{:S(2)}, u32[]{:S(2)}) collective-permute-start(bf16[192,1024]{1,0:T(8,128)(2,1)S(1)} %get-tuple-element.54), channel_id=1, source_target_pairs={{0,96},{1,25},{2,98},{3,27},{4,100},{5,29},{6,102},{7,31},{8,104},... | collective-permute-start | bytes 1179656 | tf_op jit(solution)/shard_map/ppermute | solution.py:53
  60.9 12.4 %collective-permute-start.23 = (bf16[192,1024]{1,0:T(8,128)(2,1)S(1)}, bf16[192,1024]{1,0:T(8,128)(2,1)S(1)}, u32[]{:S(2)}, u32[]{:S(2)}) collective-permute-start(bf16[192,1024]{1,0:T(8,128)(2,1)S(1)} %get-tuple-element.53.refs_0_), channel_id=1, source_target_pairs={{0,64},{1,17},{2,66},{3,19},{4,68},{5,21},{6,70},{7,23},{8,72},{9,... | collective-permute-start | bytes 1179656 | tf_op jit(solution)/shard_map/ppermute | solution.py:53
  63.2 10.5 %collective-permute-start.32 = (bf16[96,1024]{1,0:T(8,128)(2,1)S(1)}, bf16[96,1024]{1,0:T(8,128)(2,1)S(1)}, u32[]{:S(2)}, u32[]{:S(2)}) collective-permute-start(bf16[96,1024]{1,0:T(8,128)(2,1)S(1)} %get-tuple-element.66), channel_id=1, source_target_pairs={{0,32},{1,9},{2,34},{3,11},{4,36},{5,13},{6,38},{7,15},{8,40},{9,1... | collective-permute-start | bytes 589832 | tf_op jit(solution)/shard_map/ppermute | solution.py:53
  65.8 8.8 %collective-permute-start.33 = (bf16[96,1024]{1,0:T(8,128)(2,1)S(1)}, bf16[96,1024]{1,0:T(8,128)(2,1)S(1)}, u32[]{:S(2)}, u32[]{:S(2)}) collective-permute-start(bf16[96,1024]{1,0:T(8,128)(2,1)S(1)} %get-tuple-element.67), channel_id=1, source_target_pairs={{0,33},{1,8},{2,35},{3,10},{4,37},{5,12},{6,39},{7,14},{8,41},{9,1... | collective-permute-start | bytes 589832 | tf_op jit(solution)/shard_map/ppermute | solution.py:53
  67.0 8.2 %collective-permute-start.30 = (bf16[112,1024]{1,0:T(8,128)(2,1)S(1)}, bf16[112,1024]{1,0:T(8,128)(2,1)S(1)}, u32[]{:S(2)}, u32[]{:S(2)}) collective-permute-start(bf16[112,1024]{1,0:T(8,128)(2,1)S(1)} %get-tuple-element.64), channel_id=1, source_target_pairs={{0,2},{1,7},{2,0},{3,5},{4,6},{5,3},{6,4},{7,1},{8,10},{9,15},{10,... | collective-permute-start | bytes 688136 | tf_op jit(solution)/shard_map/ppermute | solution.py:53
  70.0 6.2 %collective-permute-start.31 = (bf16[112,1024]{1,0:T(8,128)(2,1)S(1)}, bf16[112,1024]{1,0:T(8,128)(2,1)S(1)}, u32[]{:S(2)}, u32[]{:S(2)}) collective-permute-start(bf16[112,1024]{1,0:T(8,128)(2,1)S(1)} %get-tuple-element.65), channel_id=1, source_target_pairs={{0,3},{1,6},{2,1},{3,4},{4,7},{5,2},{6,5},{7,0},{8,11},{9,14},{10,... | collective-permute-start | bytes 688136 | tf_op jit(solution)/shard_map/ppermute | solution.py:53
  73.6 1.6 %collective-permute-start.28 = (bf16[64,1024]{1,0:T(8,128)(2,1)S(1)}, bf16[64,1024]{1,0:T(8,128)(2,1)S(1)}, u32[]{:S(2)}, u32[]{:S(2)}) collective-permute-start(bf16[64,1024]{1,0:T(8,128)(2,1)S(1)} %get-tuple-element.62), channel_id=1, source_target_pairs={{0,1},{1,0},{2,3},{3,2},{4,5},{5,4},{6,7},{7,6},{8,9},{9,8},{10,11... | collective-permute-start | bytes 393224 | tf_op jit(solution)/shard_map/ppermute | solution.py:53
  (3 other events, 3.7 us)
